TPU v7x, 32 devices: a whole 2x2x4 slice. The times are simulated.
32 devices in a mesh: parts: 2 (over y), seq: 4 (over z), chan: 2 (over x), rep: 2 (over core).
Axes of the slice: x: 2, y: 2, z: 4, core: 2. Of those that a mesh axis runs over, the one named last changes fastest.
Arguments:
- tokens: bfloat16 [4096, 4096], P(('parts', 'seq'), ('chan', 'rep')), parts along dimension 0, may hold values from -6 to 6
- w_query: bfloat16 [4096, 4096], P('seq', ('chan', 'rep')), may hold values from -0.09375 to 0.09375
- w_key: bfloat16 [4096, 4096], P('seq', ('chan', 'rep')), may hold values from -0.09375 to 0.09375
- w_value: bfloat16 [4096, 4096], P('seq', ('chan', 'rep')), may hold values from -0.09375 to 0.09375
- decay_rate: float32 [4096, 16], P(('chan', 'rep', 'seq')), may hold values from 4.8828125e-06 to 0.04, as said below
- residue: float32 [4096, 16], P(('chan', 'rep', 'seq')), may hold values from -1.5 to 1.5
- carried: float32 [8192, 16], P(('parts', 'chan', 'rep', 'seq')), parts along dimension 0, may hold values from -6 to 6
Outputs:
- gated_output: bfloat16 [4096, 4096], P(('parts', 'seq'), ('chan', 'rep')), parts along dimension 0
- new_state: float32 [8192, 16], P(('parts', 'chan', 'rep', 'seq')), parts along dimension 0
There are 2 independent parts, one for each index of `parts`. A program takes and returns all parts, laid end to end along the dimension named above; an argument that names none is the same for every part. Nothing has to cross between parts.
Inputs may be any that keep to these rules, and one draw needn't show every extreme that they name: `decay_rate`: each rate lies between 0.01 / 2048 and 0.04.
All inputs are finite; a program needn't handle non-finite values.
Results may differ from a plain program's by a relative error of at most 0.0066.
Values may be sent and summed in bfloat16 or wider, within the bound.
No kernel may reach another device: no remote copies, remote signals or barrier semaphores. Data moves between devices by JAX's collectives and lax.ppermute only.
A program may use at most 128 MiB of HBM per device.

v0:
```python
import jax
import jax.numpy as jnp
from jax import lax
from jax.sharding import PartitionSpec as P

BLOCK = 128


HIGHEST_PRECISION = lax.Precision.HIGHEST


def mode_scale(decay_rates):
    return jnp.sqrt(-jnp.expm1(-2.0 * decay_rates))


def local_ends(blocks, decay_rates):
    block_width = blocks.shape[2]
    offsets = jnp.arange(block_width, dtype=jnp.float32)
    tail_powers = jnp.exp(-decay_rates[:, :, None] * (block_width - 1.0 - offsets)[None, None, :])
    sums_here = jnp.einsum("cnb,cmb->cnm", blocks, tail_powers, precision=HIGHEST_PRECISION)
    return mode_scale(decay_rates)[:, None, :] * sums_here


def combine_states(earlier, later):
    return (earlier[0] * later[0], later[0] * earlier[1] + later[1])


def block_sums(block_ends, decay_rates, block_width):
    step_decay = jnp.broadcast_to(jnp.exp(-decay_rates * block_width)[:, None, :], block_ends.shape)
    unused_decay, running = lax.associative_scan(combine_states, (step_decay, block_ends), axis=1)
    return running


def entering_states(running, decay_rates, start_state, block_width):
    count_blocks = running.shape[1]
    block_starts = jnp.arange(count_blocks, dtype=jnp.float32) * block_width
    decayed = (
        jnp.exp(-decay_rates[:, None, :] * block_starts[None, :, None]) * start_state[:, None, :]
    )
    earlier_sums = jnp.concatenate([jnp.zeros_like(running[:, :1]), running[:, :-1]], axis=1)
    final_state = (
        jnp.exp(-decay_rates * (count_blocks * block_width)) * start_state + running[:, -1]
    )
    return (decayed + earlier_sums, final_state)


def block_convolve(blocks, decay_rates, residues, entering):
    block_width = blocks.shape[2]
    offsets = jnp.arange(block_width, dtype=jnp.float32)
    powers = jnp.exp(-decay_rates[:, :, None] * offsets[None, None, :])
    kernel = jnp.sum((residues * mode_scale(decay_rates))[:, :, None] * powers, axis=1)
    out_index = jnp.arange(block_width, dtype=jnp.int32)[:, None]
    in_index = jnp.arange(block_width, dtype=jnp.int32)[None, :]
    lag = jnp.maximum(out_index - in_index, 0)
    causal = (out_index >= in_index).astype(jnp.float32)
    toeplitz = kernel[:, lag] * causal[None, :, :]
    direct = jnp.einsum("cij,cnj->cni", toeplitz, blocks, precision=HIGHEST_PRECISION)
    leading = residues[:, :, None] * jnp.exp(
        -decay_rates[:, :, None] * (offsets + 1.0)[None, None, :]
    )
    return direct + jnp.einsum("cnm,cmb->cnb", entering, leading, precision=HIGHEST_PRECISION)


def per_device(tokens, w_query, w_key, w_value, decay_rate, residue, carried):
    gathered = lax.all_gather(tokens, ("chan", "rep"), axis=1, tiled=True)
    pieces = (
        lax.all_gather(w_query, "seq", axis=0, tiled=True),
        lax.all_gather(w_key, "seq", axis=0, tiled=True),
        lax.all_gather(w_value, "seq", axis=0, tiled=True),
    )
    query_acc, key_acc, value_acc = tuple(
        (
            lax.dot_general(
                weight_piece, gathered, (((0,), (1,)), ((), ())), preferred_element_type=jnp.float32
            )
            for weight_piece in pieces
        )
    )
    query_rows = query_acc.astype(jnp.bfloat16)
    key_rows = key_acc.astype(jnp.bfloat16)
    value_rows = value_acc.astype(jnp.bfloat16)
    query_rows, key_rows, value_rows = lax.optimization_barrier((query_rows, key_rows, value_rows))
    product = (key_rows.astype(jnp.float32) * value_rows.astype(jnp.float32)).astype(jnp.bfloat16)
    owned = lax.all_to_all(product, "seq", split_axis=0, concat_axis=1, tiled=True)
    own_chan = owned.shape[0]
    blocks = owned.astype(jnp.float32).reshape(own_chan, -1, BLOCK)
    block_end = local_ends(blocks, decay_rate)
    running = block_sums(block_end, decay_rate, BLOCK)
    entering, new_state = entering_states(running, decay_rate, carried, BLOCK)
    conv_out = (
        block_convolve(blocks, decay_rate, residue, entering)
        .reshape(own_chan, -1)
        .astype(jnp.bfloat16)
    )
    conv_back = lax.all_to_all(conv_out, "seq", split_axis=1, concat_axis=0, tiled=True)
    conv_back = lax.optimization_barrier(conv_back)
    gated_rows = (query_rows.astype(jnp.float32) * conv_back.astype(jnp.float32)).astype(
        jnp.bfloat16
    )
    return (gated_rows.T, new_state)


def solution(mesh):
    in_specs = (
        P(("parts", "seq"), ("chan", "rep")),
        P("seq", ("chan", "rep")),
        P("seq", ("chan", "rep")),
        P("seq", ("chan", "rep")),
        P(("chan", "rep", "seq"), None),
        P(("chan", "rep", "seq"), None),
        P(("parts", "chan", "rep", "seq"), None),
    )
    out_specs = (P(("parts", "seq"), ("chan", "rep")), P(("parts", "chan", "rep", "seq"), None))
    return jax.shard_map(
        per_device, mesh=mesh, in_specs=in_specs, out_specs=out_specs, check_vma=False
    )
```

profile of v0, /device:TPU:0, one launch (start us, length us, event | category | flops | bytes accessed | tf_op | source)
XLA Modules:
  0.0 892.5 jit_solution(9906552894119461772)
XLA Ops:
  10.0 36.8 %all-gather.7.cloned.1.call-done = bf16[512,4096]{1,0:T(8,128)(2,1)} async-done(((bf16[512,1024]{1,0:T(8,128)(2,1)}), bf16[512,4096]{1,0:T(8,128)(2,1)}) %all-gather.7.cloned.1.call-update) | async-done | bytes 4194320 | tf_op jit(solution)/shard_map/all_gather | solution.py:65
  46.8 151.2 %all-gather.5.cloned.1.call-done = bf16[4096,1024]{1,0:T(8,128)(2,1)} async-done(((bf16[1024,1024]{1,0:T(8,128)(2,1)}), bf16[4096,1024]{1,0:T(8,128)(2,1)}) %all-gather.5.cloned.1.call-update) | async-done | bytes 8388624 | tf_op jit(solution)/shard_map/all_gather | solution.py:67
  198.0 10.1 %convolution_convert_fusion.2 = bf16[1024,512]{1,0:T(8,128)(2,1)} fusion(bf16[4096,1024]{1,0:T(8,128)(2,1)} %all-gather.5.cloned.1.call-done, bf16[512,4096]{1,0:T(8,128)(2,1)} %all-gather.7.cloned.1.call-done), kind=kOutput, calls=%fused_computation.25 | convolution fusion | flops 4295491584 | bytes 13631488 | tf_op jit(solution)/shard_map/dot_general | solution.py:73
  208.1 139.4 %all-gather.9.cloned.1.call-done = bf16[4096,1024]{1,0:T(8,128)(2,1)} async-done(((bf16[1024,1024]{1,0:T(8,128)(2,1)}), bf16[4096,1024]{1,0:T(8,128)(2,1)}) %all-gather.9.cloned.1.call-update) | async-done | bytes 8388624 | tf_op jit(solution)/shard_map/all_gather | solution.py:68
  347.5 9.1 %convolution_convert_fusion.1 = bf16[1024,512]{1,0:T(8,128)(2,1)S(1)} fusion(bf16[4096,1024]{1,0:T(8,128)(2,1)} %all-gather.9.cloned.1.call-done, bf16[512,4096]{1,0:T(8,128)(2,1)} %all-gather.7.cloned.1.call-done), kind=kOutput, calls=%fused_computation.24 | convolution fusion | flops 4295491584 | bytes 13631488 | tf_op jit(solution)/shard_map/dot_general | solution.py:73
  356.6 140.2 %all-gather.11.cloned.1.call-done = bf16[4096,1024]{1,0:T(8,128)(2,1)} async-done(((bf16[1024,1024]{1,0:T(8,128)(2,1)}), bf16[4096,1024]{1,0:T(8,128)(2,1)}) %all-gather.11.cloned.1.call-update) | async-done | bytes 8388624 | tf_op jit(solution)/shard_map/all_gather | solution.py:69
  496.8 9.3 %convolution_convert_fusion = bf16[1024,512]{1,0:T(8,128)(2,1)S(1)} fusion(bf16[4096,1024]{1,0:T(8,128)(2,1)} %all-gather.11.cloned.1.call-done, bf16[512,4096]{1,0:T(8,128)(2,1)} %all-gather.7.cloned.1.call-done), kind=kOutput, calls=%fused_computation.23 | convolution fusion | flops 4295491584 | bytes 13631488 | tf_op jit(solution)/shard_map/dot_general | solution.py:73
  506.2 1.3 multiply_convert_fusion.1
  507.4 3.5 all-to-all-start
  511.1 0.8 copy.74
  514.1 1.7 multiply_reduce_fusion
  515.9 62.0 %gather_fusion = f32[16384,256]{1,0:T(8,128)} fusion(f32[256,128]{0,1:T(8,128)S(1)} %copy.66, s32[16384]{0:T(1024)S(1)} %bitcast_clamp_fusion), kind=kCustom, calls=%fused_computation | custom fusion | bytes 33619968 | tf_op jit(solution)/shard_map/gather | solution.py:56
  577.9 18.0 %copy.67 = f32[128,128,256]{1,0,2:T(8,128)} copy(f32[128,128,256]{2,1,0:T(8,128)} %bitcast.30) | data formatting | bytes 33554432 | tf_op jit(solution)/shard_map/gather | solution.py:56
  596.6 0.8 copy.63
  597.9 2.9 fusion.16
  601.5 3.5 slice.88
  605.0 3.5 slice.108
  608.4 3.5 slice.89
  611.9 1.9 copy_add_fusion
  615.5 1.0 pad.29
  616.6 0.8 add.78
  617.6 2.0 pad.31
  621.8 77.4 %pad.32 = f32[256,16,16]{2,1,0:T(8,128)} pad(f32[256,8,16]{2,1,0:T(8,128)S(1)} %pad_maximum_fusion, f32[]{:T(128)} %constant.8.clone.1), padding=0_0_0x0_1_1x0_0_0 | pad | bytes 393220 | tf_op jit(solution)/shard_map/pad | solution.py:30
  699.2 77.5 %pad.33.clone = f32[256,16,16]{2,1,0:T(8,128)} pad(f32[256,8,16]{2,1,0:T(8,128)S(1)} %copy.81, f32[]{:T(128)} %constant.8.clone.1), padding=0_0_0x1_0_1x0_0_0 | pad | bytes 393220 | tf_op jit(solution)/shard_map/pad | solution.py:30
  776.7 2.5 slice_add_fusion
  779.2 3.0 fusion.4
  782.3 15.9 %add_convert_fusion = bf16[256,16,128]{2,1,0:T(8,128)(2,1)S(1)} fusion(f32[256,16,128]{2,1,0:T(8,128)S(1)} %fusion.4, bf16[256,16,128]{2,1,0:T(8,128)(2,1)S(1)} %reshape.72, f32[128,128,256]{1,0,2:T(8,128)} %copy.67, f32[128,128]{1,0:T(8,128)S(1)} %copy-done.8), kind=kOutput, calls=%fused_computation.7 | convolution fusion | flops 810549248 | bytes 21037056 | tf_op jit(solution)/shard_map/cij,cnj->cni/dot_general | solution.py:57
  798.6 1.2 copy.75
  799.8 5.0 all-to-all-start.1
  804.8 77.5 %pad.63 = f32[256,15,16]{2,1,0:T(8,128)} pad(f32[256,8,16]{2,1,0:T(8,128)S(1)} %copy.81, f32[]{:T(128)} %constant.8.clone.1), padding=0_0_0x0_0_1x0_0_0 | pad | bytes 376836
  882.3 1.3 slice.157
  884.6 1.3 copy.77
  (70 shorter events, 12.5 us)
Async XLA Ops:
  7.2 39.6 %all-gather.7.cloned.1.call-start = ((), (), s32[]{:S(2)}) async-start(), calls=%async_computation.3 | async-start | bytes 5242880 | tf_op jit(solution)/shard_map/all_gather | solution.py:65
  7.9 190.1 %all-gather.5.cloned.1.call-start = ((), (), s32[]{:S(2)}) async-start(), calls=%async_computation.2 | async-start | bytes 10485760 | tf_op jit(solution)/shard_map/all_gather | solution.py:67
  8.6 338.8 %all-gather.9.cloned.1.call-start = ((), (), s32[]{:S(2)}) async-start(), calls=%async_computation.4 | async-start | bytes 10485760 | tf_op jit(solution)/shard_map/all_gather | solution.py:68
  9.4 487.4 %all-gather.11.cloned.1.call-start = ((), (), s32[]{:S(2)}) async-start(), calls=%async_computation.5 | async-start | bytes 10485760 | tf_op jit(solution)/shard_map/all_gather | solution.py:69
  506.1 4.8 copy-start.11
  506.1 4.9 copy-start.10
  506.2 5.8 copy-start.12
  507.4 89.2 %all-to-all-start = ((bf16[4,256,512]{2,1,0:T(8,128)(2,1)}), bf16[4,256,512]{2,1,0:T(8,128)(2,1)S(1)}, u32[]{:S(2)}, u32[]{:S(2)}) async-start(bf16[4,256,512]{2,1,0:T(8,128)(2,1)} %bitcast), calls=%async_computation | async-start | bytes 2097152 | tf_op jit(solution)/shard_map/all_to_all | solution.py:84
  514.1 63.8 %copy-start.2 = (f32[256,16]{1,0:T(8,128)}, f32[256,16]{1,0:T(8,128)S(1)}, u32[]{:S(2)}) copy-start(f32[256,16]{1,0:T(8,128)S(1)} %get-tuple-element.23) | copy-start | bytes 49156
  611.9 2.6 copy-start.4
  616.5 0.9 copy-start.7
  619.7 1.2 copy-start
  619.8 1.7 copy-start.5
  776.7 2.6 copy-start.3
  776.7 2.6 copy-start.6
  776.7 2.6 copy-start.9
  779.2 3.0 copy-start.8
  799.8 84.6 %all-to-all-start.1 = ((bf16[256,4,512]{2,0,1:T(8,128)(2,1)}), bf16[256,4,512]{2,0,1:T(8,128)(2,1)S(1)}, u32[]{:S(2)}, u32[]{:S(2)}) async-start(bf16[256,4,512]{2,0,1:T(8,128)(2,1)} %copy.75), calls=%async_computation.1 | async-start | bytes 2097152 | tf_op jit(solution)/shard_map/all_to_all | solution.py:95
  804.8 79.5 %copy-start.1 = (bf16[1024,512]{1,0:T(8,128)(2,1)S(1)}, bf16[1024,512]{1,0:T(8,128)(2,1)}, u32[]{:S(2)}) copy-start(bf16[1024,512]{1,0:T(8,128)(2,1)} %convolution_convert_fusion.2) | copy-start | bytes 3145732
Sparse Core Ops, SparseCore 0:
  9.6 37.1 all-gather.6
  48.3 149.6 all-gather.4
  199.6 147.8 all-gather.8
  348.9 147.8 all-gather.10
where the time goes:
time: 893 us; the launch traced here: 892 us
  waiting for transfers between devices  470 us (53%)
  local copies, waits for them, and re-layouts  337 us (38%)
  matrix products  50.3 us (6%)
  between operations  14.1 us (2%)
  other arithmetic  12 us (1%)
    pad x6, local copies, waits for them, and re-layouts, block_sums(): lax.associative_scan(combine_states, (step_decay, block_ends), axis=1)  158 us
    all_gather x1, waiting for transfers between devices, per_device(): lax.all_gather(w_query, 'seq', axis=0, tiled=True)  151 us
    all_gather x1, waiting for transfers between devices, per_device(): lax.all_gather(w_value, 'seq', axis=0, tiled=True)  140 us
    all_gather x1, waiting for transfers between devices, per_device(): lax.all_gather(w_key, 'seq', axis=0, tiled=True)  139 us
    unnamed x33, local copies, waits for them, and re-layouts  82.2 us
    gather x2, local copies, waits for them, and re-layouts, block_convolve(): toeplitz = kernel[:, lag] * causal[None, :, :]  80 us
    all_gather x1, waiting for transfers between devices, per_device(): gathered = lax.all_gather(tokens, ('chan', 'rep'), axis=1, tiled=True)  36.8 us
    dot_general x3, matrix products, per_device(): lax.dot_general(weight_piece, gathered, (((0,), (1,)), ((), ())), preferr...  28.5 us
  transfers between devices with their start and end apart: 6, of which 4 were waited for; matrix products, arithmetic and copies ran while one was open for 21% of the time, Pallas kernels for 0%

commit v1 on v0

--- a/solution.py
+++ b/solution.py
@@ -1,9 +1,15 @@
 import jax
 import jax.numpy as jnp
 from jax import lax
+from jax.experimental import pallas as pl
+from jax.experimental.pallas import tpu as pltpu
 from jax.sharding import PartitionSpec as P
 
 BLOCK = 128
+SUBLANES, LANES = 8, 128
+TILE = 256
+UNROLL = 4
+GATHER_BYTES = 24 << 20
 
 
 HIGHEST_PRECISION = lax.Precision.HIGHEST
@@ -100,6 +106,248 @@
     return (gated_rows.T, new_state)
 
 
+def ring(size, step):
+    return [(i, (i + step) % size) for i in range(size)]
+
+
+def gather_line(own, axis, size):
+    place = lax.axis_index(axis)
+    upward, downward = {0: own}, {0: own}
+    for step in range(1, size):
+        upward[step] = lax.ppermute(
+            upward[step - 1], axis, [(i, i + 1) for i in range(step - 1, size - 1)]
+        )
+        downward[step] = lax.ppermute(
+            downward[step - 1], axis, [(i + 1, i) for i in range(size - step)]
+        )
+    arrivals = []
+    for i in range(size):
+        order = []
+        for step in range(1, size):
+            if i - step >= 0:
+                order.append(("up", step, i - step))
+            if i + step < size:
+                order.append(("down", step, i + step))
+        arrivals.append(order)
+    shards = [(own, place)]
+    for j in range(size - 1):
+        value, owner = None, jnp.int32(0)
+        for i in range(size):
+            way, step, origin = arrivals[i][j]
+            candidate = upward[step] if way == "up" else downward[step]
+            value = candidate if value is None else jnp.where(place == i, candidate, value)
+            owner = jnp.where(place == i, origin, owner)
+        shards.append((value, owner))
+    return shards
+
+
+def exchange_weights(weights, seq, parts):
+    place, part = lax.axis_index("seq"), lax.axis_index("parts")
+    depth = weights[0].shape[0]
+    share, width = depth // parts, weights[0].shape[1] // seq
+
+    def block(target, first_row, rows):
+        return jnp.concatenate(
+            [lax.dynamic_slice(w, (first_row, target * width), (rows, width)) for w in weights], axis=1
+        )
+
+    whole = jnp.zeros((seq, parts, share, width * len(weights)), weights[0].dtype)
+    own = block(place, 0, depth).reshape(1, parts, share, -1)
+    whole = lax.dynamic_update_slice(whole, own, (place, 0, 0, 0))
+    for step in range(1, seq):
+        piece = block((place + step) % seq, part * share, share)
+        piece = lax.ppermute(piece, "seq", ring(seq, step))
+        origin = (place - step) % seq
+        whole = lax.dynamic_update_slice(whole, piece[None, None], (origin, part, 0, 0))
+        for turn in range(1, parts):
+            other = lax.ppermute(piece, "parts", ring(parts, turn))
+            whole = lax.dynamic_update_slice(
+                whole, other[None, None], (origin, (part - turn) % parts, 0, 0)
+            )
+    return whole.reshape(seq, depth, -1)
+
+
+def gather_tokens(tokens, seq, chan, rep):
+    x_place, core = lax.axis_index("chan"), lax.axis_index("rep")
+    rows, width = tokens.shape
+    whole = jnp.zeros((seq, chan * rep, rows, width), tokens.dtype)
+    for value, owner in gather_line(tokens, "seq", seq):
+        for dx in range(chan):
+            over_x = lax.ppermute(value, "chan", ring(chan, dx)) if dx else value
+            for dr in range(rep):
+                chunk = lax.ppermute(over_x, "rep", ring(rep, dr)) if dr else over_x
+                feature = ((x_place - dx) % chan) * rep + (core - dr) % rep
+                whole = lax.dynamic_update_slice(whole, chunk[None, None], (owner, feature, 0, 0))
+    return whole
+
+
+def mode_kernel(x_hbm, w_hbm, modes_ref, conv_ref, state_ref, x_buf, w_buf, prod, out, ends, x_sem, w_sem):
+    seq, quarters, rows, depth = x_buf.shape
+    groups, length, lane_width = prod.shape
+    channels = groups * lane_width
+    modes = modes_ref.shape[1]
+    w_copy = pltpu.make_async_copy(w_hbm, w_buf, w_sem)
+    w_copy.start()
+    copies = [pltpu.make_async_copy(x_hbm.at[i], x_buf.at[i], x_sem.at[i]) for i in range(seq)]
+    for copy in copies:
+        copy.start()
+    w_copy.wait()
+    tile = min(rows, TILE)
+    for i in range(seq):
+        copies[i].wait()
+
+        @pl.loop(0, rows // tile)
+        def _(t):
+            at = pl.ds(pl.multiple_of(t * tile, tile), tile)
+            acc = jnp.zeros((tile, 2 * channels), jnp.float32)
+            for q in range(quarters):
+                acc += jnp.dot(x_buf[i, q, at, :], w_buf[q], preferred_element_type=jnp.float32)
+            rounded = acc.astype(jnp.bfloat16).astype(jnp.float32)
+            product = (rounded[:, :channels] * rounded[:, channels:]).astype(jnp.bfloat16)
+            for g in range(groups):
+                prod[g, pl.ds(pl.multiple_of(i * rows + t * tile, tile), tile), :] = product[
+                    :, g * LANES : (g + 1) * LANES
+                ].astype(jnp.float32)
+
+    span = length // SUBLANES
+    for g in range(groups):
+        lanes = pl.ds(g * LANES, LANES)
+        signal, result = prod.at[g], out.at[g]
+        decay = [jnp.broadcast_to(modes_ref[0, m : m + 1, lanes], (SUBLANES, LANES)) for m in range(modes)]
+        weight = [jnp.broadcast_to(modes_ref[2, m : m + 1, lanes], (SUBLANES, LANES)) for m in range(modes)]
+
+        def sums(i, states):
+            for u in range(UNROLL):
+                value = signal[pl.ds(i * UNROLL + u, SUBLANES, stride=span), :]
+                states = tuple(a * s + value for a, s in zip(decay, states))
+            return states
+
+        zero = jnp.zeros((SUBLANES, LANES), jnp.float32)
+        states = lax.fori_loop(0, span // UNROLL, sums, (zero,) * modes)
+        for m in range(modes):
+            ends[m] = states[m]
+        state = modes_ref[3, :, lanes]
+        over_span = modes_ref[1, :, lanes]
+        for b in range(SUBLANES):
+            end = ends[:, b, :]
+            ends[:, b, :] = state
+            state = over_span * state + end
+        state_ref[:, lanes] = state * modes_ref[4, :, lanes]
+
+        def outputs(i, states):
+            for u in range(UNROLL):
+                at = pl.ds(i * UNROLL + u, SUBLANES, stride=span)
+                value = signal[at, :]
+                states = tuple(a * s + value for a, s in zip(decay, states))
+                terms = [w * s for w, s in zip(weight, states)]
+                while len(terms) > 1:
+                    terms = [sum(terms[k : k + 2][1:], terms[k]) for k in range(0, len(terms), 2)]
+                result[at, :] = terms[0]
+            return states
+
+        lax.fori_loop(0, span // UNROLL, outputs, tuple(ends[m] for m in range(modes)))
+        conv_ref[:, lanes] = result[...].astype(jnp.bfloat16)
+
+
+def key_value_modes(x_all, w_all, decay_rate, residue, carried):
+    seq, quarters, rows, depth = x_all.shape
+    length, channels = seq * rows, decay_rate.shape[0]
+    modes = decay_rate.shape[1]
+    scale = mode_scale(decay_rate)
+    table = jnp.stack(
+        [
+            jnp.exp(-decay_rate),
+            jnp.exp(-decay_rate * (length // SUBLANES)),
+            residue * scale,
+            carried / scale,
+            scale,
+        ]
+    ).transpose(0, 2, 1)
+    conv, state = pl.pallas_call(
+        mode_kernel,
+        out_shape=(
+            jax.ShapeDtypeStruct((length, channels), jnp.bfloat16),
+            jax.ShapeDtypeStruct((modes, channels), jnp.float32),
+        ),
+        in_specs=[
+            pl.BlockSpec(memory_space=pl.ANY),
+            pl.BlockSpec(memory_space=pl.ANY),
+            pl.BlockSpec(memory_space=pltpu.VMEM),
+        ],
+        out_specs=(pl.BlockSpec(memory_space=pltpu.VMEM), pl.BlockSpec(memory_space=pltpu.VMEM)),
+        scratch_shapes=[
+            pltpu.VMEM(x_all.shape, x_all.dtype),
+            pltpu.VMEM(w_all.shape, w_all.dtype),
+            pltpu.VMEM((channels // LANES, length, LANES), jnp.float32),
+            pltpu.VMEM((channels // LANES, length, LANES), jnp.float32),
+            pltpu.VMEM((modes, SUBLANES, LANES), jnp.float32),
+            pltpu.SemaphoreType.DMA((seq,)),
+            pltpu.SemaphoreType.DMA,
+        ],
+        compiler_params=pltpu.CompilerParams(vmem_limit_bytes=44 << 20),
+        cost_estimate=pl.CostEstimate(
+            flops=4 * length * depth * quarters * channels,
+            bytes_accessed=2 * (x_all.size + w_all.size),
+            transcendentals=0,
+        ),
+        name="key_value_modes",
+    )(x_all, w_all, table)
+    return conv, state.T
+
+
+def gate_kernel(where_ref, x_ref, w_ref, conv_ref, out_ref):
+    del where_ref
+    quarters = x_ref.shape[1]
+    acc = jnp.zeros(out_ref.shape, jnp.float32)
+    for q in range(quarters):
+        acc += jnp.dot(x_ref[0, q], w_ref[q], preferred_element_type=jnp.float32)
+    query = acc.astype(jnp.bfloat16).astype(jnp.float32)
+    out_ref[...] = (query * conv_ref[...].astype(jnp.float32)).astype(jnp.bfloat16)
+
+
+def gate(x_all, w_all, conv, owner):
+    seq, quarters, rows, depth = x_all.shape
+    channels = conv.shape[1]
+    return pl.pallas_call(
+        gate_kernel,
+        out_shape=jax.ShapeDtypeStruct((rows, channels), jnp.bfloat16),
+        grid_spec=pltpu.PrefetchScalarGridSpec(
+            num_scalar_prefetch=1,
+            grid=(1,),
+            in_specs=[
+                pl.BlockSpec((1, quarters, rows, depth), lambda g, w: (w[0], 0, 0, 0)),
+                pl.BlockSpec(w_all.shape, lambda g, w: (0, 0, 0)),
+                pl.BlockSpec((rows, channels), lambda g, w: (w[0], 0)),
+            ],
+            out_specs=pl.BlockSpec((rows, channels), lambda g, w: (0, 0)),
+        ),
+        compiler_params=pltpu.CompilerParams(vmem_limit_bytes=32 << 20),
+        cost_estimate=pl.CostEstimate(
+            flops=2 * rows * depth * quarters * channels,
+            bytes_accessed=2 * (x_all.size // seq + w_all.size),
+            transcendentals=0,
+        ),
+        name="gate",
+    )(owner.reshape(1).astype(jnp.int32), x_all, w_all, conv)
+
+
+def by_channels(sizes, tokens, w_query, w_key, w_value, decay_rate, residue, carried):
+    seq, chan, rep, parts = sizes["seq"], sizes["chan"], sizes["rep"], sizes["parts"]
+    place = lax.axis_index("seq")
+    x_all = gather_tokens(tokens, seq, chan, rep)
+    w_key_value = exchange_weights((w_key, w_value), seq, parts)
+    w_own_query = exchange_weights((w_query,), seq, parts)
+    conv, new_state = key_value_modes(x_all, w_key_value, decay_rate, residue, carried)
+    rows, channels = tokens.shape[0], decay_rate.shape[0]
+    gated = jnp.zeros((seq, rows, channels), jnp.bfloat16)
+    for step in sorted(range(seq), key=lambda d: -min(d, seq - d)):
+        piece = gate(x_all, w_own_query, conv, (place + step) % seq)
+        if step:
+            piece = lax.ppermute(piece, "seq", ring(seq, step))
+        gated = lax.dynamic_update_slice(gated, piece[None], ((place - step) % seq, 0, 0))
+    return gated.transpose(1, 0, 2).reshape(rows, seq * channels), new_state
+
+
 def solution(mesh):
     in_specs = (
         P(("parts", "seq"), ("chan", "rep")),
@@ -111,6 +359,16 @@
         P(("parts", "chan", "rep", "seq"), None),
     )
     out_specs = (P(("parts", "seq"), ("chan", "rep")), P(("parts", "chan", "rep", "seq"), None))
+    sizes = dict(mesh.shape)
+
+    def program(*arrays):
+        tokens = arrays[0]
+        part_bytes = tokens.size * tokens.dtype.itemsize * sizes["seq"] * sizes["chan"] * sizes["rep"]
+        fits = part_bytes <= GATHER_BYTES and sizes["seq"] == sizes["chan"] * sizes["rep"]
+        if fits:
+            return by_channels(sizes, *arrays)
+        return per_device(*arrays)
+
     return jax.shard_map(
-        per_device, mesh=mesh, in_specs=in_specs, out_specs=out_specs, check_vma=False
-    )
+        program, mesh=mesh, in_specs=in_specs, out_specs=out_specs, check_vma=False
+    )

time: 893 us -> 300 us (0.34)
  waiting for transfers between devices: 470 us -> 154 us
  local copies, waits for them, and re-layouts: 337 us -> 52.2 us
  matrix products: 50.3 us -> 0 us
  Pallas kernels: 0 us -> 40.5 us
  starting transfers between devices: 8.72 us -> 41.4 us
  between operations: 14.1 us -> 1.15 us
    all_gather x4 -> x0, waiting for transfers between devices: 468 us -> none  [the longest x1 151 us: per_device(): lax.all_gather(w_query, 'seq', axis=0, tiled=True)]
    pad x6 -> x0, local copies, waits for them, and re-layouts: 158 us -> none  [block_sums(): lax.associative_scan(combine_states, (step_decay, block_ends), axis=1)]
    ppermute x0 -> x33, waiting for transfers between devices: none -> 154 us  [the longest x4 55.8 us: gather_tokens(): over_x = lax.ppermute(value, 'chan', ring(chan, dx)) if dx else value]
    unnamed x33 -> x25, local copies, waits for them, and re-layouts: 82.2 us -> 1.25 us
    gather x2 -> x0, local copies, waits for them, and re-layouts: 80 us -> none  [block_convolve(): toeplitz = kernel[:, lag] * causal[None, :, :]]
    dot_general x6 -> x0, matrix products: 50.3 us -> none  [the longest x3 28.5 us: per_device(): lax.dot_general(weight_piece, gathered, (((0,), (1,)), ((), ())), preferr...]
    ppermute x0 -> x33, starting transfers between devices: none -> 41.4 us  [the longest x6 11.7 us: exchange_weights(): piece = lax.ppermute(piece, 'seq', ring(seq, step))]
    pallas_call x0 -> x5, Pallas kernels: none -> 40.5 us  [the longest x1 26.7 us: key_value_modes(): pl.pallas_call(mode_kernel, out_shape=(jax.ShapeDtypeStruct((length, chan...]
  transfers between devices with their start and end apart: 6 -> 33, of which waited for: 4 -> 15; matrix products, arithmetic and copies ran while one was open for 21% -> 16% of each run, Pallas kernels for 0% -> 3%
where the time goes in v1:
time: 300 us; the launch traced here: 299 us
  waiting for transfers between devices  154 us (51%)
  local copies, waits for them, and re-layouts  52.2 us (17%)
  starting transfers between devices  41.4 us (14%)
  Pallas kernels  40.5 us (14%)
  other arithmetic  9.82 us (3%)
    ppermute x4, waiting for transfers between devices, gather_tokens(): over_x = lax.ppermute(value, 'chan', ring(chan, dx)) if dx else value  55.8 us
    ppermute x6, waiting for transfers between devices, exchange_weights(): piece = lax.ppermute(piece, 'seq', ring(seq, step))  47.2 us
    pallas_call x1, Pallas kernels, key_value_modes(): pl.pallas_call(mode_kernel, out_shape=(jax.ShapeDtypeStruct((length, chan...  26.7 us
    ppermute x3, waiting for transfers between devices, gather_line(): lax.ppermute(downward[step - 1], axis, [(i + 1, i) for i in range(size -...  25.4 us
    dynamic_update_slice x13, local copies, waits for them, and re-layouts, gather_tokens(): lax.dynamic_update_slice(whole, chunk[None, None], (owner, feature, 0, 0))  19.9 us
    ppermute x6, waiting for transfers between devices, exchange_weights(): other = lax.ppermute(piece, 'parts', ring(parts, turn))  14.9 us
    pallas_call x4, Pallas kernels, gate(): pl.pallas_call(gate_kernel, out_shape=jax.ShapeDtypeStruct((rows, channel...  13.8 us
    ppermute x6, starting transfers between devices, exchange_weights(): piece = lax.ppermute(piece, 'seq', ring(seq, step))  11.7 us
  transfers between devices with their start and end apart: 33, of which 15 were waited for; matrix products, arithmetic and copies ran while one was open for 16% of the time, Pallas kernels for 3%

profile of v1, /device:TPU:0, one launch (start us, length us, event | category | flops | bytes accessed | tf_op | source)
XLA Modules:
  0.0 299.2 jit_solution(1568224203032872377)
XLA Ops:
  0.6 3.0 %collective-permute-start.1 = (bf16[512,1024]{1,0:T(8,128)(2,1)}, bf16[512,1024]{1,0:T(8,128)(2,1)S(1)}, u32[]{:S(2)}, u32[]{:S(2)}) collective-permute-start(bf16[512,1024]{1,0:T(8,128)(2,1)} %param.7), channel_id=1, source_target_pairs={{0,2},{2,0},{1,3},{3,1},{4,6},{6,4},{5,7},{7,5},{8,10},{10,8},{9,1... | collective-permute-start | bytes 3145736 | tf_op jit(solution)/shard_map/ppermute | solution.py:176
  3.6 23.4 %collective-permute-done.1 = bf16[512,1024]{1,0:T(8,128)(2,1)S(1)} collective-permute-done((bf16[512,1024]{1,0:T(8,128)(2,1)}, bf16[512,1024]{1,0:T(8,128)(2,1)S(1)}, u32[]{:S(2)}, u32[]{:S(2)}) %collective-permute-start.1) | collective-permute-done | bytes 1048608 | tf_op jit(solution)/shard_map/ppermute | solution.py:176
  28.3 5.6 %collective-permute-start.3 = (bf16[512,1024]{1,0:T(8,128)(2,1)}, bf16[512,1024]{1,0:T(8,128)(2,1)}, u32[]{:S(2)}, u32[]{:S(2)}) collective-permute-start(bf16[512,1024]{1,0:T(8,128)(2,1)} %param.7), channel_id=1, source_target_pairs={{0,4},{4,8},{8,12},{1,5},{5,9},{9,13},{2,6},{6,10},{10,14},{3,7},{... | collective-permute-start | bytes 3145736 | tf_op jit(solution)/shard_map/ppermute | solution.py:117
  36.1 6.0 %broadcast_in_dim.109 = bf16[4,4,512,1024]{3,2,1,0:T(8,128)(2,1)} broadcast(bf16[]{:T(256)} %constant.182.clone.1), dimensions={} | broadcast | bytes 16777218 | tf_op jit(solution)/shard_map/broadcast_in_dim | solution.py:173
  43.2 2.3 bitcast_dynamic-update-slice_fusion.14
  47.6 7.2 %collective-permute-done.4 = bf16[512,1024]{1,0:T(8,128)(2,1)S(1)} collective-permute-done((bf16[512,1024]{1,0:T(8,128)(2,1)}, bf16[512,1024]{1,0:T(8,128)(2,1)S(1)}, u32[]{:S(2)}, u32[]{:S(2)}) %collective-permute-start.4) | collective-permute-done | bytes 1048608 | tf_op jit(solution)/shard_map/ppermute | solution.py:120
  56.1 3.1 %bitcast_dynamic-update-slice_fusion.11 = (bf16[4,4,512,1024]{3,2,1,0:T(8,128)(2,1)}, bf16[512,1024]{1,0:T(8,128)(2,1)}) fusion(bf16[4,4,512,1024]{3,2,1,0:T(8,128)(2,1)} %bitcast_dynamic-update-slice_fusion.12, s32[]{:T(128)S(6)} %select_n.358, s32[]{:T(128)S(6)} %select_n.343, bf16[512,1024]{1,0:T(8,128)(2,1)} %collective-permute-done.3, ...), kind=kLoop, calls=%fused_computation.15 | loop fusion | flops 1572864 | bytes 4194315 | tf_op jit(solution)/shard_map/dynamic_update_slice | solution.py:180
  61.7 2.5 collective-permute-start.24
  65.5 2.3 broadcast_in_dim.133
  69.9 14.2 %collective-permute-done.6 = bf16[512,1024]{1,0:T(8,128)(2,1)} collective-permute-done((bf16[512,1024]{1,0:T(8,128)(2,1)}, bf16[512,1024]{1,0:T(8,128)(2,1)}, u32[]{:S(2)}, u32[]{:S(2)}) %collective-permute-start.6) | collective-permute-done | bytes 1048608 | tf_op jit(solution)/shard_map/ppermute | solution.py:176
  87.1 6.5 %collective-permute-start.18 = (bf16[512,256]{1,0:T(8,128)(2,1)}, bf16[512,256]{1,0:T(8,128)(2,1)}, u32[]{:S(2)}, u32[]{:S(2)}) collective-permute-start(bf16[512,256]{1,0:T(8,128)(2,1)} %get-tuple-element.19), channel_id=1, source_target_pairs={{0,4},{4,8},{8,12},{12,0},{1,5},{5,9},{9,13},{13,1},{2,6},{6,10},{... | collective-permute-start | bytes 786440 | tf_op jit(solution)/shard_map/ppermute | solution.py:159
  93.5 2.3 bitcast_dynamic-update-slice_fusion.10
  95.8 2.3 bitcast_dynamic-update-slice_fusion.9
  98.2 2.4 bitcast_dynamic-update-slice_fusion.8
  100.6 18.2 %collective-permute-done.9 = bf16[512,1024]{1,0:T(8,128)(2,1)S(1)} collective-permute-done((bf16[512,1024]{1,0:T(8,128)(2,1)S(1)}, bf16[512,1024]{1,0:T(8,128)(2,1)S(1)}, u32[]{:S(2)}, u32[]{:S(2)}) %collective-permute-start.9) | collective-permute-done | bytes 1048608 | tf_op jit(solution)/shard_map/ppermute | solution.py:120
  127.2 4.2 %collective-permute-done.20 = bf16[512,256]{1,0:T(8,128)(2,1)} collective-permute-done((bf16[512,256]{1,0:T(8,128)(2,1)}, bf16[512,256]{1,0:T(8,128)(2,1)}, u32[]{:S(2)}, u32[]{:S(2)}) %collective-permute-start.20) | collective-permute-done | bytes 262176 | tf_op jit(solution)/shard_map/ppermute | solution.py:159
  131.3 2.7 collective-permute-start.26
  134.5 11.7 %collective-permute-done.11 = bf16[512,1024]{1,0:T(8,128)(2,1)} collective-permute-done((bf16[512,1024]{1,0:T(8,128)(2,1)}, bf16[512,1024]{1,0:T(8,128)(2,1)}, u32[]{:S(2)}, u32[]{:S(2)}) %collective-permute-start.11) | collective-permute-done | bytes 1048608 | tf_op jit(solution)/shard_map/ppermute | solution.py:176
  152.3 34.7 %collective-permute-done.22 = bf16[512,256]{1,0:T(8,128)(2,1)S(1)} collective-permute-done((bf16[512,256]{1,0:T(8,128)(2,1)}, bf16[512,256]{1,0:T(8,128)(2,1)S(1)}, u32[]{:S(2)}, u32[]{:S(2)}) %collective-permute-start.22) | collective-permute-done | bytes 262176 | tf_op jit(solution)/shard_map/ppermute | solution.py:159
  192.3 8.4 %collective-permute-done.28 = bf16[512,512]{1,0:T(8,128)(2,1)S(1)} collective-permute-done((bf16[512,512]{1,0:T(8,128)(2,1)S(1)}, bf16[512,512]{1,0:T(8,128)(2,1)S(1)}, u32[]{:S(2)}, u32[]{:S(2)}) %collective-permute-start.28) | collective-permute-done | bytes 524320 | tf_op jit(solution)/shard_map/ppermute | solution.py:159
  206.4 3.2 %collective-permute-done.25 = bf16[512,512]{1,0:T(8,128)(2,1)S(1)} collective-permute-done((bf16[512,512]{1,0:T(8,128)(2,1)}, bf16[512,512]{1,0:T(8,128)(2,1)S(1)}, u32[]{:S(2)}, u32[]{:S(2)}) %collective-permute-start.25) | collective-permute-done | bytes 524320 | tf_op jit(solution)/shard_map/ppermute | solution.py:163
  211.3 9.6 %collective-permute-done.27 = bf16[512,512]{1,0:T(8,128)(2,1)S(1)} collective-permute-done((bf16[512,512]{1,0:T(8,128)(2,1)S(1)}, bf16[512,512]{1,0:T(8,128)(2,1)S(1)}, u32[]{:S(2)}, u32[]{:S(2)}) %collective-permute-start.27) | collective-permute-done | bytes 524320 | tf_op jit(solution)/shard_map/ppermute | solution.py:163
  221.7 6.5 %collective-permute-done.16 = bf16[512,1024]{1,0:T(8,128)(2,1)S(1)} collective-permute-done((bf16[512,1024]{1,0:T(8,128)(2,1)S(1)}, bf16[512,1024]{1,0:T(8,128)(2,1)S(1)}, u32[]{:S(2)}, u32[]{:S(2)}) %collective-permute-start.16) | collective-permute-done | bytes 1048608 | tf_op jit(solution)/shard_map/ppermute | solution.py:176
  235.1 26.7 %key_value_modes.1 = (bf16[2048,256]{1,0:T(8,128)(2,1)S(1)}, f32[16,256]{1,0:T(8,128)}) custom-call(bf16[4,4,512,1024]{3,2,1,0:T(8,128)(2,1)} %bitcast_dynamic-update-slice_fusion.x_hbm.x_ref, bf16[4,1024,512]{2,1,0:T(8,128)(2,1)} %bitcast.32.w_hbm, f32[5,16,256]{2,1,0:T(8,128)S(1)} %bitcast.91), custom_call_target="tpu_custom_call" | custom-call | flops 8589934592 | bytes 20971520 | tf_op jit(solution)/shard_map/key_value_modes/pallas_call | solution.py:266
  261.8 3.4 %gate.4 = bf16[512,256]{1,0:T(8,128)(2,1)S(1)} custom-call(s32[1]{0:T(128)} %bitcast.where_ref, bf16[4,4,512,1024]{3,2,1,0:T(8,128)(2,1)} %bitcast_dynamic-update-slice_fusion.x_hbm.x_ref, bf16[4,1024,256]{2,1,0:T(8,128)(2,1)S(1)} %bitcast.86, bf16[2048,256]{1,0:T(8,128)(2,1)S(1)} %get-tuple-element.4.conv_ref), custom_call_target="tpu_custom_call" | custom-call | flops 1073741824 | bytes 6291456 | tf_op jit(solution)/shard_map/gate/pallas_call | solution.py:311
  266.1 3.4 %gate.5 = bf16[512,256]{1,0:T(8,128)(2,1)S(1)} custom-call(s32[1]{0:T(128)} %bitcast.40.where_ref, bf16[4,4,512,1024]{3,2,1,0:T(8,128)(2,1)} %bitcast_dynamic-update-slice_fusion.x_hbm.x_ref, bf16[4,1024,256]{2,1,0:T(8,128)(2,1)S(1)} %bitcast.87, bf16[2048,256]{1,0:T(8,128)(2,1)S(1)} %get-tuple-element.4.conv_ref), custom_call_target="tpu_custom_call" | custom-call | flops 1073741824 | bytes 6291456 | tf_op jit(solution)/shard_map/gate/pallas_call | solution.py:311
  270.6 3.4 %gate.7 = bf16[512,256]{1,0:T(8,128)(2,1)S(1)} custom-call(s32[1]{0:T(128)} %bitcast.44.where_ref, bf16[4,4,512,1024]{3,2,1,0:T(8,128)(2,1)} %bitcast_dynamic-update-slice_fusion.x_hbm.x_ref, bf16[4,1024,256]{2,1,0:T(8,128)(2,1)S(1)} %bitcast.88, bf16[2048,256]{1,0:T(8,128)(2,1)S(1)} %get-tuple-element.4.conv_ref), custom_call_target="tpu_custom_call" | custom-call | flops 1073741824 | bytes 6291456 | tf_op jit(solution)/shard_map/gate/pallas_call | solution.py:311
  274.0 3.4 %gate.6 = bf16[512,256]{1,0:T(8,128)(2,1)S(1)} custom-call(s32[1]{0:T(128)} %bitcast.42.where_ref, bf16[4,4,512,1024]{3,2,1,0:T(8,128)(2,1)} %bitcast_dynamic-update-slice_fusion.x_hbm.x_ref, bf16[4,1024,256]{2,1,0:T(8,128)(2,1)S(1)} %bitcast.89, bf16[2048,256]{1,0:T(8,128)(2,1)S(1)} %get-tuple-element.4.conv_ref), custom_call_target="tpu_custom_call" | custom-call | flops 1073741824 | bytes 6291456 | tf_op jit(solution)/shard_map/gate/pallas_call | solution.py:311
  277.9 2.9 collective-permute-start.32
  280.8 5.2 %collective-permute-done.30 = bf16[512,256]{1,0:T(8,128)(2,1)S(1)} collective-permute-done((bf16[512,256]{1,0:T(8,128)(2,1)S(1)}, bf16[512,256]{1,0:T(8,128)(2,1)S(1)}, u32[]{:S(2)}, u32[]{:S(2)}) %collective-permute-start.30) | collective-permute-done | bytes 262176 | tf_op jit(solution)/shard_map/ppermute | solution.py:346
  286.1 4.4 %collective-permute-done.32 = bf16[512,256]{1,0:T(8,128)(2,1)S(1)} collective-permute-done((bf16[512,256]{1,0:T(8,128)(2,1)S(1)}, bf16[512,256]{1,0:T(8,128)(2,1)S(1)}, u32[]{:S(2)}, u32[]{:S(2)}) %collective-permute-start.32) | collective-permute-done | bytes 262176 | tf_op jit(solution)/shard_map/ppermute | solution.py:346
  291.3 6.7 %dynamic_update_slice.135 = bf16[4,512,256]{2,0,1:T(4,128)(2,1)S(1)} dynamic-update-slice(bf16[4,512,256]{2,0,1:T(4,128)(2,1)S(1)} %copy.9, bf16[1,512,256]{2,0,1:T(2,128)(2,1)S(1)} %copy.10, s32[]{:T(128)S(6)} %select_n.390, s32[]{:T(128)} %constant.186.clone.1, s32[]{:T(128)} %constant.186.clone.1) | dynamic-update-slice | bytes 524292 | tf_op jit(solution)/shard_map/dynamic_update_slice | solution.py:347
  (117 shorter events, 56.4 us)
Async XLA Ops:
  0.6 26.4 %collective-permute-start.1 = (bf16[512,1024]{1,0:T(8,128)(2,1)}, bf16[512,1024]{1,0:T(8,128)(2,1)S(1)}, u32[]{:S(2)}, u32[]{:S(2)}) collective-permute-start(bf16[512,1024]{1,0:T(8,128)(2,1)} %param.7), channel_id=1, source_target_pairs={{0,2},{2,0},{1,3},{3,1},{4,6},{6,4},{5,7},{7,5},{8,10},{10,8},{9,1... | collective-permute-start | bytes 3145736 | tf_op jit(solution)/shard_map/ppermute | solution.py:176
  3.6 39.6 %collective-permute-start = (bf16[512,1024]{1,0:T(8,128)(2,1)}, bf16[512,1024]{1,0:T(8,128)(2,1)}, u32[]{:S(2)}, u32[]{:S(2)}) collective-permute-start(bf16[512,1024]{1,0:T(8,128)(2,1)} %param.7), channel_id=1, source_target_pairs={{0,1},{1,0},{2,3},{3,2},{4,5},{5,4},{6,7},{7,6},{8,9},{9,8},{10,11... | collective-permute-start | bytes 3145736 | tf_op jit(solution)/shard_map/ppermute | solution.py:178
  27.0 19.5 %collective-permute-start.2 = (bf16[512,1024]{1,0:T(8,128)(2,1)S(1)}, bf16[512,1024]{1,0:T(8,128)(2,1)S(1)}, u32[]{:S(2)}, u32[]{:S(2)}) collective-permute-start(bf16[512,1024]{1,0:T(8,128)(2,1)S(1)} %collective-permute-done.1), channel_id=1, source_target_pairs={{0,1},{1,0},{2,3},{3,2},{4,5},{5,4},{6,7},{7,6},{8,9},{9,8},{10,11... | collective-permute-start | bytes 3145736 | tf_op jit(solution)/shard_map/ppermute | solution.py:178
  27.0 27.8 %collective-permute-start.4 = (bf16[512,1024]{1,0:T(8,128)(2,1)}, bf16[512,1024]{1,0:T(8,128)(2,1)S(1)}, u32[]{:S(2)}, u32[]{:S(2)}) collective-permute-start(bf16[512,1024]{1,0:T(8,128)(2,1)} %param.7), channel_id=1, source_target_pairs={{4,0},{8,4},{12,8},{5,1},{9,5},{13,9},{6,2},{10,6},{14,10},{7,3},{... | collective-permute-start | bytes 3145736 | tf_op jit(solution)/shard_map/ppermute | solution.py:120
  28.3 27.8 %collective-permute-start.3 = (bf16[512,1024]{1,0:T(8,128)(2,1)}, bf16[512,1024]{1,0:T(8,128)(2,1)}, u32[]{:S(2)}, u32[]{:S(2)}) collective-permute-start(bf16[512,1024]{1,0:T(8,128)(2,1)} %param.7), channel_id=1, source_target_pairs={{0,4},{4,8},{8,12},{1,5},{5,9},{9,13},{2,6},{6,10},{10,14},{3,7},{... | collective-permute-start | bytes 3145736 | tf_op jit(solution)/shard_map/ppermute | solution.py:117
  59.2 24.9 %collective-permute-start.6 = (bf16[512,1024]{1,0:T(8,128)(2,1)}, bf16[512,1024]{1,0:T(8,128)(2,1)}, u32[]{:S(2)}, u32[]{:S(2)}) collective-permute-start(bf16[512,1024]{1,0:T(8,128)(2,1)} %get-tuple-element.11), channel_id=1, source_target_pairs={{0,2},{2,0},{1,3},{3,1},{4,6},{6,4},{5,7},{7,5},{8,10},{10,8},{9,1... | collective-permute-start | bytes 3145736 | tf_op jit(solution)/shard_map/ppermute | solution.py:176
  61.7 85.5 %collective-permute-start.24 = (bf16[512,512]{1,0:T(8,128)(2,1)}, bf16[512,512]{1,0:T(8,128)(2,1)}, u32[]{:S(2)}, u32[]{:S(2)}) collective-permute-start(bf16[512,512]{1,0:T(8,128)(2,1)} %pad_maximum_fusion.1), channel_id=1, source_target_pairs={{0,4},{4,8},{8,12},{12,0},{1,5},{5,9},{9,13},{13,1},{2,6},{6,10},{... | collective-permute-start | bytes 1572872 | tf_op jit(solution)/shard_map/ppermute | solution.py:159
  68.9 18.1 %collective-permute-start.5 = (bf16[512,1024]{1,0:T(8,128)(2,1)}, bf16[512,1024]{1,0:T(8,128)(2,1)}, u32[]{:S(2)}, u32[]{:S(2)}) collective-permute-start(bf16[512,1024]{1,0:T(8,128)(2,1)} %get-tuple-element.11), channel_id=1, source_target_pairs={{0,1},{1,0},{2,3},{3,2},{4,5},{5,4},{6,7},{7,6},{8,9},{9,8},{10,11... | collective-permute-start | bytes 3145736 | tf_op jit(solution)/shard_map/ppermute | solution.py:178
  84.1 14.0 %collective-permute-start.7 = (bf16[512,1024]{1,0:T(8,128)(2,1)}, bf16[512,1024]{1,0:T(8,128)(2,1)}, u32[]{:S(2)}, u32[]{:S(2)}) collective-permute-start(bf16[512,1024]{1,0:T(8,128)(2,1)} %collective-permute-done.6), channel_id=1, source_target_pairs={{0,1},{1,0},{2,3},{3,2},{4,5},{5,4},{6,7},{7,6},{8,9},{9,8},{10,11... | collective-permute-start | bytes 3145736 | tf_op jit(solution)/shard_map/ppermute | solution.py:178
  85.0 33.8 %collective-permute-start.9 = (bf16[512,1024]{1,0:T(8,128)(2,1)S(1)}, bf16[512,1024]{1,0:T(8,128)(2,1)S(1)}, u32[]{:S(2)}, u32[]{:S(2)}) collective-permute-start(bf16[512,1024]{1,0:T(8,128)(2,1)S(1)} %collective-permute-done.4), channel_id=1, source_target_pairs={{4,0},{8,4},{5,1},{9,5},{6,2},{10,6},{7,3},{11,7},{20,16},{24,20},... | collective-permute-start | bytes 3145736 | tf_op jit(solution)/shard_map/ppermute | solution.py:120
  86.3 32.5 %collective-permute-start.8 = (bf16[512,1024]{1,0:T(8,128)(2,1)}, bf16[512,1024]{1,0:T(8,128)(2,1)S(1)}, u32[]{:S(2)}, u32[]{:S(2)}) collective-permute-start(bf16[512,1024]{1,0:T(8,128)(2,1)} %collective-permute-done.3), channel_id=1, source_target_pairs={{4,8},{8,12},{5,9},{9,13},{6,10},{10,14},{7,11},{11,15},{20,24},{2... | collective-permute-start | bytes 3145736 | tf_op jit(solution)/shard_map/ppermute | solution.py:117
  87.1 37.1 %collective-permute-start.18 = (bf16[512,256]{1,0:T(8,128)(2,1)}, bf16[512,256]{1,0:T(8,128)(2,1)}, u32[]{:S(2)}, u32[]{:S(2)}) collective-permute-start(bf16[512,256]{1,0:T(8,128)(2,1)} %get-tuple-element.19), channel_id=1, source_target_pairs={{0,4},{4,8},{8,12},{12,0},{1,5},{5,9},{9,13},{13,1},{2,6},{6,10},{... | collective-permute-start | bytes 786440 | tf_op jit(solution)/shard_map/ppermute | solution.py:159
  98.1 33.2 %collective-permute-start.20 = (bf16[512,256]{1,0:T(8,128)(2,1)}, bf16[512,256]{1,0:T(8,128)(2,1)}, u32[]{:S(2)}, u32[]{:S(2)}) collective-permute-start(bf16[512,256]{1,0:T(8,128)(2,1)} %get-tuple-element.20), channel_id=1, source_target_pairs={{0,8},{4,12},{8,0},{12,4},{1,9},{5,13},{9,1},{13,5},{2,10},{6,14},... | collective-permute-start | bytes 786440 | tf_op jit(solution)/shard_map/ppermute | solution.py:159
  120.9 25.3 %collective-permute-start.11 = (bf16[512,1024]{1,0:T(8,128)(2,1)}, bf16[512,1024]{1,0:T(8,128)(2,1)}, u32[]{:S(2)}, u32[]{:S(2)}) collective-permute-start(bf16[512,1024]{1,0:T(8,128)(2,1)} %get-tuple-element.9), channel_id=1, source_target_pairs={{0,2},{2,0},{1,3},{3,1},{4,6},{6,4},{5,7},{7,5},{8,10},{10,8},{9,1... | collective-permute-start | bytes 3145736 | tf_op jit(solution)/shard_map/ppermute | solution.py:176
  124.1 9.8 %collective-permute-start.19 = (bf16[512,256]{1,0:T(8,128)(2,1)}, bf16[512,256]{1,0:T(8,128)(2,1)S(1)}, u32[]{:S(2)}, u32[]{:S(2)}) collective-permute-start(bf16[512,256]{1,0:T(8,128)(2,1)} %collective-permute-done.18), channel_id=1, source_target_pairs={{0,16},{16,0},{1,17},{17,1},{2,18},{18,2},{3,19},{19,3},{4,20},{20... | collective-permute-start | bytes 786440 | tf_op jit(solution)/shard_map/ppermute | solution.py:163
  126.1 25.1 %collective-permute-start.10 = (bf16[512,1024]{1,0:T(8,128)(2,1)}, bf16[512,1024]{1,0:T(8,128)(2,1)S(1)}, u32[]{:S(2)}, u32[]{:S(2)}) collective-permute-start(bf16[512,1024]{1,0:T(8,128)(2,1)} %get-tuple-element.9), channel_id=1, source_target_pairs={{0,1},{1,0},{2,3},{3,2},{4,5},{5,4},{6,7},{7,6},{8,9},{9,8},{10,11... | collective-permute-start | bytes 3145736 | tf_op jit(solution)/shard_map/ppermute | solution.py:178
  131.3 60.6 %collective-permute-start.26 = (bf16[512,512]{1,0:T(8,128)(2,1)}, bf16[512,512]{1,0:T(8,128)(2,1)S(1)}, u32[]{:S(2)}, u32[]{:S(2)}) collective-permute-start(bf16[512,512]{1,0:T(8,128)(2,1)} %pad_maximum_fusion.2), channel_id=1, source_target_pairs={{0,8},{4,12},{8,0},{12,4},{1,9},{5,13},{9,1},{13,5},{2,10},{6,14},... | collective-permute-start | bytes 1572872 | tf_op jit(solution)/shard_map/ppermute | solution.py:159
  134.0 16.4 %collective-permute-start.21 = (bf16[512,256]{1,0:T(8,128)(2,1)}, bf16[512,256]{1,0:T(8,128)(2,1)S(1)}, u32[]{:S(2)}, u32[]{:S(2)}) collective-permute-start(bf16[512,256]{1,0:T(8,128)(2,1)} %collective-permute-done.20), channel_id=1, source_target_pairs={{0,16},{16,0},{1,17},{17,1},{2,18},{18,2},{3,19},{19,3},{4,20},{20... | collective-permute-start | bytes 786440 | tf_op jit(solution)/shard_map/ppermute | solution.py:163
  146.2 43.0 %collective-permute-start.12 = (bf16[512,1024]{1,0:T(8,128)(2,1)}, bf16[512,1024]{1,0:T(8,128)(2,1)S(1)}, u32[]{:S(2)}, u32[]{:S(2)}) collective-permute-start(bf16[512,1024]{1,0:T(8,128)(2,1)} %collective-permute-done.11), channel_id=1, source_target_pairs={{0,1},{1,0},{2,3},{3,2},{4,5},{5,4},{6,7},{7,6},{8,9},{9,8},{10,11... | collective-permute-start | bytes 3145736 | tf_op jit(solution)/shard_map/ppermute | solution.py:178
  149.1 53.2 %collective-permute-start.14 = (bf16[512,1024]{1,0:T(8,128)(2,1)S(1)}, bf16[512,1024]{1,0:T(8,128)(2,1)S(1)}, u32[]{:S(2)}, u32[]{:S(2)}) collective-permute-start(bf16[512,1024]{1,0:T(8,128)(2,1)S(1)} %collective-permute-done.9), channel_id=1, source_target_pairs={{4,0},{5,1},{6,2},{7,3},{20,16},{21,17},{22,18},{23,19}} | collective-permute-start | bytes 3145736 | tf_op jit(solution)/shard_map/ppermute | solution.py:120
  150.4 52.4 %collective-permute-start.13 = (bf16[512,1024]{1,0:T(8,128)(2,1)}, bf16[512,1024]{1,0:T(8,128)(2,1)S(1)}, u32[]{:S(2)}, u32[]{:S(2)}) collective-permute-start(bf16[512,1024]{1,0:T(8,128)(2,1)} %copy-done), channel_id=1, source_target_pairs={{8,12},{9,13},{10,14},{11,15},{24,28},{25,29},{26,30},{27,31}} | collective-permute-start | bytes 3145736 | tf_op jit(solution)/shard_map/ppermute | solution.py:117
  151.2 35.8 %collective-permute-start.22 = (bf16[512,256]{1,0:T(8,128)(2,1)}, bf16[512,256]{1,0:T(8,128)(2,1)S(1)}, u32[]{:S(2)}, u32[]{:S(2)}) collective-permute-start(bf16[512,256]{1,0:T(8,128)(2,1)} %get-tuple-element.18), channel_id=1, source_target_pairs={{0,12},{4,0},{8,4},{12,8},{1,13},{5,1},{9,5},{13,9},{2,14},{6,2},{... | collective-permute-start | bytes 786440 | tf_op jit(solution)/shard_map/ppermute | solution.py:159
  186.9 13.8 %collective-permute-start.28 = (bf16[512,512]{1,0:T(8,128)(2,1)S(1)}, bf16[512,512]{1,0:T(8,128)(2,1)S(1)}, u32[]{:S(2)}, u32[]{:S(2)}) collective-permute-start(bf16[512,512]{1,0:T(8,128)(2,1)S(1)} %copy-done.8), channel_id=1, source_target_pairs={{0,12},{4,0},{8,4},{12,8},{1,13},{5,1},{9,5},{13,9},{2,14},{6,2},{... | collective-permute-start | bytes 1572872 | tf_op jit(solution)/shard_map/ppermute | solution.py:159
  189.2 17.1 %collective-permute-start.23 = (bf16[512,256]{1,0:T(8,128)(2,1)S(1)}, bf16[512,256]{1,0:T(8,128)(2,1)S(1)}, u32[]{:S(2)}, u32[]{:S(2)}) collective-permute-start(bf16[512,256]{1,0:T(8,128)(2,1)S(1)} %collective-permute-done.22), channel_id=1, source_target_pairs={{0,16},{16,0},{1,17},{17,1},{2,18},{18,2},{3,19},{19,3},{4,20},{20... | collective-permute-start | bytes 786440 | tf_op jit(solution)/shard_map/ppermute | solution.py:163
  191.9 17.7 %collective-permute-start.25 = (bf16[512,512]{1,0:T(8,128)(2,1)}, bf16[512,512]{1,0:T(8,128)(2,1)S(1)}, u32[]{:S(2)}, u32[]{:S(2)}) collective-permute-start(bf16[512,512]{1,0:T(8,128)(2,1)} %collective-permute-done.24), channel_id=1, source_target_pairs={{0,16},{16,0},{1,17},{17,1},{2,18},{18,2},{3,19},{19,3},{4,20},{20... | collective-permute-start | bytes 1572872 | tf_op jit(solution)/shard_map/ppermute | solution.py:163
  200.7 20.1 %collective-permute-start.27 = (bf16[512,512]{1,0:T(8,128)(2,1)S(1)}, bf16[512,512]{1,0:T(8,128)(2,1)S(1)}, u32[]{:S(2)}, u32[]{:S(2)}) collective-permute-start(bf16[512,512]{1,0:T(8,128)(2,1)S(1)} %collective-permute-done.26), channel_id=1, source_target_pairs={{0,16},{16,0},{1,17},{17,1},{2,18},{18,2},{3,19},{19,3},{4,20},{20... | collective-permute-start | bytes 1572872 | tf_op jit(solution)/shard_map/ppermute | solution.py:163
  202.3 28.8 %collective-permute-start.29 = (bf16[512,512]{1,0:T(8,128)(2,1)S(1)}, bf16[512,512]{1,0:T(8,128)(2,1)S(1)}, u32[]{:S(2)}, u32[]{:S(2)}) collective-permute-start(bf16[512,512]{1,0:T(8,128)(2,1)S(1)} %collective-permute-done.28), channel_id=1, source_target_pairs={{0,16},{16,0},{1,17},{17,1},{2,18},{18,2},{3,19},{19,3},{4,20},{20... | collective-permute-start | bytes 1572872 | tf_op jit(solution)/shard_map/ppermute | solution.py:163
  204.7 23.5 %collective-permute-start.16 = (bf16[512,1024]{1,0:T(8,128)(2,1)S(1)}, bf16[512,1024]{1,0:T(8,128)(2,1)S(1)}, u32[]{:S(2)}, u32[]{:S(2)}) collective-permute-start(bf16[512,1024]{1,0:T(8,128)(2,1)S(1)} %get-tuple-element.7), channel_id=1, source_target_pairs={{0,2},{2,0},{1,3},{3,1},{4,6},{6,4},{5,7},{7,5},{8,10},{10,8},{9,1... | collective-permute-start | bytes 3145736 | tf_op jit(solution)/shard_map/ppermute | solution.py:176
  206.3 25.6 %collective-permute-start.15 = (bf16[512,1024]{1,0:T(8,128)(2,1)S(1)}, bf16[512,1024]{1,0:T(8,128)(2,1)S(1)}, u32[]{:S(2)}, u32[]{:S(2)}) collective-permute-start(bf16[512,1024]{1,0:T(8,128)(2,1)S(1)} %get-tuple-element.7), channel_id=1, source_target_pairs={{0,1},{1,0},{2,3},{3,2},{4,5},{5,4},{6,7},{7,6},{8,9},{9,8},{10,11... | collective-permute-start | bytes 3145736 | tf_op jit(solution)/shard_map/ppermute | solution.py:178
  265.3 20.6 %collective-permute-start.30 = (bf16[512,256]{1,0:T(8,128)(2,1)S(1)}, bf16[512,256]{1,0:T(8,128)(2,1)S(1)}, u32[]{:S(2)}, u32[]{:S(2)}) collective-permute-start(bf16[512,256]{1,0:T(8,128)(2,1)S(1)} %gate.4), channel_id=1, source_target_pairs={{0,8},{4,12},{8,0},{12,4},{1,9},{5,13},{9,1},{13,5},{2,10},{6,14},... | collective-permute-start | bytes 786440 | tf_op jit(solution)/shard_map/ppermute | solution.py:346
  269.5 16.5 %collective-permute-start.31 = (bf16[512,256]{1,0:T(8,128)(2,1)S(1)}, bf16[512,256]{1,0:T(8,128)(2,1)S(1)}, u32[]{:S(2)}, u32[]{:S(2)}) collective-permute-start(bf16[512,256]{1,0:T(8,128)(2,1)S(1)} %gate.5), channel_id=1, source_target_pairs={{0,4},{4,8},{8,12},{12,0},{1,5},{5,9},{9,13},{13,1},{2,6},{6,10},{... | collective-permute-start | bytes 786440 | tf_op jit(solution)/shard_map/ppermute | solution.py:346
  277.9 12.6 %collective-permute-start.32 = (bf16[512,256]{1,0:T(8,128)(2,1)S(1)}, bf16[512,256]{1,0:T(8,128)(2,1)S(1)}, u32[]{:S(2)}, u32[]{:S(2)}) collective-permute-start(bf16[512,256]{1,0:T(8,128)(2,1)S(1)} %gate.6), channel_id=1, source_target_pairs={{0,12},{4,0},{8,4},{12,8},{1,13},{5,1},{9,5},{13,9},{2,14},{6,2},{... | collective-permute-start | bytes 786440 | tf_op jit(solution)/shard_map/ppermute | solution.py:346
  (13 other events, 295.8 us)

commit v2 on v1

--- a/solution.py
+++ b/solution.py
@@ -110,37 +110,6 @@
     return [(i, (i + step) % size) for i in range(size)]
 
 
-def gather_line(own, axis, size):
-    place = lax.axis_index(axis)
-    upward, downward = {0: own}, {0: own}
-    for step in range(1, size):
-        upward[step] = lax.ppermute(
-            upward[step - 1], axis, [(i, i + 1) for i in range(step - 1, size - 1)]
-        )
-        downward[step] = lax.ppermute(
-            downward[step - 1], axis, [(i + 1, i) for i in range(size - step)]
-        )
-    arrivals = []
-    for i in range(size):
-        order = []
-        for step in range(1, size):
-            if i - step >= 0:
-                order.append(("up", step, i - step))
-            if i + step < size:
-                order.append(("down", step, i + step))
-        arrivals.append(order)
-    shards = [(own, place)]
-    for j in range(size - 1):
-        value, owner = None, jnp.int32(0)
-        for i in range(size):
-            way, step, origin = arrivals[i][j]
-            candidate = upward[step] if way == "up" else downward[step]
-            value = candidate if value is None else jnp.where(place == i, candidate, value)
-            owner = jnp.where(place == i, origin, owner)
-        shards.append((value, owner))
-    return shards
-
-
 def exchange_weights(weights, seq, parts):
     place, part = lax.axis_index("seq"), lax.axis_index("parts")
     depth = weights[0].shape[0]
@@ -168,17 +137,8 @@
 
 
 def gather_tokens(tokens, seq, chan, rep):
-    x_place, core = lax.axis_index("chan"), lax.axis_index("rep")
-    rows, width = tokens.shape
-    whole = jnp.zeros((seq, chan * rep, rows, width), tokens.dtype)
-    for value, owner in gather_line(tokens, "seq", seq):
-        for dx in range(chan):
-            over_x = lax.ppermute(value, "chan", ring(chan, dx)) if dx else value
-            for dr in range(rep):
-                chunk = lax.ppermute(over_x, "rep", ring(rep, dr)) if dr else over_x
-                feature = ((x_place - dx) % chan) * rep + (core - dr) % rep
-                whole = lax.dynamic_update_slice(whole, chunk[None, None], (owner, feature, 0, 0))
-    return whole
+    whole = lax.all_gather(tokens, ("seq", "chan", "rep"), axis=0)
+    return whole.reshape(seq, chan * rep, *tokens.shape)
 
 
 def mode_kernel(x_hbm, w_hbm, modes_ref, conv_ref, state_ref, x_buf, w_buf, prod, out, ends, x_sem, w_sem):

time: 300 us -> 265 us (0.88)
  starting transfers between devices: 41.4 us -> 21 us
  local copies, waits for them, and re-layouts: 52.2 us -> 34.6 us
  between operations: 1.15 us -> 14.4 us
  Pallas kernels: 40.5 us -> 31.7 us
  other arithmetic: 9.82 us -> 2.69 us
  waiting for transfers between devices: 154 us -> 160 us
    ppermute x18 -> x0, waiting for transfers between devices: 82.5 us -> none  [the longest x4 55.8 us: gather_tokens(): over_x = lax.ppermute(value, 'chan', ring(chan, dx)) if dx else value]
    ppermute x6, waiting for transfers between devices: 47.2 us -> 87.7 us  [exchange_weights(): piece = lax.ppermute(piece, 'seq', ring(seq, step))]
    all_gather x0 -> x1, waiting for transfers between devices: none -> 24.5 us  [gather_tokens(): whole = lax.all_gather(tokens, ('seq', 'chan', 'rep'), axis=0)]
    dynamic_update_slice x13 -> x0, local copies, waits for them, and re-layouts: 19.9 us -> none  [gather_tokens(): lax.dynamic_update_slice(whole, chunk[None, None], (owner, feature, 0, 0))]
    ppermute x18 -> x0, starting transfers between devices: 18.7 us -> none  [the longest x4 7.72 us: gather_tokens(): over_x = lax.ppermute(value, 'chan', ring(chan, dx)) if dx else value]
    ppermute x6, waiting for transfers between devices: 14.9 us -> 32.3 us  [exchange_weights(): other = lax.ppermute(piece, 'parts', ring(parts, turn))]
    pallas_call x4, Pallas kernels: 13.8 us -> 5.01 us  [gate(): pl.pallas_call(gate_kernel, out_shape=jax.ShapeDtypeStruct((rows, channel...]
    dynamic_update_slice x3 -> x0, other arithmetic: 7.14 us -> none  [gather_tokens(): lax.dynamic_update_slice(whole, chunk[None, None], (owner, feature, 0, 0))]
  transfers between devices with their start and end apart: 33 -> 16, of which waited for: 15 -> 11; matrix products, arithmetic and copies ran while one was open for 16% -> 9% of each run, Pallas kernels for 3% -> 1%
where the time goes in v2:
time: 265 us
  waiting for transfers between devices  160 us (60%)
  local copies, waits for them, and re-layouts  34.6 us (13%)
  Pallas kernels  31.7 us (12%)
  starting transfers between devices  21 us (8%)
  between operations  14.4 us (5%)
  other arithmetic  2.69 us (1%)
    ppermute x6, waiting for transfers between devices, exchange_weights(): piece = lax.ppermute(piece, 'seq', ring(seq, step))  87.7 us
    ppermute x6, waiting for transfers between devices, exchange_weights(): other = lax.ppermute(piece, 'parts', ring(parts, turn))  32.3 us
    pallas_call x1, Pallas kernels, key_value_modes(): pl.pallas_call(mode_kernel, out_shape=(jax.ShapeDtypeStruct((length, chan...  26.7 us
    all_gather x1, waiting for transfers between devices, gather_tokens(): whole = lax.all_gather(tokens, ('seq', 'chan', 'rep'), axis=0)  24.5 us
    ppermute x3, waiting for transfers between devices, by_channels(): piece = lax.ppermute(piece, 'seq', ring(seq, step))  15.2 us
    ppermute x6, starting transfers between devices, exchange_weights(): piece = lax.ppermute(piece, 'seq', ring(seq, step))  7.89 us
    ppermute x6, starting transfers between devices, exchange_weights(): other = lax.ppermute(piece, 'parts', ring(parts, turn))  7.62 us
    dynamic_update_slice x5, local copies, waits for them, and re-layouts, by_channels(): lax.dynamic_update_slice(gated, piece[None], ((place - step) % seq, 0, 0))  7.58 us
  transfers between devices with their start and end apart: 16, of which 11 were waited for; matrix products, arithmetic and copies ran while one was open for 9% of the time, Pallas kernels for 1%

profile of v2, /device:TPU:0, one launch (start us, length us, event | category | flops | bytes accessed | tf_op | source)
XLA Modules:
  0.0 264.9 jit_solution(13687525065563055266)
XLA Ops:
  7.9 1.5 fusion
  10.3 3.0 %collective-permute-start.6 = (bf16[512,512]{1,0:T(8,128)(2,1)}, bf16[512,512]{1,0:T(8,128)(2,1)}, u32[]{:S(2)}, u32[]{:S(2)}) collective-permute-start(bf16[512,512]{1,0:T(8,128)(2,1)} %pad_maximum_fusion.1), channel_id=1, source_target_pairs={{0,4},{4,8},{8,12},{12,0},{1,5},{5,9},{9,13},{13,1},{2,6},{6,10},{... | collective-permute-start | bytes 1572872 | tf_op jit(solution)/shard_map/ppermute | solution.py:128
  14.1 2.6 collective-permute-start.8
  17.6 1.3 collective-permute-start.10
  18.9 2.0 fusion.2
  21.8 1.4 constant_dynamic-slice_fusion
  24.6 2.3 broadcast_in_dim.65
  27.9 57.4 %collective-permute-done = bf16[512,256]{1,0:T(8,128)(2,1)} collective-permute-done((bf16[512,256]{1,0:T(8,128)(2,1)S(1)}, bf16[512,256]{1,0:T(8,128)(2,1)}, u32[]{:S(2)}, u32[]{:S(2)}) %collective-permute-start) | collective-permute-done | bytes 262176 | tf_op jit(solution)/shard_map/ppermute | solution.py:128
  85.4 26.5 %collective-permute-done.2 = bf16[512,256]{1,0:T(8,128)(2,1)S(1)} collective-permute-done((bf16[512,256]{1,0:T(8,128)(2,1)S(1)}, bf16[512,256]{1,0:T(8,128)(2,1)S(1)}, u32[]{:S(2)}, u32[]{:S(2)}) %collective-permute-start.2) | collective-permute-done | bytes 262176 | tf_op jit(solution)/shard_map/ppermute | solution.py:128
  111.9 1.5 collective-permute-start.1
  114.6 3.8 %collective-permute-done.4 = bf16[512,256]{1,0:T(8,128)(2,1)} collective-permute-done((bf16[512,256]{1,0:T(8,128)(2,1)}, bf16[512,256]{1,0:T(8,128)(2,1)}, u32[]{:S(2)}, u32[]{:S(2)}) %collective-permute-start.4) | collective-permute-done | bytes 262176 | tf_op jit(solution)/shard_map/ppermute | solution.py:128
  118.4 2.1 collective-permute-start.3
  120.5 2.0 collective-permute-start.7
  122.6 2.0 collective-permute-start.11
  125.6 2.1 collective-permute-done.3
  128.7 1.9 bitcast_dynamic-update-slice_fusion.5
  130.6 2.7 %collective-permute-done.5 = bf16[512,256]{1,0:T(8,128)(2,1)S(1)} collective-permute-done((bf16[512,256]{1,0:T(8,128)(2,1)}, bf16[512,256]{1,0:T(8,128)(2,1)S(1)}, u32[]{:S(2)}, u32[]{:S(2)}) %collective-permute-start.5) | collective-permute-done | bytes 262176 | tf_op jit(solution)/shard_map/ppermute | solution.py:132
  133.3 11.2 %collective-permute-done.7 = bf16[512,512]{1,0:T(8,128)(2,1)S(1)} collective-permute-done((bf16[512,512]{1,0:T(8,128)(2,1)}, bf16[512,512]{1,0:T(8,128)(2,1)S(1)}, u32[]{:S(2)}, u32[]{:S(2)}) %collective-permute-start.7) | collective-permute-done | bytes 524320 | tf_op jit(solution)/shard_map/ppermute | solution.py:132
  145.4 1.9 bitcast_dynamic-update-slice_fusion.3
  147.2 8.5 %collective-permute-done.9 = bf16[512,512]{1,0:T(8,128)(2,1)S(1)} collective-permute-done((bf16[512,512]{1,0:T(8,128)(2,1)}, bf16[512,512]{1,0:T(8,128)(2,1)S(1)}, u32[]{:S(2)}, u32[]{:S(2)}) %collective-permute-start.9) | collective-permute-done | bytes 524320 | tf_op jit(solution)/shard_map/ppermute | solution.py:132
  157.4 7.7 %collective-permute-done.11 = bf16[512,512]{1,0:T(8,128)(2,1)S(1)} collective-permute-done((bf16[512,512]{1,0:T(8,128)(2,1)S(1)}, bf16[512,512]{1,0:T(8,128)(2,1)S(1)}, u32[]{:S(2)}, u32[]{:S(2)}) %collective-permute-start.11) | collective-permute-done | bytes 524320 | tf_op jit(solution)/shard_map/ppermute | solution.py:132
  166.0 24.5 %all-gather.3.cloned.1.call-done = bf16[8192,1024]{1,0:T(8,128)(2,1)} async-done(((bf16[512,1024]{1,0:T(8,128)(2,1)}), bf16[8192,1024]{1,0:T(8,128)(2,1)}) %all-gather.3.cloned.1.call-update) | async-done | bytes 16777232 | tf_op jit(solution)/shard_map/all_gather | solution.py:140
  190.5 26.7 %key_value_modes.1 = (bf16[2048,256]{1,0:T(8,128)(2,1)S(1)}, f32[16,256]{1,0:T(8,128)}) custom-call(bf16[4,4,512,1024]{3,2,1,0:T(8,128)(2,1)} %bitcast.55, bf16[4,1024,512]{2,1,0:T(8,128)(2,1)} %bitcast.17.w_hbm, f32[5,16,256]{2,1,0:T(8,128)S(1)} %bitcast.65), custom_call_target="tpu_custom_call" | custom-call | flops 8589934592 | bytes 20971520 | tf_op jit(solution)/shard_map/key_value_modes/pallas_call | solution.py:226
  217.2 5.8 %copy-done = bf16[8192,1024]{1,0:T(8,128)(2,1)S(1)} copy-done((bf16[8192,1024]{1,0:T(8,128)(2,1)S(1)}, bf16[8192,1024]{1,0:T(8,128)(2,1)}, u32[]{:S(2)}) %copy-start) | copy-done | bytes 16777240
  224.2 1.6 collective-permute-start.12
  225.8 1.3 gate.5
  227.6 1.3 gate.7
  228.8 1.3 gate.6
  230.5 3.4 %collective-permute-start.14 = (bf16[512,256]{1,0:T(8,128)(2,1)S(1)}, bf16[512,256]{1,0:T(8,128)(2,1)S(1)}, u32[]{:S(2)}, u32[]{:S(2)}) collective-permute-start(bf16[512,256]{1,0:T(8,128)(2,1)S(1)} %gate.6), channel_id=1, source_target_pairs={{0,12},{4,0},{8,4},{12,8},{1,13},{5,1},{9,5},{13,9},{2,14},{6,2},{... | collective-permute-start | bytes 786440 | tf_op jit(solution)/shard_map/ppermute | solution.py:306
  233.9 10.2 %collective-permute-done.12 = bf16[512,256]{1,0:T(8,128)(2,1)S(1)} collective-permute-done((bf16[512,256]{1,0:T(8,128)(2,1)S(1)}, bf16[512,256]{1,0:T(8,128)(2,1)S(1)}, u32[]{:S(2)}, u32[]{:S(2)}) %collective-permute-start.12) | collective-permute-done | bytes 262176 | tf_op jit(solution)/shard_map/ppermute | solution.py:306
  244.2 5.0 %collective-permute-done.14 = bf16[512,256]{1,0:T(8,128)(2,1)S(1)} collective-permute-done((bf16[512,256]{1,0:T(8,128)(2,1)S(1)}, bf16[512,256]{1,0:T(8,128)(2,1)S(1)}, u32[]{:S(2)}, u32[]{:S(2)}) %collective-permute-start.14) | collective-permute-done | bytes 262176 | tf_op jit(solution)/shard_map/ppermute | solution.py:306
  250.1 6.7 %dynamic_update_slice.71 = bf16[4,512,256]{2,0,1:T(4,128)(2,1)S(1)} dynamic-update-slice(bf16[4,512,256]{2,0,1:T(4,128)(2,1)S(1)} %copy.9, bf16[1,512,256]{2,0,1:T(2,128)(2,1)S(1)} %copy.10, s32[]{:T(128)S(6)} %select_n.165, s32[]{:T(128)} %constant.104.clone.1, s32[]{:T(128)} %constant.104.clone.1) | dynamic-update-slice | bytes 524292 | tf_op jit(solution)/shard_map/dynamic_update_slice | solution.py:307
  (51 shorter events, 17.4 us)
Async XLA Ops:
  7.2 183.3 %all-gather.3.cloned.1.call-start = ((), (), s32[]{:S(2)}) async-start(), calls=%async_computation | async-start | bytes 17825792 | tf_op jit(solution)/shard_map/all_gather | solution.py:140
  10.3 110.2 %collective-permute-start.6 = (bf16[512,512]{1,0:T(8,128)(2,1)}, bf16[512,512]{1,0:T(8,128)(2,1)}, u32[]{:S(2)}, u32[]{:S(2)}) collective-permute-start(bf16[512,512]{1,0:T(8,128)(2,1)} %pad_maximum_fusion.1), channel_id=1, source_target_pairs={{0,4},{4,8},{8,12},{12,0},{1,5},{5,9},{9,13},{13,1},{2,6},{6,10},{... | collective-permute-start | bytes 1572872 | tf_op jit(solution)/shard_map/ppermute | solution.py:128
  14.1 106.4 %collective-permute-start.8 = (bf16[512,512]{1,0:T(8,128)(2,1)}, bf16[512,512]{1,0:T(8,128)(2,1)}, u32[]{:S(2)}, u32[]{:S(2)}) collective-permute-start(bf16[512,512]{1,0:T(8,128)(2,1)} %pad_maximum_fusion.2), channel_id=1, source_target_pairs={{0,8},{4,12},{8,0},{12,4},{1,9},{5,13},{9,1},{13,5},{2,10},{6,14},... | collective-permute-start | bytes 1572872 | tf_op jit(solution)/shard_map/ppermute | solution.py:128
  17.6 104.9 %collective-permute-start.10 = (bf16[512,512]{1,0:T(8,128)(2,1)}, bf16[512,512]{1,0:T(8,128)(2,1)S(1)}, u32[]{:S(2)}, u32[]{:S(2)}) collective-permute-start(bf16[512,512]{1,0:T(8,128)(2,1)} %pad_maximum_fusion.3), channel_id=1, source_target_pairs={{0,12},{4,0},{8,4},{12,8},{1,13},{5,1},{9,5},{13,9},{2,14},{6,2},{... | collective-permute-start | bytes 1572872 | tf_op jit(solution)/shard_map/ppermute | solution.py:128
  20.9 64.5 %collective-permute-start = (bf16[512,256]{1,0:T(8,128)(2,1)S(1)}, bf16[512,256]{1,0:T(8,128)(2,1)}, u32[]{:S(2)}, u32[]{:S(2)}) collective-permute-start(bf16[512,256]{1,0:T(8,128)(2,1)S(1)} %get-tuple-element.13), channel_id=1, source_target_pairs={{0,4},{4,8},{8,12},{12,0},{1,5},{5,9},{9,13},{13,1},{2,6},{6,10},{... | collective-permute-start | bytes 786440 | tf_op jit(solution)/shard_map/ppermute | solution.py:128
  21.5 90.4 %collective-permute-start.2 = (bf16[512,256]{1,0:T(8,128)(2,1)S(1)}, bf16[512,256]{1,0:T(8,128)(2,1)S(1)}, u32[]{:S(2)}, u32[]{:S(2)}) collective-permute-start(bf16[512,256]{1,0:T(8,128)(2,1)S(1)} %get-tuple-element.14), channel_id=1, source_target_pairs={{0,8},{4,12},{8,0},{12,4},{1,9},{5,13},{9,1},{13,5},{2,10},{6,14},... | collective-permute-start | bytes 786440 | tf_op jit(solution)/shard_map/ppermute | solution.py:128
  21.8 1.5 copy-start.1
  21.8 1.6 copy-start.2
  21.8 1.6 copy-start.3
  85.4 33.0 %collective-permute-start.4 = (bf16[512,256]{1,0:T(8,128)(2,1)}, bf16[512,256]{1,0:T(8,128)(2,1)}, u32[]{:S(2)}, u32[]{:S(2)}) collective-permute-start(bf16[512,256]{1,0:T(8,128)(2,1)} %get-tuple-element.12), channel_id=1, source_target_pairs={{0,12},{4,0},{8,4},{12,8},{1,13},{5,1},{9,5},{13,9},{2,14},{6,2},{... | collective-permute-start | bytes 786440 | tf_op jit(solution)/shard_map/ppermute | solution.py:128
  111.9 10.7 %collective-permute-start.1 = (bf16[512,256]{1,0:T(8,128)(2,1)}, bf16[512,256]{1,0:T(8,128)(2,1)}, u32[]{:S(2)}, u32[]{:S(2)}) collective-permute-start(bf16[512,256]{1,0:T(8,128)(2,1)} %collective-permute-done), channel_id=1, source_target_pairs={{0,16},{16,0},{1,17},{17,1},{2,18},{18,2},{3,19},{19,3},{4,20},{20... | collective-permute-start | bytes 786440 | tf_op jit(solution)/shard_map/ppermute | solution.py:132
  118.4 9.3 %collective-permute-start.3 = (bf16[512,256]{1,0:T(8,128)(2,1)S(1)}, bf16[512,256]{1,0:T(8,128)(2,1)S(1)}, u32[]{:S(2)}, u32[]{:S(2)}) collective-permute-start(bf16[512,256]{1,0:T(8,128)(2,1)S(1)} %collective-permute-done.2), channel_id=1, source_target_pairs={{0,16},{16,0},{1,17},{17,1},{2,18},{18,2},{3,19},{19,3},{4,20},{20... | collective-permute-start | bytes 786440 | tf_op jit(solution)/shard_map/ppermute | solution.py:132
  120.5 12.8 %collective-permute-start.5 = (bf16[512,256]{1,0:T(8,128)(2,1)}, bf16[512,256]{1,0:T(8,128)(2,1)S(1)}, u32[]{:S(2)}, u32[]{:S(2)}) collective-permute-start(bf16[512,256]{1,0:T(8,128)(2,1)} %collective-permute-done.4), channel_id=1, source_target_pairs={{0,16},{16,0},{1,17},{17,1},{2,18},{18,2},{3,19},{19,3},{4,20},{20... | collective-permute-start | bytes 786440 | tf_op jit(solution)/shard_map/ppermute | solution.py:132
  120.5 24.0 %collective-permute-start.7 = (bf16[512,512]{1,0:T(8,128)(2,1)}, bf16[512,512]{1,0:T(8,128)(2,1)S(1)}, u32[]{:S(2)}, u32[]{:S(2)}) collective-permute-start(bf16[512,512]{1,0:T(8,128)(2,1)} %collective-permute-done.6), channel_id=1, source_target_pairs={{0,16},{16,0},{1,17},{17,1},{2,18},{18,2},{3,19},{19,3},{4,20},{20... | collective-permute-start | bytes 1572872 | tf_op jit(solution)/shard_map/ppermute | solution.py:132
  122.5 33.3 %collective-permute-start.9 = (bf16[512,512]{1,0:T(8,128)(2,1)}, bf16[512,512]{1,0:T(8,128)(2,1)S(1)}, u32[]{:S(2)}, u32[]{:S(2)}) collective-permute-start(bf16[512,512]{1,0:T(8,128)(2,1)} %collective-permute-done.8), channel_id=1, source_target_pairs={{0,16},{16,0},{1,17},{17,1},{2,18},{18,2},{3,19},{19,3},{4,20},{20... | collective-permute-start | bytes 1572872 | tf_op jit(solution)/shard_map/ppermute | solution.py:132
  122.6 42.6 %collective-permute-start.11 = (bf16[512,512]{1,0:T(8,128)(2,1)S(1)}, bf16[512,512]{1,0:T(8,128)(2,1)S(1)}, u32[]{:S(2)}, u32[]{:S(2)}) collective-permute-start(bf16[512,512]{1,0:T(8,128)(2,1)S(1)} %collective-permute-done.10), channel_id=1, source_target_pairs={{0,16},{16,0},{1,17},{17,1},{2,18},{18,2},{3,19},{19,3},{4,20},{20... | collective-permute-start | bytes 1572872 | tf_op jit(solution)/shard_map/ppermute | solution.py:132
  217.2 5.8 %copy-start = (bf16[8192,1024]{1,0:T(8,128)(2,1)S(1)}, bf16[8192,1024]{1,0:T(8,128)(2,1)}, u32[]{:S(2)}) copy-start(bf16[8192,1024]{1,0:T(8,128)(2,1)} %all-gather.3.cloned.1.call-done) | copy-start | bytes 50331652
  224.2 19.8 %collective-permute-start.12 = (bf16[512,256]{1,0:T(8,128)(2,1)S(1)}, bf16[512,256]{1,0:T(8,128)(2,1)S(1)}, u32[]{:S(2)}, u32[]{:S(2)}) collective-permute-start(bf16[512,256]{1,0:T(8,128)(2,1)S(1)} %gate.4), channel_id=1, source_target_pairs={{0,8},{4,12},{8,0},{12,4},{1,9},{5,13},{9,1},{13,5},{2,10},{6,14},... | collective-permute-start | bytes 786440 | tf_op jit(solution)/shard_map/ppermute | solution.py:306
  227.1 17.1 %collective-permute-start.13 = (bf16[512,256]{1,0:T(8,128)(2,1)S(1)}, bf16[512,256]{1,0:T(8,128)(2,1)S(1)}, u32[]{:S(2)}, u32[]{:S(2)}) collective-permute-start(bf16[512,256]{1,0:T(8,128)(2,1)S(1)} %gate.5), channel_id=1, source_target_pairs={{0,4},{4,8},{8,12},{12,0},{1,5},{5,9},{9,13},{13,1},{2,6},{6,10},{... | collective-permute-start | bytes 786440 | tf_op jit(solution)/shard_map/ppermute | solution.py:306
  230.5 18.8 %collective-permute-start.14 = (bf16[512,256]{1,0:T(8,128)(2,1)S(1)}, bf16[512,256]{1,0:T(8,128)(2,1)S(1)}, u32[]{:S(2)}, u32[]{:S(2)}) collective-permute-start(bf16[512,256]{1,0:T(8,128)(2,1)S(1)} %gate.6), channel_id=1, source_target_pairs={{0,12},{4,0},{8,4},{12,8},{1,13},{5,1},{9,5},{13,9},{2,14},{6,2},{... | collective-permute-start | bytes 786440 | tf_op jit(solution)/shard_map/ppermute | solution.py:306
Sparse Core Ops, SparseCore 0:
  10.2 180.2 all-gather.2

commit v3 on v0

--- a/solution.py
+++ b/solution.py
@@ -1,9 +1,19 @@
+import functools
+
 import jax
 import jax.numpy as jnp
 from jax import lax
+from jax.experimental import pallas as pl
+from jax.experimental.pallas import tpu as pltpu
 from jax.sharding import PartitionSpec as P
 
 BLOCK = 128
+SUBLANES, LANES = 8, 128
+TILE = 256
+UNROLL = 4
+GATHER_BYTES = 24 << 20
+KERNEL_BYTES = 56 << 20
+FINISH_COST = 4
 
 
 HIGHEST_PRECISION = lax.Precision.HIGHEST
@@ -100,6 +110,287 @@
     return (gated_rows.T, new_state)
 
 
+def ring(size, step):
+    return [(i, (i + step) % size) for i in range(size)]
+
+
+def mirror(size, step):
+    return [(i, i ^ step) for i in range(size)]
+
+
+def after(x, *earlier):
+    for other in earlier:
+        if other is not None:
+            probe = lax.slice(other, [n - 1 for n in other.shape], other.shape).reshape(())
+            x = jnp.where(probe != probe, jnp.zeros((), x.dtype), x)
+    return x
+
+
+def arrival_order(size):
+    orders = []
+    for i in range(size):
+        order = []
+        for step in range(1, size):
+            if i - step >= 0:
+                order.append((0, step, i - step))
+            if i + step < size:
+                order.append((1, step, i + step))
+        orders.append(order)
+    return orders
+
+
+def exchange_weights(weight, sizes):
+    seq, parts = sizes["seq"], sizes["parts"]
+    place, part = lax.axis_index("seq"), lax.axis_index("parts")
+    depth, width = weight.shape[0], weight.shape[1] // seq
+    share = depth // parts
+    mine = lax.dynamic_slice(weight, (part * share, 0), (share, weight.shape[1]))
+    mine = mine.reshape(share, seq, width).transpose(1, 0, 2)
+    mine = lax.all_to_all(mine, "seq", split_axis=0, concat_axis=0, tiled=True)
+    fetched = jnp.concatenate(
+        [lax.dynamic_slice(mine, (place ^ step, 0, 0), (1, share, width)) for step in range(1, seq)]
+    )
+    shares = [mine]
+    for turn in range(1, parts):
+        first = (part - turn) % parts * share
+        own = lax.dynamic_slice(weight, (first, place * width), (share, width))
+        shares.append(jnp.concatenate([own[None], lax.ppermute(fetched, "parts", ring(parts, turn))]))
+    return shares
+
+
+def weight_copies(order_ref, w_hbm, w_buf, w_sem):
+    quarters, share, width = w_hbm[0].shape
+    parts = w_buf.shape[0] // (quarters * share)
+    copies = []
+    for k, ref in enumerate(w_hbm):
+        columns = pl.ds(k // parts * width, width)
+        shift = order_ref[quarters + k % parts] * share
+        for q in range(quarters):
+            at = pl.ds(pl.multiple_of(q * parts * share + shift, share), share)
+            block = order_ref[q] if k % parts == 0 else order_ref[quarters + parts + q]
+            copies.append(pltpu.make_async_copy(ref.at[block], w_buf.at[at, columns], w_sem.at[k, q]))
+    return copies
+
+
+def token_copies(x_hbm, x_buf, x_sem):
+    some, rows, depth = x_hbm[0].shape
+    return [
+        pltpu.make_async_copy(
+            x_hbm[e].at[f], x_buf.at[:, pl.ds((e * some + f) * depth, depth)], x_sem.at[e * some + f]
+        )
+        for e in range(len(x_hbm))
+        for f in range(some)
+    ]
+
+
+def modes_over_time(modes_ref, prod, out, ends, conv_ref, state_ref):
+    groups, length, lane_width = prod.shape
+    modes = modes_ref.shape[1]
+    span = length // SUBLANES
+    zero = jnp.zeros((SUBLANES, LANES), jnp.float32)
+    for g in range(groups):
+        lanes = pl.ds(g * LANES, LANES)
+        signal, result = prod.at[g], out.at[g]
+        decay = [jnp.broadcast_to(modes_ref[0, m : m + 1, lanes], (SUBLANES, LANES)) for m in range(modes)]
+        weight = [jnp.broadcast_to(modes_ref[2, m : m + 1, lanes], (SUBLANES, LANES)) for m in range(modes)]
+
+        def sums(i, states):
+            for u in range(UNROLL):
+                value = signal[pl.ds(i * UNROLL + u, SUBLANES, stride=span), :]
+                states = tuple(a * s + value for a, s in zip(decay, states))
+            return states
+
+        states = lax.fori_loop(0, span // UNROLL, sums, (zero,) * modes)
+        for m in range(modes):
+            ends[m] = states[m]
+        state = modes_ref[3, :, lanes]
+        over_span = modes_ref[1, :, lanes]
+        for b in range(SUBLANES):
+            end = ends[:, b, :]
+            ends[:, b, :] = state
+            state = over_span * state + end
+        state_ref[:, lanes] = state * modes_ref[4, :, lanes]
+
+        def outputs(i, states):
+            for u in range(UNROLL):
+                at = pl.ds(i * UNROLL + u, SUBLANES, stride=span)
+                value = signal[at, :]
+                states = tuple(a * s + value for a, s in zip(decay, states))
+                terms = [w * s for w, s in zip(weight, states)]
+                while len(terms) > 1:
+                    terms = [sum(terms[k : k + 2][1:], terms[k]) for k in range(0, len(terms), 2)]
+                result[at, :] = terms[0]
+            return states
+
+        lax.fori_loop(0, span // UNROLL, outputs, tuple(ends[m] for m in range(modes)))
+        conv_ref[:, lanes] = result[...].astype(jnp.bfloat16)
+
+
+def finish_kernel(n_weights, seq, order_ref, modes_ref, *refs):
+    refs = list(refs)
+
+    def take(count):
+        taken = refs[:count]
+        del refs[:count]
+        return taken
+
+    pair_hbm, query_hbm = take(2 * n_weights), take(n_weights)
+    each = (len(refs) - 11 - seq) // seq
+    x_hbm = [take(each) for _ in range(seq)]
+    outs, (state_ref,) = take(seq), take(1)
+    x_buf, pair_buf, query_buf, prod, out, ends, conv_buf, x_sem, pair_sem, query_sem = take(10)
+    rows = x_buf.shape[1]
+    channels = conv_buf.shape[1]
+    groups = prod.shape[0]
+    first = 2 * pair_sem.shape[1] + n_weights
+    x_copies = [token_copies(x_hbm[i], x_buf.at[i], x_sem.at[i]) for i in range(seq)]
+    pair_copies = weight_copies(order_ref, pair_hbm, pair_buf, pair_sem)
+    query_copies = weight_copies(order_ref, query_hbm, query_buf, query_sem)
+    for copy in pair_copies + x_copies[0] + x_copies[1]:
+        copy.start()
+    for copy in pair_copies:
+        copy.wait()
+    for i in range(seq):
+        for copy in x_copies[i]:
+            copy.wait()
+        for copy in x_copies[i + 2] if i + 2 < seq else query_copies if i + 2 == seq else ():
+            copy.start()
+        acc = jnp.dot(x_buf[i], pair_buf[...], preferred_element_type=jnp.float32)
+        rounded = acc.astype(jnp.bfloat16).astype(jnp.float32)
+        product = (rounded[:, :channels] * rounded[:, channels:]).astype(jnp.bfloat16)
+        to = pl.ds(pl.multiple_of(order_ref[first + i] * rows, rows), rows)
+        for g in range(groups):
+            prod[g, to, :] = product[:, g * LANES : (g + 1) * LANES].astype(jnp.float32)
+    modes_over_time(modes_ref, prod, out, ends, conv_buf, state_ref)
+    for copy in query_copies:
+        copy.wait()
+    for i in range(seq):
+        shard = order_ref[first + i]
+        acc = jnp.dot(x_buf[i], query_buf[...], preferred_element_type=jnp.float32)
+        query = acc.astype(jnp.bfloat16).astype(jnp.float32)
+        conv = conv_buf[pl.ds(pl.multiple_of(shard * rows, rows), rows), :].astype(jnp.float32)
+        gated = (query * conv).astype(jnp.bfloat16)
+        for step in range(seq):
+
+            @pl.when(order_ref[first + seq + i] == step)
+            def _():
+                outs[step][...] = gated
+
+
+def finish(order, xs, pair, query, decay_rate, residue, carried):
+    quarters, share, width = query[0].shape
+    seq = len(xs)
+    rows, depth = xs[0][0].shape[1:]
+    length, modes = seq * rows, decay_rate.shape[1]
+    scale = mode_scale(decay_rate)
+    table = jnp.stack(
+        [
+            jnp.exp(-decay_rate),
+            jnp.exp(-decay_rate * (length // SUBLANES)),
+            residue * scale,
+            carried / scale,
+            scale,
+        ]
+    ).transpose(0, 2, 1)
+    vmem, anywhere = pl.BlockSpec(memory_space=pltpu.VMEM), pl.BlockSpec(memory_space=pl.ANY)
+    arrays = [*pair, *query, *sum(xs, [])]
+    *gated, state = pl.pallas_call(
+        functools.partial(finish_kernel, len(query), seq),
+        out_shape=tuple(jax.ShapeDtypeStruct((rows, width), jnp.bfloat16) for _ in range(seq))
+        + (jax.ShapeDtypeStruct((modes, width), jnp.float32),),
+        in_specs=[pl.BlockSpec(memory_space=pltpu.SMEM), vmem]
+        + [anywhere] * len(arrays),
+        out_specs=(vmem,) * (seq + 1),
+        scratch_shapes=[
+            pltpu.VMEM((seq, rows, quarters * depth), jnp.bfloat16),
+            pltpu.VMEM((quarters * depth, 2 * width), jnp.bfloat16),
+            pltpu.VMEM((quarters * depth, width), jnp.bfloat16),
+            pltpu.VMEM((width // LANES, length, LANES), jnp.float32),
+            pltpu.VMEM((width // LANES, length, LANES), jnp.float32),
+            pltpu.VMEM((modes, SUBLANES, LANES), jnp.float32),
+            pltpu.VMEM((length, width), jnp.bfloat16),
+            pltpu.SemaphoreType.DMA((seq, quarters)),
+            pltpu.SemaphoreType.DMA((len(pair), quarters)),
+            pltpu.SemaphoreType.DMA((len(query), quarters)),
+        ],
+        compiler_params=pltpu.CompilerParams(vmem_limit_bytes=KERNEL_BYTES),
+        cost_estimate=pl.CostEstimate(
+            flops=FINISH_COST * length * quarters * depth * width,
+            bytes_accessed=2 * quarters * depth * (length + 3 * width),
+            transcendentals=0,
+        ),
+        name="finish",
+    )(order, table, *arrays)
+    return gated, state.T
+
+
+def place_columns(pieces, place):
+    seq = len(pieces)
+    rows, width = pieces[0].shape
+
+    def kernel(place_ref, *refs):
+        out_ref = refs[-1]
+        for step in range(seq):
+            origin = place_ref[0] ^ step
+            out_ref[:, pl.ds(pl.multiple_of(origin * width, width), width)] = refs[step][...]
+
+    return pl.pallas_call(
+        kernel,
+        out_shape=jax.ShapeDtypeStruct((rows, seq * width), pieces[0].dtype),
+        in_specs=[pl.BlockSpec(memory_space=pltpu.SMEM)] + [pl.BlockSpec(memory_space=pltpu.VMEM)] * seq,
+        out_specs=pl.BlockSpec(memory_space=pltpu.VMEM),
+        name="place_columns",
+    )(place.reshape(1).astype(jnp.int32), *pieces)
+
+
+def by_channels(sizes, tokens, w_query, w_key, w_value, decay_rate, residue, carried):
+    seq, chan, rep, parts = sizes["seq"], sizes["chan"], sizes["rep"], sizes["parts"]
+    place, x_place, core = lax.axis_index("seq"), lax.axis_index("chan"), lax.axis_index("rep")
+    orders = arrival_order(seq)
+
+    def at_place(choices):
+        value = choices[0]
+        for i in range(1, seq):
+            value = jnp.where(place == i, choices[i], value)
+        return value
+
+    w_keys, w_values, w_queries = [exchange_weights(w, sizes) for w in (w_key, w_value, w_query)]
+    before = {2: w_keys[:1], 3: w_keys[1:] + w_values[:1], 4: w_values[1:]}
+    shares = [(lax.axis_index("parts") - turn) % parts for turn in range(parts)]
+    features = [
+        ((x_place - turn) % chan) * rep + (core - other) % rep for other in range(rep) for turn in range(chan)
+    ]
+    by_feature = jnp.stack([jnp.int32(i) for i in features + shares + [f ^ place for f in features]])
+    arrival, ways, xs, origins, last = tokens, [{0: tokens}, {0: tokens}], [], [place], None
+    for phase in range(1, seq + 1):
+        group = [arrival]
+        for turn in range(1, chan):
+            last = lax.ppermute(after(arrival, last, *before.get(phase, ())), "chan", ring(chan, turn))
+            group.append(last)
+        if phase == seq:
+            group[-1] = after(group[-1], *w_queries[1:])
+        both = jnp.stack(group)
+        xs.append([both] + [lax.ppermute(both, "rep", ring(rep, turn)) for turn in range(1, rep)])
+        if phase == seq:
+            break
+        ups = [(i, i + 1) for i in range(phase - 1, seq - 1)]
+        downs = [(i + 1, i) for i in range(seq - phase)]
+        ways[0][phase] = lax.ppermute(ways[0][phase - 1], "seq", ups)
+        ways[1][phase] = lax.ppermute(ways[1][phase - 1], "seq", downs)
+        chosen = [orders[i][phase - 1] for i in range(seq)]
+        arrival = at_place([ways[way][step] for way, step, origin in chosen])
+        origins.append(at_place([jnp.int32(origin) for way, step, origin in chosen]))
+
+    steps = [place ^ origin for origin in origins]
+    order = jnp.concatenate([by_feature, jnp.stack([jnp.int32(i) for i in origins + steps])])
+
+    gated, new_state = finish(order, xs, w_keys + w_values, w_queries, decay_rate, residue, carried)
+    pieces = [
+        lax.ppermute(gated[step], "seq", mirror(seq, step)) if step else gated[0] for step in range(seq)
+    ]
+    return place_columns(pieces, place), new_state
+
+
 def solution(mesh):
     in_specs = (
         P(("parts", "seq"), ("chan", "rep")),
@@ -111,6 +402,18 @@
         P(("parts", "chan", "rep", "seq"), None),
     )
     out_specs = (P(("parts", "seq"), ("chan", "rep")), P(("parts", "chan", "rep", "seq"), None))
+    sizes = dict(mesh.shape)
+
+    def program(*arrays):
+        tokens = arrays[0]
+        part_bytes = tokens.size * tokens.dtype.itemsize * sizes["seq"] * sizes["chan"] * sizes["rep"]
+        seq = sizes["seq"]
+        fits = part_bytes <= GATHER_BYTES and seq == sizes["chan"] * sizes["rep"]
+        fits = fits and seq >= 4 and seq & (seq - 1) == 0
+        if fits:
+            return by_channels(sizes, *arrays)
+        return per_device(*arrays)
+
     return jax.shard_map(
-        per_device, mesh=mesh, in_specs=in_specs, out_specs=out_specs, check_vma=False
-    )
+        program, mesh=mesh, in_specs=in_specs, out_specs=out_specs, check_vma=False
+    )

time: 893 us -> 253 us (0.28)
  waiting for transfers between devices: 470 us -> 88.9 us
  local copies, waits for them, and re-layouts: 337 us -> 31.6 us
  matrix products: 50.3 us -> 0 us
  starting transfers between devices: 8.72 us -> 54 us
  Pallas kernels: 0 us -> 37.8 us
  other arithmetic: 12 us -> 25.2 us
    all_gather x4 -> x0, waiting for transfers between devices: 468 us -> none  [the longest x1 151 us: per_device(): lax.all_gather(w_query, 'seq', axis=0, tiled=True)]
    pad x6 -> x0, local copies, waits for them, and re-layouts: 158 us -> none  [block_sums(): lax.associative_scan(combine_states, (step_decay, block_ends), axis=1)]
    gather x2 -> x0, local copies, waits for them, and re-layouts: 80 us -> none  [block_convolve(): toeplitz = kernel[:, lag] * causal[None, :, :]]
    unnamed x33 -> x25, local copies, waits for them, and re-layouts: 82.2 us -> 7.42 us
    ppermute x0 -> x20, waiting for transfers between devices: none -> 60.5 us  [the longest x3 29.4 us: by_channels(): ways[1][phase] = lax.ppermute(ways[1][phase - 1], 'seq', downs)]
    dot_general x6 -> x0, matrix products: 50.3 us -> none  [the longest x3 28.5 us: per_device(): lax.dot_general(weight_piece, gathered, (((0,), (1,)), ((), ())), preferr...]
    pallas_call x0 -> x2, Pallas kernels: none -> 37.8 us  [the longest x1 35.5 us: finish(): pl.pallas_call(functools.partial(finish_kernel, len(query), seq), out_sha...]
    ppermute x0 -> x20, starting transfers between devices: none -> 35 us  [the longest x3 11.1 us: by_channels(): lax.ppermute(gated[step], 'seq', mirror(seq, step))]
  transfers between devices with their start and end apart: 6 -> 23, of which waited for: 4 -> 10; matrix products, arithmetic and copies ran while one was open for 21% -> 20% of each run, Pallas kernels for 0% -> 0%
where the time goes in v3:
time: 253 us; the launch traced here: 249 us
  waiting for transfers between devices  88.9 us (35%)
  starting transfers between devices  54 us (21%)
  Pallas kernels  37.8 us (15%)
  local copies, waits for them, and re-layouts  31.6 us (12%)
  other arithmetic  25.2 us (10%)
  between operations  11.4 us (5%)
    pallas_call x1, Pallas kernels, finish(): pl.pallas_call(functools.partial(finish_kernel, len(query), seq), out_sha...  35.5 us
    ppermute x3, waiting for transfers between devices, by_channels(): ways[1][phase] = lax.ppermute(ways[1][phase - 1], 'seq', downs)  29.4 us
    all_to_all x3, waiting for transfers between devices, exchange_weights(): mine = lax.all_to_all(mine, 'seq', split_axis=0, concat_axis=0, tiled=True)  28.5 us
    ppermute x3, waiting for transfers between devices, by_channels(): lax.ppermute(gated[step], 'seq', mirror(seq, step))  19.1 us
    all_to_all x3, starting transfers between devices, exchange_weights(): mine = lax.all_to_all(mine, 'seq', split_axis=0, concat_axis=0, tiled=True)  19 us
    another operation x6, other arithmetic, by_channels(): both = jnp.stack(group)  13.4 us
    ppermute x3, starting transfers between devices, by_channels(): lax.ppermute(gated[step], 'seq', mirror(seq, step))  11.1 us
    ppermute x4, waiting for transfers between devices, by_channels(): lax.ppermute(after(arrival, last, *before.get(phase, ())), 'chan', ring(c...  9.81 us
  transfers between devices with their start and end apart: 23, of which 10 were waited for; matrix products, arithmetic and copies ran while one was open for 20% of the time, Pallas kernels for 0%

profile of v3, /device:TPU:0, one launch (start us, length us, event | category | flops | bytes accessed | tf_op | source)
XLA Modules:
  0.0 249.0 jit_solution(13014845035374545404)
XLA Ops:
  3.6 2.3 copy.10
  5.9 6.3 %all-to-all-start = ((bf16[4,512,256]{2,1,0:T(8,128)(2,1)}), bf16[4,512,256]{2,1,0:T(8,128)(2,1)}, u32[]{:S(2)}, u32[]{:S(2)}) async-start(bf16[4,512,256]{2,1,0:T(8,128)(2,1)} %bitcast.24), calls=%async_computation | async-start | bytes 2097152 | tf_op jit(solution)/shard_map/all_to_all | solution.py:149
  15.0 5.6 %collective-permute-start.5 = (bf16[512,1024]{1,0:T(8,128)(2,1)}, bf16[512,1024]{1,0:T(8,128)(2,1)}, u32[]{:S(2)}, u32[]{:S(2)}) collective-permute-start(bf16[512,1024]{1,0:T(8,128)(2,1)} %param.7), channel_id=1, source_target_pairs={{0,4},{4,8},{8,12},{1,5},{5,9},{9,13},{2,6},{6,10},{10,14},{3,7},{... | collective-permute-start | bytes 3145736 | tf_op jit(solution)/shard_map/ppermute | solution.py:378
  20.5 2.7 %constant_dynamic-slice_fusion.3 = (bf16[512,1024]{1,0:T(8,128)(2,1)S(1)}, bf16[512,1024]{1,0:T(8,128)(2,1)}) fusion(bf16[1024,1024]{1,0:T(8,128)(2,1)} %param.8, s32[]{:T(128)S(6)} %select_n.201, bf16[1024,1024]{1,0:T(8,128)(2,1)} %param.10), kind=kLoop, calls=%fused_computation.31 | loop fusion | bytes 4194308 | tf_op jit(solution)/shard_map/dynamic_slice | solution.py:147
  23.2 2.3 copy.16
  25.5 2.3 copy.12
  27.8 11.3 %all-to-all-done.refs_0_ = bf16[4,512,256]{2,1,0:T(8,128)(2,1)} async-done(((bf16[4,512,256]{2,1,0:T(8,128)(2,1)}), bf16[4,512,256]{2,1,0:T(8,128)(2,1)}, u32[]{:S(2)}, u32[]{:S(2)}) %all-to-all-start) | async-done | bytes 1048608 | tf_op jit(solution)/shard_map/all_to_all | solution.py:149
  39.1 4.3 %all-to-all-start.1 = ((bf16[4,512,256]{2,1,0:T(8,128)(2,1)}), bf16[4,512,256]{2,1,0:T(8,128)(2,1)}, u32[]{:S(2)}, u32[]{:S(2)}) async-start(bf16[4,512,256]{2,1,0:T(8,128)(2,1)} %bitcast.59), calls=%async_computation.1 | async-start | bytes 2097152 | tf_op jit(solution)/shard_map/all_to_all | solution.py:149
  46.0 10.5 %collective-permute-done.6 = bf16[512,1024]{1,0:T(8,128)(2,1)} collective-permute-done((bf16[512,1024]{1,0:T(8,128)(2,1)}, bf16[512,1024]{1,0:T(8,128)(2,1)}, u32[]{:S(2)}, u32[]{:S(2)}) %collective-permute-start.6) | collective-permute-done | bytes 1048608 | tf_op jit(solution)/shard_map/ppermute | solution.py:379
  57.7 1.6 collective-permute-start.9
  61.9 3.1 %fusion.1 = (bf16[1,512,1024]{2,1,0:T(8,128)(2,1)}, bf16[512,1024]{1,0:T(8,128)(2,1)}) fusion(bf16[512,1024]{1,0:T(8,128)(2,1)} %collective-permute-done.5, bf16[512,1024]{1,0:T(8,128)(2,1)} %collective-permute-done.6, pred[]{:T(512)S(6)} %eq.40, pred[]{:T(512)S(6)} %eq.39, pred[]{:T(512)S(6)} %eq.38, pred[]{:T(512)} %bitcast.36, pred[]{:T(512)} %bitcast.35), kind=kLoop, calls=%fused_computation.21 | loop fusion | flops 2621440 | bytes 4194309 | tf_op jit(solution)/shard_map/stack | solution.py:372
  71.5 2.3 copy.14
  73.8 10.3 %all-to-all-done.1.refs_2_ = bf16[4,512,256]{2,1,0:T(8,128)(2,1)} async-done(((bf16[4,512,256]{2,1,0:T(8,128)(2,1)}), bf16[4,512,256]{2,1,0:T(8,128)(2,1)}, u32[]{:S(2)}, u32[]{:S(2)}) %all-to-all-start.1) | async-done | bytes 1048608 | tf_op jit(solution)/shard_map/all_to_all | solution.py:149
  84.1 8.5 %all-to-all-start.2 = ((bf16[4,512,256]{2,1,0:T(8,128)(2,1)}), bf16[4,512,256]{2,1,0:T(8,128)(2,1)}, u32[]{:S(2)}, u32[]{:S(2)}) async-start(bf16[4,512,256]{2,1,0:T(8,128)(2,1)} %bitcast.30), calls=%async_computation.2 | async-start | bytes 2097152 | tf_op jit(solution)/shard_map/all_to_all | solution.py:149
  95.1 10.2 %collective-permute-done.10 = bf16[512,1024]{1,0:T(8,128)(2,1)} collective-permute-done((bf16[512,1024]{1,0:T(8,128)(2,1)}, bf16[512,1024]{1,0:T(8,128)(2,1)}, u32[]{:S(2)}, u32[]{:S(2)}) %collective-permute-start.10) | collective-permute-done | bytes 1048608 | tf_op jit(solution)/shard_map/ppermute | solution.py:379
  106.7 1.7 collective-permute-start.13
  113.4 2.7 %select_select_fusion.4 = (bf16[512,1024]{1,0:T(8,128)(2,1)}, bf16[512,1024]{1,0:T(8,128)(2,1)S(1)}) fusion(pred[]{:T(512)} %bitcast.41, pred[]{:T(512)} %bitcast.40, pred[]{:T(512)} %bitcast.39, bf16[512,1024]{1,0:T(8,128)(2,1)} %collective-permute-done.9, bf16[512,1024]{1,0:T(8,128)(2,1)} %collective-permute-done.6, ...), kind=kLoop, calls=%fused_computation.13 | loop fusion | flops 3145728 | bytes 5242886 | tf_op jit(solution)/shard_map/jit(_where)/select_n | solution.py:125
  121.3 6.8 %all-to-all-done.2.refs_4_ = bf16[4,512,256]{2,1,0:T(8,128)(2,1)} async-done(((bf16[4,512,256]{2,1,0:T(8,128)(2,1)}), bf16[4,512,256]{2,1,0:T(8,128)(2,1)}, u32[]{:S(2)}, u32[]{:S(2)}) %all-to-all-start.2) | async-done | bytes 1048608 | tf_op jit(solution)/shard_map/all_to_all | solution.py:149
  130.9 2.1 collective-permute-done.1
  138.2 8.8 %collective-permute-done.14 = bf16[512,1024]{1,0:T(8,128)(2,1)} collective-permute-done((bf16[512,1024]{1,0:T(8,128)(2,1)}, bf16[512,1024]{1,0:T(8,128)(2,1)}, u32[]{:S(2)}, u32[]{:S(2)}) %collective-permute-start.14) | collective-permute-done | bytes 1048608 | tf_op jit(solution)/shard_map/ppermute | solution.py:379
  149.9 3.2 %pad_maximum_fusion.refs_6_ = bf16[2,512,1024]{2,1,0:T(8,128)(2,1)} fusion(bf16[1,512,1024]{2,1,0:T(8,128)(2,1)} %bitcast.33, bf16[1,512,1024]{2,1,0:T(8,128)(2,1)} %bitcast.32), kind=kLoop, calls=%fused_computation | loop fusion | flops 1048576 | bytes 4194304 | tf_op jit(solution)/shard_map/stack | solution.py:372
  155.1 2.8 %pad_maximum_fusion.1.refs_8_ = bf16[2,512,1024]{2,1,0:T(8,128)(2,1)} fusion(bf16[1,512,1024]{2,1,0:T(8,128)(2,1)} %bitcast.37, bf16[1,512,1024]{2,1,0:T(8,128)(2,1)S(1)} %copy-done.1), kind=kLoop, calls=%fused_computation.1 | loop fusion | flops 1048576 | bytes 4194304 | tf_op jit(solution)/shard_map/stack | solution.py:372
  158.4 2.7 %pad_maximum_fusion.2.refs_10_ = bf16[2,512,1024]{2,1,0:T(8,128)(2,1)} fusion(bf16[1,512,1024]{2,1,0:T(8,128)(2,1)} %bitcast.42, bf16[1,512,1024]{2,1,0:T(8,128)(2,1)S(1)} %bitcast.63), kind=kLoop, calls=%fused_computation.2 | loop fusion | flops 1048576 | bytes 4194304 | tf_op jit(solution)/shard_map/stack | solution.py:372
  161.2 9.8 %collective-permute-done.15 = bf16[512,1024]{1,0:T(8,128)(2,1)S(1)} collective-permute-done((bf16[512,1024]{1,0:T(8,128)(2,1)S(1)}, bf16[512,1024]{1,0:T(8,128)(2,1)S(1)}, u32[]{:S(2)}, u32[]{:S(2)}) %collective-permute-start.15) | collective-permute-done | bytes 1048608 | tf_op jit(solution)/shard_map/ppermute | solution.py:368
  174.5 2.2 pad_maximum_fusion.4.refs_1_
  177.9 2.2 pad_maximum_fusion.5.refs_3_
  180.1 35.5 %finish.1 = (bf16[512,256]{1,0:T(8,128)(2,1)}, bf16[512,256]{1,0:T(8,128)(2,1)}, bf16[512,256]{1,0:T(8,128)(2,1)}, bf16[512,256]{1,0:T(8,128)(2,1)}, f32[16,256]{1,0:T(8,128)}) custom-call(s32[18]{0:T(128)} %concatenate.21.order_ref, f32[5,16,256]{2,1,0:T(8,128)} %bitcast.65, bf16[4,512,256]{2,1,0:T(8,128)(2,1)} %all-to-all-done.refs_0_, ...), custom_call_target="tpu_custom_call" | custom-call | flops 8589934592 | bytes 23068672 | tf_op jit(solution)/shard_map/finish/pallas_call | solution.py:297
  215.6 8.7 %collective-permute-start.17 = (bf16[512,256]{1,0:T(8,128)(2,1)}, bf16[512,256]{1,0:T(8,128)(2,1)S(1)}, u32[]{:S(2)}, u32[]{:S(2)}) collective-permute-start(bf16[512,256]{1,0:T(8,128)(2,1)} %get-tuple-element.8), channel_id=1, source_target_pairs={{0,4},{4,0},{8,12},{12,8},{1,5},{5,1},{9,13},{13,9},{2,6},{6,2},{1... | collective-permute-start | bytes 786440 | tf_op jit(solution)/shard_map/ppermute | solution.py:389
  224.3 2.4 collective-permute-start.19
  226.8 8.8 %collective-permute-done.17.refs_1_ = bf16[512,256]{1,0:T(8,128)(2,1)S(1)} collective-permute-done((bf16[512,256]{1,0:T(8,128)(2,1)}, bf16[512,256]{1,0:T(8,128)(2,1)S(1)}, u32[]{:S(2)}, u32[]{:S(2)}) %collective-permute-start.17) | collective-permute-done | bytes 262176 | tf_op jit(solution)/shard_map/ppermute | solution.py:389
  235.6 10.2 %collective-permute-done.18.refs_2_ = bf16[512,256]{1,0:T(8,128)(2,1)S(1)} collective-permute-done((bf16[512,256]{1,0:T(8,128)(2,1)}, bf16[512,256]{1,0:T(8,128)(2,1)S(1)}, u32[]{:S(2)}, u32[]{:S(2)}) %collective-permute-start.18) | collective-permute-done | bytes 262176 | tf_op jit(solution)/shard_map/ppermute | solution.py:389
  246.7 2.3 place_columns.1
  (79 shorter events, 41.1 us)
Async XLA Ops:
  0.6 1.6 copy-start
  5.9 33.2 %all-to-all-start = ((bf16[4,512,256]{2,1,0:T(8,128)(2,1)}), bf16[4,512,256]{2,1,0:T(8,128)(2,1)}, u32[]{:S(2)}, u32[]{:S(2)}) async-start(bf16[4,512,256]{2,1,0:T(8,128)(2,1)} %bitcast.24), calls=%async_computation | async-start | bytes 2097152 | tf_op jit(solution)/shard_map/all_to_all | solution.py:149
  12.2 31.2 %collective-permute-start.3 = (bf16[512,1024]{1,0:T(8,128)(2,1)}, bf16[512,1024]{1,0:T(8,128)(2,1)}, u32[]{:S(2)}, u32[]{:S(2)}) collective-permute-start(bf16[512,1024]{1,0:T(8,128)(2,1)} %param.7), channel_id=1, source_target_pairs={{0,2},{2,0},{1,3},{3,1},{4,6},{6,4},{5,7},{7,5},{8,10},{10,8},{9,1... | collective-permute-start | bytes 3145736 | tf_op jit(solution)/shard_map/ppermute | solution.py:368
  13.7 42.8 %collective-permute-start.6 = (bf16[512,1024]{1,0:T(8,128)(2,1)}, bf16[512,1024]{1,0:T(8,128)(2,1)}, u32[]{:S(2)}, u32[]{:S(2)}) collective-permute-start(bf16[512,1024]{1,0:T(8,128)(2,1)} %param.7), channel_id=1, source_target_pairs={{4,0},{8,4},{12,8},{5,1},{9,5},{13,9},{6,2},{10,6},{14,10},{7,3},{... | collective-permute-start | bytes 3145736 | tf_op jit(solution)/shard_map/ppermute | solution.py:379
  15.0 42.8 %collective-permute-start.5 = (bf16[512,1024]{1,0:T(8,128)(2,1)}, bf16[512,1024]{1,0:T(8,128)(2,1)}, u32[]{:S(2)}, u32[]{:S(2)}) collective-permute-start(bf16[512,1024]{1,0:T(8,128)(2,1)} %param.7), channel_id=1, source_target_pairs={{0,4},{4,8},{8,12},{1,5},{5,9},{9,13},{2,6},{6,10},{10,14},{3,7},{... | collective-permute-start | bytes 3145736 | tf_op jit(solution)/shard_map/ppermute | solution.py:378
  39.1 45.0 %all-to-all-start.1 = ((bf16[4,512,256]{2,1,0:T(8,128)(2,1)}), bf16[4,512,256]{2,1,0:T(8,128)(2,1)}, u32[]{:S(2)}, u32[]{:S(2)}) async-start(bf16[4,512,256]{2,1,0:T(8,128)(2,1)} %bitcast.59), calls=%async_computation.1 | async-start | bytes 2097152 | tf_op jit(solution)/shard_map/all_to_all | solution.py:149
  56.4 48.9 %collective-permute-start.10 = (bf16[512,1024]{1,0:T(8,128)(2,1)}, bf16[512,1024]{1,0:T(8,128)(2,1)}, u32[]{:S(2)}, u32[]{:S(2)}) collective-permute-start(bf16[512,1024]{1,0:T(8,128)(2,1)} %collective-permute-done.6), channel_id=1, source_target_pairs={{4,0},{8,4},{5,1},{9,5},{6,2},{10,6},{7,3},{11,7},{20,16},{24,20},... | collective-permute-start | bytes 3145736 | tf_op jit(solution)/shard_map/ppermute | solution.py:379
  57.7 48.9 %collective-permute-start.9 = (bf16[512,1024]{1,0:T(8,128)(2,1)}, bf16[512,1024]{1,0:T(8,128)(2,1)}, u32[]{:S(2)}, u32[]{:S(2)}) collective-permute-start(bf16[512,1024]{1,0:T(8,128)(2,1)} %collective-permute-done.5), channel_id=1, source_target_pairs={{4,8},{8,12},{5,9},{9,13},{6,10},{10,14},{7,11},{11,15},{20,24},{2... | collective-permute-start | bytes 3145736 | tf_op jit(solution)/shard_map/ppermute | solution.py:378
  65.0 45.9 %collective-permute-start.7 = (bf16[512,1024]{1,0:T(8,128)(2,1)}, bf16[512,1024]{1,0:T(8,128)(2,1)}, u32[]{:S(2)}, u32[]{:S(2)}) collective-permute-start(bf16[512,1024]{1,0:T(8,128)(2,1)} %get-tuple-element.17), channel_id=1, source_target_pairs={{0,2},{2,0},{1,3},{3,1},{4,6},{6,4},{5,7},{7,5},{8,10},{10,8},{9,1... | collective-permute-start | bytes 3145736 | tf_op jit(solution)/shard_map/ppermute | solution.py:368
  68.6 39.7 %collective-permute-start = (bf16[3,512,256]{2,1,0:T(8,128)(2,1)}, bf16[3,512,256]{2,1,0:T(8,128)(2,1)}, u32[]{:S(2)}, u32[]{:S(2)}) collective-permute-start(bf16[3,512,256]{2,1,0:T(8,128)(2,1)} %pad_maximum_fusion.7), channel_id=1, source_target_pairs={{0,16},{16,0},{1,17},{17,1},{2,18},{18,2},{3,19},{19,3},{4,20},{20... | collective-permute-start | bytes 2359304 | tf_op jit(solution)/shard_map/ppermute | solution.py:157
  84.1 44.0 %all-to-all-start.2 = ((bf16[4,512,256]{2,1,0:T(8,128)(2,1)}), bf16[4,512,256]{2,1,0:T(8,128)(2,1)}, u32[]{:S(2)}, u32[]{:S(2)}) async-start(bf16[4,512,256]{2,1,0:T(8,128)(2,1)} %bitcast.30), calls=%async_computation.2 | async-start | bytes 2097152 | tf_op jit(solution)/shard_map/all_to_all | solution.py:149
  105.4 41.6 %collective-permute-start.14 = (bf16[512,1024]{1,0:T(8,128)(2,1)}, bf16[512,1024]{1,0:T(8,128)(2,1)}, u32[]{:S(2)}, u32[]{:S(2)}) collective-permute-start(bf16[512,1024]{1,0:T(8,128)(2,1)} %collective-permute-done.10), channel_id=1, source_target_pairs={{4,0},{5,1},{6,2},{7,3},{20,16},{21,17},{22,18},{23,19}} | collective-permute-start | bytes 3145736 | tf_op jit(solution)/shard_map/ppermute | solution.py:379
  106.7 40.3 %collective-permute-start.13 = (bf16[512,1024]{1,0:T(8,128)(2,1)}, bf16[512,1024]{1,0:T(8,128)(2,1)}, u32[]{:S(2)}, u32[]{:S(2)}) collective-permute-start(bf16[512,1024]{1,0:T(8,128)(2,1)} %collective-permute-done.9), channel_id=1, source_target_pairs={{8,12},{9,13},{10,14},{11,15},{24,28},{25,29},{26,30},{27,31}} | collective-permute-start | bytes 3145736 | tf_op jit(solution)/shard_map/ppermute | solution.py:378
  116.2 19.4 %collective-permute-start.11 = (bf16[512,1024]{1,0:T(8,128)(2,1)}, bf16[512,1024]{1,0:T(8,128)(2,1)}, u32[]{:S(2)}, u32[]{:S(2)}) collective-permute-start(bf16[512,1024]{1,0:T(8,128)(2,1)} %get-tuple-element.14), channel_id=1, source_target_pairs={{0,2},{2,0},{1,3},{3,1},{4,6},{6,4},{5,7},{7,5},{8,10},{10,8},{9,1... | collective-permute-start | bytes 3145736 | tf_op jit(solution)/shard_map/ppermute | solution.py:368
  119.8 13.2 %collective-permute-start.1 = (bf16[3,512,256]{2,1,0:T(8,128)(2,1)}, bf16[3,512,256]{2,1,0:T(8,128)(2,1)}, u32[]{:S(2)}, u32[]{:S(2)}) collective-permute-start(bf16[3,512,256]{2,1,0:T(8,128)(2,1)} %pad_maximum_fusion.8), channel_id=1, source_target_pairs={{0,16},{16,0},{1,17},{17,1},{2,18},{18,2},{3,19},{19,3},{4,20},{20... | collective-permute-start | bytes 2359304 | tf_op jit(solution)/shard_map/ppermute | solution.py:157
  129.4 23.7 %collective-permute-start.2 = (bf16[3,512,256]{2,1,0:T(8,128)(2,1)S(1)}, bf16[3,512,256]{2,1,0:T(8,128)(2,1)S(1)}, u32[]{:S(2)}, u32[]{:S(2)}) collective-permute-start(bf16[3,512,256]{2,1,0:T(8,128)(2,1)S(1)} %pad_maximum_fusion.9), channel_id=1, source_target_pairs={{0,16},{16,0},{1,17},{17,1},{2,18},{18,2},{3,19},{19,3},{4,20},{20... | collective-permute-start | bytes 2359304 | tf_op jit(solution)/shard_map/ppermute | solution.py:157
  148.4 22.6 %collective-permute-start.15 = (bf16[512,1024]{1,0:T(8,128)(2,1)S(1)}, bf16[512,1024]{1,0:T(8,128)(2,1)S(1)}, u32[]{:S(2)}, u32[]{:S(2)}) collective-permute-start(bf16[512,1024]{1,0:T(8,128)(2,1)S(1)} %get-tuple-element.12), channel_id=1, source_target_pairs={{0,2},{2,0},{1,3},{3,1},{4,6},{6,4},{5,7},{7,5},{8,10},{10,8},{9,1... | collective-permute-start | bytes 3145736 | tf_op jit(solution)/shard_map/ppermute | solution.py:368
  149.9 5.2 %copy-start.1 = (bf16[1,512,1024]{2,1,0:T(8,128)(2,1)S(1)}, bf16[1,512,1024]{2,1,0:T(8,128)(2,1)}, u32[]{:S(2)}) copy-start(bf16[1,512,1024]{2,1,0:T(8,128)(2,1)} %get-tuple-element.16) | copy-start | bytes 3145732
  153.1 27.0 %collective-permute-start.4 = (bf16[2,512,1024]{2,1,0:T(8,128)(2,1)}, bf16[2,512,1024]{2,1,0:T(8,128)(2,1)}, u32[]{:S(2)}, u32[]{:S(2)}) collective-permute-start(bf16[2,512,1024]{2,1,0:T(8,128)(2,1)} %pad_maximum_fusion.refs_6_), channel_id=1, source_target_pairs={{0,1},{1,0},{2,3},{3,2},{4,5},{5,4},{6,7},{7,6},{8,9},{9,8},{10,11... | collective-permute-start | bytes 6291464 | tf_op jit(solution)/shard_map/ppermute | solution.py:373
  153.1 4.8 %copy-start.2 = (bf16[3,512,256]{2,1,0:T(8,128)(2,1)}, bf16[3,512,256]{2,1,0:T(8,128)(2,1)S(1)}, u32[]{:S(2)}) copy-start(bf16[3,512,256]{2,1,0:T(8,128)(2,1)S(1)} %collective-permute-done.2) | copy-start | bytes 2359300
  157.9 22.2 %collective-permute-start.8 = (bf16[2,512,1024]{2,1,0:T(8,128)(2,1)}, bf16[2,512,1024]{2,1,0:T(8,128)(2,1)}, u32[]{:S(2)}, u32[]{:S(2)}) collective-permute-start(bf16[2,512,1024]{2,1,0:T(8,128)(2,1)} %pad_maximum_fusion.1.refs_8_), channel_id=1, source_target_pairs={{0,1},{1,0},{2,3},{3,2},{4,5},{5,4},{6,7},{7,6},{8,9},{9,8},{10,11... | collective-permute-start | bytes 6291464 | tf_op jit(solution)/shard_map/ppermute | solution.py:373
  161.1 18.9 %collective-permute-start.12 = (bf16[2,512,1024]{2,1,0:T(8,128)(2,1)}, bf16[2,512,1024]{2,1,0:T(8,128)(2,1)}, u32[]{:S(2)}, u32[]{:S(2)}) collective-permute-start(bf16[2,512,1024]{2,1,0:T(8,128)(2,1)} %pad_maximum_fusion.2.refs_10_), channel_id=1, source_target_pairs={{0,1},{1,0},{2,3},{3,2},{4,5},{5,4},{6,7},{7,6},{8,9},{9,8},{10,11... | collective-permute-start | bytes 6291464 | tf_op jit(solution)/shard_map/ppermute | solution.py:373
  171.0 3.3 %copy-start.4 = (f32[256,16]{0,1:T(8,128)S(1)}, f32[256,16]{0,1:T(8,128)}, u32[]{:S(2)}) copy-start(f32[256,16]{0,1:T(8,128)} %param.11) | copy-start | bytes 49156
  171.0 3.4 %copy-start.8 = (f32[256,16]{0,1:T(8,128)S(1)}, f32[256,16]{0,1:T(8,128)}, u32[]{:S(2)}) copy-start(f32[256,16]{0,1:T(8,128)} %param.12) | copy-start | bytes 49156
  171.0 3.4 %copy-start.9 = (f32[256,16]{0,1:T(8,128)S(1)}, f32[256,16]{0,1:T(8,128)}, u32[]{:S(2)}) copy-start(f32[256,16]{0,1:T(8,128)} %param.13) | copy-start | bytes 49156
  172.5 4.2 %copy-start.3 = (bf16[3,512,256]{2,1,0:T(8,128)(2,1)S(1)}, bf16[3,512,256]{2,1,0:T(8,128)(2,1)}, u32[]{:S(2)}) copy-start(bf16[3,512,256]{2,1,0:T(8,128)(2,1)} %copy-done.2) | copy-start | bytes 2359300
  172.5 7.5 %collective-permute-start.16 = (bf16[2,512,1024]{2,1,0:T(8,128)(2,1)}, bf16[2,512,1024]{2,1,0:T(8,128)(2,1)}, u32[]{:S(2)}, u32[]{:S(2)}) collective-permute-start(bf16[2,512,1024]{2,1,0:T(8,128)(2,1)} %pad_maximum_fusion.3.refs_12_), channel_id=1, source_target_pairs={{0,1},{1,0},{2,3},{3,2},{4,5},{5,4},{6,7},{7,6},{8,9},{9,8},{10,11... | collective-permute-start | bytes 6291464 | tf_op jit(solution)/shard_map/ppermute | solution.py:373
  174.5 3.3 %copy-start.10 = (f32[5,256,16]{1,2,0:T(8,128)}, f32[5,256,16]{1,2,0:T(8,128)S(1)}, u32[]{:S(2)}) copy-start(f32[5,256,16]{1,2,0:T(8,128)S(1)} %bitcast_dynamic-update-slice_fusion) | copy-start | bytes 245764
  215.6 20.0 %collective-permute-start.17 = (bf16[512,256]{1,0:T(8,128)(2,1)}, bf16[512,256]{1,0:T(8,128)(2,1)S(1)}, u32[]{:S(2)}, u32[]{:S(2)}) collective-permute-start(bf16[512,256]{1,0:T(8,128)(2,1)} %get-tuple-element.8), channel_id=1, source_target_pairs={{0,4},{4,0},{8,12},{12,8},{1,5},{5,1},{9,13},{13,9},{2,6},{6,2},{1... | collective-permute-start | bytes 786440 | tf_op jit(solution)/shard_map/ppermute | solution.py:389
  224.3 21.5 %collective-permute-start.18 = (bf16[512,256]{1,0:T(8,128)(2,1)}, bf16[512,256]{1,0:T(8,128)(2,1)S(1)}, u32[]{:S(2)}, u32[]{:S(2)}) collective-permute-start(bf16[512,256]{1,0:T(8,128)(2,1)} %get-tuple-element.9), channel_id=1, source_target_pairs={{0,8},{4,12},{8,0},{12,4},{1,9},{5,13},{9,1},{13,5},{2,10},{6,14},... | collective-permute-start | bytes 786440 | tf_op jit(solution)/shard_map/ppermute | solution.py:389
  224.3 21.5 %collective-permute-start.19 = (bf16[512,256]{1,0:T(8,128)(2,1)}, bf16[512,256]{1,0:T(8,128)(2,1)S(1)}, u32[]{:S(2)}, u32[]{:S(2)}) collective-permute-start(bf16[512,256]{1,0:T(8,128)(2,1)} %get-tuple-element.10), channel_id=1, source_target_pairs={{0,12},{4,8},{8,4},{12,0},{1,13},{5,9},{9,5},{13,1},{2,14},{6,10},... | collective-permute-start | bytes 786440 | tf_op jit(solution)/shard_map/ppermute | solution.py:389
  235.6 10.3 %copy-start.5 = (bf16[512,256]{1,0:T(8,128)(2,1)}, bf16[512,256]{1,0:T(8,128)(2,1)S(1)}, u32[]{:S(2)}) copy-start(bf16[512,256]{1,0:T(8,128)(2,1)S(1)} %collective-permute-done.17.refs_1_) | copy-start | bytes 786436
  (2 other events, 1.5 us)

commit v4 on v3

--- a/solution.py
+++ b/solution.py
@@ -10,10 +10,11 @@
 BLOCK = 128
 SUBLANES, LANES = 8, 128
 TILE = 256
-UNROLL = 4
+UNROLL = 8
 GATHER_BYTES = 24 << 20
 KERNEL_BYTES = 56 << 20
 FINISH_COST = 4
+WEIGHT = 23 * 10**9
 
 
 HIGHEST_PRECISION = lax.Precision.HIGHEST
@@ -118,12 +119,42 @@
     return [(i, i ^ step) for i in range(size)]
 
 
-def after(x, *earlier):
-    for other in earlier:
-        if other is not None:
-            probe = lax.slice(other, [n - 1 for n in other.shape], other.shape).reshape(())
-            x = jnp.where(probe != probe, jnp.zeros((), x.dtype), x)
-    return x
+def choose(index, candidates, waits, weight=0):
+    shape = candidates[0]
+
+    def kernel(index_ref, *refs):
+        for i in range(len(candidates)):
+
+            @pl.when(index_ref[0] == i)
+            def _():
+                refs[-1][...] = refs[i][...]
+
+    vmem = pl.BlockSpec(memory_space=pltpu.VMEM)
+    return pl.pallas_call(
+        kernel,
+        out_shape=jax.ShapeDtypeStruct(shape.shape, shape.dtype),
+        in_specs=[pl.BlockSpec(memory_space=pltpu.SMEM)]
+        + [vmem] * len(candidates)
+        + [pl.BlockSpec(memory_space=pl.ANY)] * len(waits),
+        out_specs=vmem,
+        cost_estimate=pl.CostEstimate(flops=weight, bytes_accessed=2 * shape.size, transcendentals=0),
+        name="choose",
+    )(index.reshape(1).astype(jnp.int32), *candidates, *waits)
+
+
+def after(x, *waits):
+    def nothing(*refs):
+        del refs
+
+    anywhere = pl.BlockSpec(memory_space=pl.ANY)
+    return pl.pallas_call(
+        nothing,
+        out_shape=jax.ShapeDtypeStruct(x.shape, x.dtype),
+        in_specs=[anywhere] * (1 + len(waits)),
+        out_specs=anywhere,
+        input_output_aliases={0: 0},
+        name="after",
+    )(x, *waits)
 
 
 def arrival_order(size):
@@ -144,8 +175,9 @@
     place, part = lax.axis_index("seq"), lax.axis_index("parts")
     depth, width = weight.shape[0], weight.shape[1] // seq
     share = depth // parts
-    mine = lax.dynamic_slice(weight, (part * share, 0), (share, weight.shape[1]))
-    mine = mine.reshape(share, seq, width).transpose(1, 0, 2)
+    mine = jnp.stack(
+        [lax.dynamic_slice(weight, (part * share, i * width), (share, width)) for i in range(seq)]
+    )
     mine = lax.all_to_all(mine, "seq", split_axis=0, concat_axis=0, tiled=True)
     fetched = jnp.concatenate(
         [lax.dynamic_slice(mine, (place ^ step, 0, 0), (1, share, width)) for step in range(1, seq)]
@@ -154,21 +186,30 @@
     for turn in range(1, parts):
         first = (part - turn) % parts * share
         own = lax.dynamic_slice(weight, (first, place * width), (share, width))
-        shares.append(jnp.concatenate([own[None], lax.ppermute(fetched, "parts", ring(parts, turn))]))
+        shares += [own, lax.ppermute(fetched, "parts", ring(parts, turn))]
     return shares
 
 
 def weight_copies(order_ref, w_hbm, w_buf, w_sem):
     quarters, share, width = w_hbm[0].shape
     parts = w_buf.shape[0] // (quarters * share)
+    each = 2 * parts - 1
     copies = []
-    for k, ref in enumerate(w_hbm):
-        columns = pl.ds(k // parts * width, width)
-        shift = order_ref[quarters + k % parts] * share
+
+    def add(source, k, quarter, turn, index):
+        row = quarter * (parts * share) + order_ref[quarters + turn] * share
+        at = w_buf.at[pl.ds(pl.multiple_of(row, share), share), pl.ds(k * width, width)]
+        copies.append(pltpu.make_async_copy(source, at, w_sem.at[k * parts + turn, index]))
+
+    for k in range(len(w_hbm) // each):
+        mine, *others = w_hbm[k * each : (k + 1) * each]
         for q in range(quarters):
-            at = pl.ds(pl.multiple_of(q * parts * share + shift, share), share)
-            block = order_ref[q] if k % parts == 0 else order_ref[quarters + parts + q]
-            copies.append(pltpu.make_async_copy(ref.at[block], w_buf.at[at, columns], w_sem.at[k, q]))
+            add(mine.at[order_ref[q]], k, q, 0, q)
+        for turn in range(1, parts):
+            own, fetched = others[2 * turn - 2 : 2 * turn]
+            for step in range(quarters):
+                source = fetched.at[step - 1] if step else own
+                add(source, k, order_ref[quarters + parts + step], turn, step)
     return copies
 
 
@@ -226,8 +267,8 @@
         conv_ref[:, lanes] = result[...].astype(jnp.bfloat16)
 
 
-def finish_kernel(n_weights, seq, order_ref, modes_ref, *refs):
-    refs = list(refs)
+def finish_kernel(n_weights, counts, order_ref, modes_ref, *refs):
+    refs, seq = list(refs), len(counts)
 
     def take(count):
         taken = refs[:count]
@@ -235,14 +276,13 @@
         return taken
 
     pair_hbm, query_hbm = take(2 * n_weights), take(n_weights)
-    each = (len(refs) - 11 - seq) // seq
-    x_hbm = [take(each) for _ in range(seq)]
+    x_hbm = [take(count) for count in counts]
     outs, (state_ref,) = take(seq), take(1)
     x_buf, pair_buf, query_buf, prod, out, ends, conv_buf, x_sem, pair_sem, query_sem = take(10)
     rows = x_buf.shape[1]
     channels = conv_buf.shape[1]
     groups = prod.shape[0]
-    first = 2 * pair_sem.shape[1] + n_weights
+    first = 2 * pair_sem.shape[1] + (n_weights + 1) // 2
     x_copies = [token_copies(x_hbm[i], x_buf.at[i], x_sem.at[i]) for i in range(seq)]
     pair_copies = weight_copies(order_ref, pair_hbm, pair_buf, pair_sem)
     query_copies = weight_copies(order_ref, query_hbm, query_buf, query_sem)
@@ -295,7 +335,7 @@
     vmem, anywhere = pl.BlockSpec(memory_space=pltpu.VMEM), pl.BlockSpec(memory_space=pl.ANY)
     arrays = [*pair, *query, *sum(xs, [])]
     *gated, state = pl.pallas_call(
-        functools.partial(finish_kernel, len(query), seq),
+        functools.partial(finish_kernel, len(query), [len(x) for x in xs]),
         out_shape=tuple(jax.ShapeDtypeStruct((rows, width), jnp.bfloat16) for _ in range(seq))
         + (jax.ShapeDtypeStruct((modes, width), jnp.float32),),
         in_specs=[pl.BlockSpec(memory_space=pltpu.SMEM), vmem]
@@ -310,8 +350,8 @@
             pltpu.VMEM((modes, SUBLANES, LANES), jnp.float32),
             pltpu.VMEM((length, width), jnp.bfloat16),
             pltpu.SemaphoreType.DMA((seq, quarters)),
-            pltpu.SemaphoreType.DMA((len(pair), quarters)),
-            pltpu.SemaphoreType.DMA((len(query), quarters)),
+            pltpu.SemaphoreType.DMA((len(pair) + 2 >> 1, quarters)),
+            pltpu.SemaphoreType.DMA((len(query) + 1 >> 1, quarters)),
         ],
         compiler_params=pltpu.CompilerParams(vmem_limit_bytes=KERNEL_BYTES),
         cost_estimate=pl.CostEstimate(
@@ -355,22 +395,26 @@
         return value
 
     w_keys, w_values, w_queries = [exchange_weights(w, sizes) for w in (w_key, w_value, w_query)]
-    before = {2: w_keys[:1], 3: w_keys[1:] + w_values[:1], 4: w_values[1:]}
+    before = {2: w_keys[:1], 3: w_keys[-1:] + w_values[:1], 4: w_values[-1:]}
     shares = [(lax.axis_index("parts") - turn) % parts for turn in range(parts)]
     features = [
         ((x_place - turn) % chan) * rep + (core - other) % rep for other in range(rep) for turn in range(chan)
     ]
-    by_feature = jnp.stack([jnp.int32(i) for i in features + shares + [f ^ place for f in features]])
+    positions = [sum(jnp.where(f == place ^ step, q, 0) for q, f in enumerate(features)) for step in range(seq)]
+    by_feature = jnp.stack([jnp.int32(i) for i in features + shares + positions])
     arrival, ways, xs, origins, last = tokens, [{0: tokens}, {0: tokens}], [], [place], None
     for phase in range(1, seq + 1):
         group = [arrival]
         for turn in range(1, chan):
-            last = lax.ppermute(after(arrival, last, *before.get(phase, ())), "chan", ring(chan, turn))
+            last = lax.ppermute(arrival, "chan", ring(chan, turn))
             group.append(last)
         if phase == seq:
-            group[-1] = after(group[-1], *w_queries[1:])
-        both = jnp.stack(group)
-        xs.append([both] + [lax.ppermute(both, "rep", ring(rep, turn)) for turn in range(1, rep)])
+            group[-1] = after(group[-1], w_queries[-1])
+            group = [x[None] for x in group]
+        else:
+            group = [jnp.stack(group)]
+        swapped = [lax.ppermute(x, "rep", ring(rep, turn)) for turn in range(1, rep) for x in group]
+        xs.append(group + swapped)
         if phase == seq:
             break
         ups = [(i, i + 1) for i in range(phase - 1, seq - 1)]
@@ -378,7 +422,14 @@
         ways[0][phase] = lax.ppermute(ways[0][phase - 1], "seq", ups)
         ways[1][phase] = lax.ppermute(ways[1][phase - 1], "seq", downs)
         chosen = [orders[i][phase - 1] for i in range(seq)]
-        arrival = at_place([ways[way][step] for way, step, origin in chosen])
+        sources = sorted({(way, step) for way, step, origin in chosen})
+        index = at_place([jnp.int32(sources.index((way, step))) for way, step, origin in chosen])
+        arrival = choose(
+            index,
+            [ways[way][step] for way, step in sources],
+            [last, *before.get(phase + 1, ())],
+            WEIGHT if phase == seq - 1 else 0,
+        )
         origins.append(at_place([jnp.int32(origin) for way, step, origin in chosen]))
 
     steps = [place ^ origin for origin in origins]

time: 253 us -> 233 us (0.921)
  waiting for transfers between devices: 88.9 us -> 108 us
  local copies, waits for them, and re-layouts: 31.6 us -> 13.1 us
  other arithmetic: 25.2 us -> 12.1 us
  between operations: 11.4 us -> 0.95 us
  Pallas kernels: 37.8 us -> 45.7 us
  starting transfers between devices: 54 us -> 50.4 us
    ppermute x3, waiting for transfers between devices: 29.4 us -> 54.5 us  [by_channels(): ways[1][phase] = lax.ppermute(ways[1][phase - 1], 'seq', downs)]
    all_to_all x3, waiting for transfers between devices: 28.5 us -> 15.3 us  [exchange_weights(): mine = lax.all_to_all(mine, 'seq', split_axis=0, concat_axis=0, tiled=True)]
    slice x8 -> x0, local copies, waits for them, and re-layouts: 9.41 us -> none  [after(): lax.slice(other, [n - 1 for n in other.shape], other.shape).reshape(())]
    ppermute x11 -> x12, waiting for transfers between devices: 11.9 us -> 20.6 us  [the longest x3 17.9 us: exchange_weights(): shares += [own, lax.ppermute(fetched, 'parts', ring(parts, turn))]]
    pallas_call x1 -> x5, Pallas kernels: 35.5 us -> 43.4 us  [the longest x1 34.4 us: finish(): pl.pallas_call(functools.partial(finish_kernel, len(query), [len(x) for x...]
    reshape x3 -> x0, local copies, waits for them, and re-layouts: 6.78 us -> none  [exchange_weights(): mine = mine.reshape(share, seq, width).transpose(1, 0, 2)]
    ppermute x3, starting transfers between devices: 11.1 us -> 4.45 us  [by_channels(): lax.ppermute(gated[step], 'seq', mirror(seq, step))]
    concatenate x3 -> x0, other arithmetic: 5.54 us -> none  [exchange_weights(): jnp.concatenate([own[None], lax.ppermute(fetched, 'parts', ring(parts, tu...]
  transfers between devices with their start and end apart: 23 -> 24, of which waited for: 10 -> 9; matrix products, arithmetic and copies ran while one was open for 20% -> 7% of each run, Pallas kernels for 0% -> 4%
where the time goes in v4:
time: 233 us; the launch traced here: 230 us
  waiting for transfers between devices  108 us (46%)
  starting transfers between devices  50.4 us (22%)
  Pallas kernels  45.7 us (20%)
  local copies, waits for them, and re-layouts  13.1 us (6%)
  other arithmetic  12.1 us (5%)
    ppermute x3, waiting for transfers between devices, by_channels(): ways[1][phase] = lax.ppermute(ways[1][phase - 1], 'seq', downs)  54.5 us
    pallas_call x1, Pallas kernels, finish(): pl.pallas_call(functools.partial(finish_kernel, len(query), [len(x) for x...  34.4 us
    all_to_all x3, starting transfers between devices, exchange_weights(): mine = lax.all_to_all(mine, 'seq', split_axis=0, concat_axis=0, tiled=True)  21.5 us
    ppermute x3, waiting for transfers between devices, exchange_weights(): shares += [own, lax.ppermute(fetched, 'parts', ring(parts, turn))]  17.9 us
    ppermute x3, waiting for transfers between devices, by_channels(): lax.ppermute(gated[step], 'seq', mirror(seq, step))  17.4 us
    all_to_all x3, waiting for transfers between devices, exchange_weights(): mine = lax.all_to_all(mine, 'seq', split_axis=0, concat_axis=0, tiled=True)  15.3 us
    pallas_call x3, Pallas kernels, choose(): pl.pallas_call(kernel, out_shape=jax.ShapeDtypeStruct(shape.shape, shape....  8.99 us
    ppermute x3, starting transfers between devices, by_channels(): ways[0][phase] = lax.ppermute(ways[0][phase - 1], 'seq', ups)  8.83 us
  transfers between devices with their start and end apart: 24, of which 9 were waited for; matrix products, arithmetic and copies ran while one was open for 7% of the time, Pallas kernels for 4%

profile of v4, /device:TPU:0, one launch (start us, length us, event | category | flops | bytes accessed | tf_op | source)
XLA Modules:
  0.0 230.1 jit_solution(5484192309076395536)
XLA Ops:
  0.7 2.1 fusion.2
  3.8 6.3 %all-to-all-start = ((bf16[4,512,256]{2,1,0:T(8,128)(2,1)}), bf16[4,512,256]{2,1,0:T(8,128)(2,1)S(1)}, u32[]{:S(2)}, u32[]{:S(2)}) async-start(bf16[4,512,256]{2,1,0:T(8,128)(2,1)} %pad_maximum_fusion.3), calls=%async_computation | async-start | bytes 2097152 | tf_op jit(solution)/shard_map/all_to_all | solution.py:181
  11.4 5.5 %collective-permute-start.5 = (bf16[512,1024]{1,0:T(8,128)(2,1)}, bf16[512,1024]{1,0:T(8,128)(2,1)}, u32[]{:S(2)}, u32[]{:S(2)}) collective-permute-start(bf16[512,1024]{1,0:T(8,128)(2,1)} %param.7), channel_id=1, source_target_pairs={{0,4},{4,8},{8,12},{1,5},{5,9},{9,13},{2,6},{6,10},{10,14},{3,7},{... | collective-permute-start | bytes 3145736 | tf_op jit(solution)/shard_map/ppermute | solution.py:422
  17.0 1.5 collective-permute-start.3
  18.5 2.1 fusion.1
  21.7 15.3 %all-to-all-done.refs_3_.refs_0_ = bf16[4,512,256]{2,1,0:T(8,128)(2,1)S(1)} async-done(((bf16[4,512,256]{2,1,0:T(8,128)(2,1)}), bf16[4,512,256]{2,1,0:T(8,128)(2,1)S(1)}, u32[]{:S(2)}, u32[]{:S(2)}) %all-to-all-start) | async-done | bytes 1048608 | tf_op jit(solution)/shard_map/all_to_all | solution.py:181
  37.0 3.5 %all-to-all-start.1 = ((bf16[4,512,256]{2,1,0:T(8,128)(2,1)}), bf16[4,512,256]{2,1,0:T(8,128)(2,1)S(1)}, u32[]{:S(2)}, u32[]{:S(2)}) async-start(bf16[4,512,256]{2,1,0:T(8,128)(2,1)} %pad_maximum_fusion.4), calls=%async_computation.1 | async-start | bytes 2097152 | tf_op jit(solution)/shard_map/all_to_all | solution.py:181
  40.5 13.8 %collective-permute-done.6.refs_1_ = bf16[512,1024]{1,0:T(8,128)(2,1)S(1)} collective-permute-done((bf16[512,1024]{1,0:T(8,128)(2,1)}, bf16[512,1024]{1,0:T(8,128)(2,1)S(1)}, u32[]{:S(2)}, u32[]{:S(2)}) %collective-permute-start.6) | collective-permute-done | bytes 1048608 | tf_op jit(solution)/shard_map/ppermute | solution.py:423
  55.6 1.6 collective-permute-start.9
  57.2 2.6 %choose.3 = bf16[512,1024]{1,0:T(8,128)(2,1)} custom-call(s32[1]{0:T(128)} %bitcast.37.index_ref, bf16[512,1024]{1,0:T(8,128)(2,1)} %collective-permute-done.5.refs_0_, bf16[512,1024]{1,0:T(8,128)(2,1)} %copy-done.2, bf16[512,1024]{1,0:T(8,128)(2,1)} %collective-permute-done.3.refs_2_, bf16[4,512,256]{2,1,0:T(8,128)(2,1)} %copy-done.1), custom_call_target="tpu_custom_call" | custom-call | bytes 1048576 | tf_op jit(solution)/shard_map/choose/pallas_call | solution.py:133
  59.8 1.5 collective-permute-start.7
  63.5 1.5 collective-permute-start
  65.0 29.6 %collective-permute-done.10.refs_2_ = bf16[512,1024]{1,0:T(8,128)(2,1)} collective-permute-done((bf16[512,1024]{1,0:T(8,128)(2,1)S(1)}, bf16[512,1024]{1,0:T(8,128)(2,1)}, u32[]{:S(2)}, u32[]{:S(2)}) %collective-permute-start.10) | collective-permute-done | bytes 1048608 | tf_op jit(solution)/shard_map/ppermute | solution.py:423
  95.9 1.7 collective-permute-start.13
  98.9 2.9 %choose.4 = bf16[512,1024]{1,0:T(8,128)(2,1)} custom-call(s32[1]{0:T(128)} %bitcast.40.index_ref, bf16[512,1024]{1,0:T(8,128)(2,1)} %collective-permute-done.9.refs_0_, bf16[512,1024]{1,0:T(8,128)(2,1)} %copy-done.2, bf16[512,1024]{1,0:T(8,128)(2,1)} %collective-permute-done.10.refs_2_, bf16[512,1024]{1,0:T(8,128)(2,1)} %copy-done.3, ...), custom_call_target="tpu_custom_call" | custom-call | bytes 1048576 | tf_op jit(solution)/shard_map/choose/pallas_call | solution.py:133
  101.8 1.5 collective-permute-start.11
  104.5 1.6 collective-permute-start.1
  108.0 11.7 %all-to-all-start.2 = ((bf16[4,512,256]{2,1,0:T(8,128)(2,1)}), bf16[4,512,256]{2,1,0:T(8,128)(2,1)S(1)}, u32[]{:S(2)}, u32[]{:S(2)}) async-start(bf16[4,512,256]{2,1,0:T(8,128)(2,1)} %pad_maximum_fusion.5), calls=%async_computation.2 | async-start | bytes 2097152 | tf_op jit(solution)/shard_map/all_to_all | solution.py:181
  119.7 3.2 %pad_maximum_fusion.refs_9_ = bf16[2,512,1024]{2,1,0:T(8,128)(2,1)} fusion(bf16[1,512,1024]{2,1,0:T(8,128)(2,1)} %bitcast.36, bf16[1,512,1024]{2,1,0:T(8,128)(2,1)} %bitcast.35), kind=kLoop, calls=%fused_computation | loop fusion | flops 1048576 | bytes 4194304 | tf_op jit(solution)/shard_map/stack | solution.py:415
  123.0 1.5 pad_maximum_fusion.1.refs_11_
  125.0 11.2 %collective-permute-done.14.refs_3_ = bf16[512,1024]{1,0:T(8,128)(2,1)} collective-permute-done((bf16[512,1024]{1,0:T(8,128)(2,1)}, bf16[512,1024]{1,0:T(8,128)(2,1)}, u32[]{:S(2)}, u32[]{:S(2)}) %collective-permute-start.14) | collective-permute-done | bytes 1048608 | tf_op jit(solution)/shard_map/ppermute | solution.py:423
  137.2 3.5 %choose.5 = bf16[512,1024]{1,0:T(8,128)(2,1)} custom-call(s32[1]{0:T(128)} %bitcast.43.index_ref, bf16[512,1024]{1,0:T(8,128)(2,1)} %collective-permute-done.9.refs_0_, bf16[512,1024]{1,0:T(8,128)(2,1)} %collective-permute-done.13.refs_1_, bf16[512,1024]{1,0:T(8,128)(2,1)} %collective-permute-done.10.refs_2_, ...), custom_call_target="tpu_custom_call" | custom-call | flops 23000000512 | bytes 1048576 | tf_op jit(solution)/shard_map/choose/pallas_call | solution.py:133
  140.7 1.6 collective-permute-start.15
  142.3 2.7 %pad_maximum_fusion.2.refs_13_ = bf16[2,512,1024]{2,1,0:T(8,128)(2,1)} fusion(bf16[1,512,1024]{2,1,0:T(8,128)(2,1)} %bitcast.69, bf16[1,512,1024]{2,1,0:T(8,128)(2,1)S(1)} %bitcast.65), kind=kLoop, calls=%fused_computation.2 | loop fusion | flops 1048576 | bytes 4194304 | tf_op jit(solution)/shard_map/stack | solution.py:415
  145.3 1.6 collective-permute-start.2
  147.5 17.9 %collective-permute-done.2.refs_1_.refs_8_ = bf16[3,512,256]{2,1,0:T(8,128)(2,1)} collective-permute-done((bf16[3,512,256]{2,1,0:T(8,128)(2,1)S(1)}, bf16[3,512,256]{2,1,0:T(8,128)(2,1)}, u32[]{:S(2)}, u32[]{:S(2)}) %collective-permute-start.2) | collective-permute-done | bytes 786464 | tf_op jit(solution)/shard_map/ppermute | solution.py:189
  170.8 34.4 %finish.1 = (bf16[512,256]{1,0:T(8,128)(2,1)}, bf16[512,256]{1,0:T(8,128)(2,1)}, bf16[512,256]{1,0:T(8,128)(2,1)}, bf16[512,256]{1,0:T(8,128)(2,1)}, f32[16,256]{1,0:T(8,128)}) custom-call(s32[18]{0:T(128)} %concatenate.12.order_ref, f32[5,16,256]{2,1,0:T(8,128)} %bitcast.70, bf16[4,512,256]{2,1,0:T(8,128)(2,1)} %copy-done.1, ...), custom_call_target="tpu_custom_call" | custom-call | flops 8589934592 | bytes 23068672 | tf_op jit(solution)/shard_map/finish/pallas_call | solution.py:337
  205.5 1.9 collective-permute-start.19
  207.4 2.2 collective-permute-start.20
  209.6 8.7 %collective-permute-done.18.refs_1_ = bf16[512,256]{1,0:T(8,128)(2,1)S(1)} collective-permute-done((bf16[512,256]{1,0:T(8,128)(2,1)}, bf16[512,256]{1,0:T(8,128)(2,1)S(1)}, u32[]{:S(2)}, u32[]{:S(2)}) %collective-permute-start.18) | collective-permute-done | bytes 262176 | tf_op jit(solution)/shard_map/ppermute | solution.py:440
  218.3 8.7 %collective-permute-done.19.refs_2_ = bf16[512,256]{1,0:T(8,128)(2,1)S(1)} collective-permute-done((bf16[512,256]{1,0:T(8,128)(2,1)}, bf16[512,256]{1,0:T(8,128)(2,1)S(1)}, u32[]{:S(2)}, u32[]{:S(2)}) %collective-permute-start.19) | collective-permute-done | bytes 262176 | tf_op jit(solution)/shard_map/ppermute | solution.py:440
  227.8 2.3 place_columns.1
  (81 shorter events, 21.5 us)
Async XLA Ops:
  3.8 33.1 %all-to-all-start = ((bf16[4,512,256]{2,1,0:T(8,128)(2,1)}), bf16[4,512,256]{2,1,0:T(8,128)(2,1)S(1)}, u32[]{:S(2)}, u32[]{:S(2)}) async-start(bf16[4,512,256]{2,1,0:T(8,128)(2,1)} %pad_maximum_fusion.3), calls=%async_computation | async-start | bytes 2097152 | tf_op jit(solution)/shard_map/all_to_all | solution.py:181
  10.1 44.1 %collective-permute-start.6 = (bf16[512,1024]{1,0:T(8,128)(2,1)}, bf16[512,1024]{1,0:T(8,128)(2,1)S(1)}, u32[]{:S(2)}, u32[]{:S(2)}) collective-permute-start(bf16[512,1024]{1,0:T(8,128)(2,1)} %param.7), channel_id=1, source_target_pairs={{4,0},{8,4},{12,8},{5,1},{9,5},{13,9},{6,2},{10,6},{14,10},{7,3},{... | collective-permute-start | bytes 3145736 | tf_op jit(solution)/shard_map/ppermute | solution.py:423
  11.4 44.1 %collective-permute-start.5 = (bf16[512,1024]{1,0:T(8,128)(2,1)}, bf16[512,1024]{1,0:T(8,128)(2,1)}, u32[]{:S(2)}, u32[]{:S(2)}) collective-permute-start(bf16[512,1024]{1,0:T(8,128)(2,1)} %param.7), channel_id=1, source_target_pairs={{0,4},{4,8},{8,12},{1,5},{5,9},{9,13},{2,6},{6,10},{10,14},{3,7},{... | collective-permute-start | bytes 3145736 | tf_op jit(solution)/shard_map/ppermute | solution.py:422
  17.0 40.2 %collective-permute-start.3 = (bf16[512,1024]{1,0:T(8,128)(2,1)}, bf16[512,1024]{1,0:T(8,128)(2,1)}, u32[]{:S(2)}, u32[]{:S(2)}) collective-permute-start(bf16[512,1024]{1,0:T(8,128)(2,1)} %param.7), channel_id=1, source_target_pairs={{0,2},{2,0},{1,3},{3,1},{4,6},{6,4},{5,7},{7,5},{8,10},{10,8},{9,1... | collective-permute-start | bytes 3145736 | tf_op jit(solution)/shard_map/ppermute | solution.py:409
  37.0 20.3 %copy-start.1 = (bf16[4,512,256]{2,1,0:T(8,128)(2,1)}, bf16[4,512,256]{2,1,0:T(8,128)(2,1)S(1)}, u32[]{:S(2)}) copy-start(bf16[4,512,256]{2,1,0:T(8,128)(2,1)S(1)} %all-to-all-done.refs_3_.refs_0_) | copy-start | bytes 3145732
  37.0 60.6 %all-to-all-start.1 = ((bf16[4,512,256]{2,1,0:T(8,128)(2,1)}), bf16[4,512,256]{2,1,0:T(8,128)(2,1)S(1)}, u32[]{:S(2)}, u32[]{:S(2)}) async-start(bf16[4,512,256]{2,1,0:T(8,128)(2,1)} %pad_maximum_fusion.4), calls=%async_computation.1 | async-start | bytes 2097152 | tf_op jit(solution)/shard_map/all_to_all | solution.py:181
  54.3 40.3 %collective-permute-start.10 = (bf16[512,1024]{1,0:T(8,128)(2,1)S(1)}, bf16[512,1024]{1,0:T(8,128)(2,1)}, u32[]{:S(2)}, u32[]{:S(2)}) collective-permute-start(bf16[512,1024]{1,0:T(8,128)(2,1)S(1)} %collective-permute-done.6.refs_1_), channel_id=1, source_target_pairs={{4,0},{8,4},{5,1},{9,5},{6,2},{10,6},{7,3},{11,7},{20,16},{24,20},... | collective-permute-start | bytes 3145736 | tf_op jit(solution)/shard_map/ppermute | solution.py:423
  55.6 40.3 %collective-permute-start.9 = (bf16[512,1024]{1,0:T(8,128)(2,1)}, bf16[512,1024]{1,0:T(8,128)(2,1)}, u32[]{:S(2)}, u32[]{:S(2)}) collective-permute-start(bf16[512,1024]{1,0:T(8,128)(2,1)} %collective-permute-done.5.refs_0_), channel_id=1, source_target_pairs={{4,8},{8,12},{5,9},{9,13},{6,10},{10,14},{7,11},{11,15},{20,24},{2... | collective-permute-start | bytes 3145736 | tf_op jit(solution)/shard_map/ppermute | solution.py:422
  59.8 37.7 %collective-permute-start.7 = (bf16[512,1024]{1,0:T(8,128)(2,1)}, bf16[512,1024]{1,0:T(8,128)(2,1)S(1)}, u32[]{:S(2)}, u32[]{:S(2)}) collective-permute-start(bf16[512,1024]{1,0:T(8,128)(2,1)} %choose.3), channel_id=1, source_target_pairs={{0,2},{2,0},{1,3},{3,1},{4,6},{6,4},{5,7},{7,5},{8,10},{10,8},{9,1... | collective-permute-start | bytes 3145736 | tf_op jit(solution)/shard_map/ppermute | solution.py:409
  63.5 34.1 %collective-permute-start = (bf16[3,512,256]{2,1,0:T(8,128)(2,1)}, bf16[3,512,256]{2,1,0:T(8,128)(2,1)}, u32[]{:S(2)}, u32[]{:S(2)}) collective-permute-start(bf16[3,512,256]{2,1,0:T(8,128)(2,1)} %pad_maximum_fusion.6), channel_id=1, source_target_pairs={{0,16},{16,0},{1,17},{17,1},{2,18},{18,2},{3,19},{19,3},{4,20},{20... | collective-permute-start | bytes 2359304 | tf_op jit(solution)/shard_map/ppermute | solution.py:189
  94.6 41.6 %collective-permute-start.14 = (bf16[512,1024]{1,0:T(8,128)(2,1)}, bf16[512,1024]{1,0:T(8,128)(2,1)}, u32[]{:S(2)}, u32[]{:S(2)}) collective-permute-start(bf16[512,1024]{1,0:T(8,128)(2,1)} %collective-permute-done.10.refs_2_), channel_id=1, source_target_pairs={{4,0},{5,1},{6,2},{7,3},{20,16},{21,17},{22,18},{23,19}} | collective-permute-start | bytes 3145736 | tf_op jit(solution)/shard_map/ppermute | solution.py:423
  95.9 40.3 %collective-permute-start.13 = (bf16[512,1024]{1,0:T(8,128)(2,1)}, bf16[512,1024]{1,0:T(8,128)(2,1)}, u32[]{:S(2)}, u32[]{:S(2)}) collective-permute-start(bf16[512,1024]{1,0:T(8,128)(2,1)} %collective-permute-done.9.refs_0_), channel_id=1, source_target_pairs={{8,12},{9,13},{10,14},{11,15},{24,28},{25,29},{26,30},{27,31}} | collective-permute-start | bytes 3145736 | tf_op jit(solution)/shard_map/ppermute | solution.py:422
  101.8 4.3 %copy-start.10 = (bf16[1024,1024]{1,0:T(8,128)(2,1)S(1)}, bf16[1024,1024]{1,0:T(8,128)(2,1)}, u32[]{:S(2)}) copy-start(bf16[1024,1024]{1,0:T(8,128)(2,1)} %param.8) | copy-start | bytes 6291460
  101.8 34.4 %collective-permute-start.11 = (bf16[512,1024]{1,0:T(8,128)(2,1)}, bf16[512,1024]{1,0:T(8,128)(2,1)S(1)}, u32[]{:S(2)}, u32[]{:S(2)}) collective-permute-start(bf16[512,1024]{1,0:T(8,128)(2,1)} %choose.4), channel_id=1, source_target_pairs={{0,2},{2,0},{1,3},{3,1},{4,6},{6,4},{5,7},{7,5},{8,10},{10,8},{9,1... | collective-permute-start | bytes 3145736 | tf_op jit(solution)/shard_map/ppermute | solution.py:409
  104.5 20.0 %collective-permute-start.1 = (bf16[3,512,256]{2,1,0:T(8,128)(2,1)S(1)}, bf16[3,512,256]{2,1,0:T(8,128)(2,1)}, u32[]{:S(2)}, u32[]{:S(2)}) collective-permute-start(bf16[3,512,256]{2,1,0:T(8,128)(2,1)S(1)} %pad_maximum_fusion.7), channel_id=1, source_target_pairs={{0,16},{16,0},{1,17},{17,1},{2,18},{18,2},{3,19},{19,3},{4,20},{20... | collective-permute-start | bytes 2359304 | tf_op jit(solution)/shard_map/ppermute | solution.py:189
  108.0 37.0 %all-to-all-start.2 = ((bf16[4,512,256]{2,1,0:T(8,128)(2,1)}), bf16[4,512,256]{2,1,0:T(8,128)(2,1)S(1)}, u32[]{:S(2)}, u32[]{:S(2)}) async-start(bf16[4,512,256]{2,1,0:T(8,128)(2,1)} %pad_maximum_fusion.5), calls=%async_computation.2 | async-start | bytes 2097152 | tf_op jit(solution)/shard_map/all_to_all | solution.py:181
  122.9 44.1 %collective-permute-start.4 = (bf16[2,512,1024]{2,1,0:T(8,128)(2,1)}, bf16[2,512,1024]{2,1,0:T(8,128)(2,1)}, u32[]{:S(2)}, u32[]{:S(2)}) collective-permute-start(bf16[2,512,1024]{2,1,0:T(8,128)(2,1)} %pad_maximum_fusion.refs_9_), channel_id=1, source_target_pairs={{0,1},{1,0},{2,3},{3,2},{4,5},{5,4},{6,7},{7,6},{8,9},{9,8},{10,11... | collective-permute-start | bytes 6291464 | tf_op jit(solution)/shard_map/ppermute | solution.py:416
  124.5 42.5 %collective-permute-start.8 = (bf16[2,512,1024]{2,1,0:T(8,128)(2,1)}, bf16[2,512,1024]{2,1,0:T(8,128)(2,1)}, u32[]{:S(2)}, u32[]{:S(2)}) collective-permute-start(bf16[2,512,1024]{2,1,0:T(8,128)(2,1)} %pad_maximum_fusion.1.refs_11_), channel_id=1, source_target_pairs={{0,1},{1,0},{2,3},{3,2},{4,5},{5,4},{6,7},{7,6},{8,9},{9,8},{10,11... | collective-permute-start | bytes 6291464 | tf_op jit(solution)/shard_map/ppermute | solution.py:416
  137.2 5.1 %copy-start.5 = (bf16[512,1024]{1,0:T(8,128)(2,1)S(1)}, bf16[512,1024]{1,0:T(8,128)(2,1)}, u32[]{:S(2)}) copy-start(bf16[512,1024]{1,0:T(8,128)(2,1)} %choose.4) | copy-start | bytes 3145732
  140.7 24.7 %collective-permute-start.15 = (bf16[512,1024]{1,0:T(8,128)(2,1)}, bf16[512,1024]{1,0:T(8,128)(2,1)S(1)}, u32[]{:S(2)}, u32[]{:S(2)}) collective-permute-start(bf16[512,1024]{1,0:T(8,128)(2,1)} %choose.5), channel_id=1, source_target_pairs={{0,2},{2,0},{1,3},{3,1},{4,6},{6,4},{5,7},{7,5},{8,10},{10,8},{9,1... | collective-permute-start | bytes 3145736 | tf_op jit(solution)/shard_map/ppermute | solution.py:409
  145.1 24.7 %collective-permute-start.12 = (bf16[2,512,1024]{2,1,0:T(8,128)(2,1)}, bf16[2,512,1024]{2,1,0:T(8,128)(2,1)}, u32[]{:S(2)}, u32[]{:S(2)}) collective-permute-start(bf16[2,512,1024]{2,1,0:T(8,128)(2,1)} %pad_maximum_fusion.2.refs_13_), channel_id=1, source_target_pairs={{0,1},{1,0},{2,3},{3,2},{4,5},{5,4},{6,7},{7,6},{8,9},{9,8},{10,11... | collective-permute-start | bytes 6291464 | tf_op jit(solution)/shard_map/ppermute | solution.py:416
  145.1 21.3 %copy-start.7 = (bf16[4,512,256]{2,1,0:T(8,128)(2,1)}, bf16[4,512,256]{2,1,0:T(8,128)(2,1)S(1)}, u32[]{:S(2)}) copy-start(bf16[4,512,256]{2,1,0:T(8,128)(2,1)S(1)} %all-to-all-done.2.refs_6_) | copy-start | bytes 3145732
  145.1 21.7 %copy-start.11 = (f32[256,16]{0,1:T(8,128)S(1)}, f32[256,16]{0,1:T(8,128)}, u32[]{:S(2)}) copy-start(f32[256,16]{0,1:T(8,128)} %param.11) | copy-start | bytes 49156
  145.2 21.8 %copy-start.15 = (f32[256,16]{0,1:T(8,128)S(1)}, f32[256,16]{0,1:T(8,128)}, u32[]{:S(2)}) copy-start(f32[256,16]{0,1:T(8,128)} %param.12) | copy-start | bytes 49156
  145.2 21.8 %copy-start.16 = (f32[256,16]{0,1:T(8,128)S(1)}, f32[256,16]{0,1:T(8,128)}, u32[]{:S(2)}) copy-start(f32[256,16]{0,1:T(8,128)} %param.13) | copy-start | bytes 49156
  145.3 20.1 %collective-permute-start.2 = (bf16[3,512,256]{2,1,0:T(8,128)(2,1)S(1)}, bf16[3,512,256]{2,1,0:T(8,128)(2,1)}, u32[]{:S(2)}, u32[]{:S(2)}) collective-permute-start(bf16[3,512,256]{2,1,0:T(8,128)(2,1)S(1)} %pad_maximum_fusion.8), channel_id=1, source_target_pairs={{0,16},{16,0},{1,17},{17,1},{2,18},{18,2},{3,19},{19,3},{4,20},{20... | collective-permute-start | bytes 2359304 | tf_op jit(solution)/shard_map/ppermute | solution.py:189
  165.4 3.0 %collective-permute-start.16 = (bf16[1,512,1024]{2,1,0:T(8,128)(2,1)}, bf16[1,512,1024]{2,1,0:T(8,128)(2,1)}, u32[]{:S(2)}, u32[]{:S(2)}) collective-permute-start(bf16[1,512,1024]{2,1,0:T(8,128)(2,1)} %bitcast.71), channel_id=1, source_target_pairs={{0,1},{1,0},{2,3},{3,2},{4,5},{5,4},{6,7},{7,6},{8,9},{9,8},{10,11... | collective-permute-start | bytes 3145736 | tf_op jit(solution)/shard_map/ppermute | solution.py:416
  166.4 3.4 %collective-permute-start.17 = (bf16[1,512,1024]{2,1,0:T(8,128)(2,1)}, bf16[1,512,1024]{2,1,0:T(8,128)(2,1)S(1)}, u32[]{:S(2)}, u32[]{:S(2)}) collective-permute-start(bf16[1,512,1024]{2,1,0:T(8,128)(2,1)} %bitcast.67), channel_id=1, source_target_pairs={{0,1},{1,0},{2,3},{3,2},{4,5},{5,4},{6,7},{7,6},{8,9},{9,8},{10,11... | collective-permute-start | bytes 3145736 | tf_op jit(solution)/shard_map/ppermute | solution.py:416
  205.2 13.2 %collective-permute-start.18 = (bf16[512,256]{1,0:T(8,128)(2,1)}, bf16[512,256]{1,0:T(8,128)(2,1)S(1)}, u32[]{:S(2)}, u32[]{:S(2)}) collective-permute-start(bf16[512,256]{1,0:T(8,128)(2,1)} %get-tuple-element.8), channel_id=1, source_target_pairs={{0,4},{4,0},{8,12},{12,8},{1,5},{5,1},{9,13},{13,9},{2,6},{6,2},{1... | collective-permute-start | bytes 786440 | tf_op jit(solution)/shard_map/ppermute | solution.py:440
  205.5 21.6 %collective-permute-start.19 = (bf16[512,256]{1,0:T(8,128)(2,1)}, bf16[512,256]{1,0:T(8,128)(2,1)S(1)}, u32[]{:S(2)}, u32[]{:S(2)}) collective-permute-start(bf16[512,256]{1,0:T(8,128)(2,1)} %get-tuple-element.9), channel_id=1, source_target_pairs={{0,8},{4,12},{8,0},{12,4},{1,9},{5,13},{9,1},{13,5},{2,10},{6,14},... | collective-permute-start | bytes 786440 | tf_op jit(solution)/shard_map/ppermute | solution.py:440
  207.4 19.6 %collective-permute-start.20 = (bf16[512,256]{1,0:T(8,128)(2,1)}, bf16[512,256]{1,0:T(8,128)(2,1)S(1)}, u32[]{:S(2)}, u32[]{:S(2)}) collective-permute-start(bf16[512,256]{1,0:T(8,128)(2,1)} %get-tuple-element.10), channel_id=1, source_target_pairs={{0,12},{4,8},{8,4},{12,0},{1,13},{5,9},{9,5},{13,1},{2,14},{6,10},... | collective-permute-start | bytes 786440 | tf_op jit(solution)/shard_map/ppermute | solution.py:440
  218.3 8.7 %copy-start.12 = (bf16[512,256]{1,0:T(8,128)(2,1)}, bf16[512,256]{1,0:T(8,128)(2,1)S(1)}, u32[]{:S(2)}) copy-start(bf16[512,256]{1,0:T(8,128)(2,1)S(1)} %collective-permute-done.18.refs_1_) | copy-start | bytes 786436
  (11 other events, 18.9 us)

commit v5 on v4

--- a/solution.py
+++ b/solution.py
@@ -224,6 +224,57 @@
     ]
 
 
+def product_rows(x_buf, pair_buf, channels):
+    acc = jnp.dot(x_buf[...], pair_buf[...], preferred_element_type=jnp.float32)
+    rounded = acc.astype(jnp.bfloat16).astype(jnp.float32)
+    return (rounded[:, :channels] * rounded[:, channels:]).astype(jnp.bfloat16)
+
+
+def product_kernel(n_weights, each, order_ref, *refs):
+    pair_hbm, x_hbm, (out_ref, x_buf, pair_buf, x_sem, pair_sem) = refs[:n_weights], refs[n_weights:-5], refs[-5:]
+    count, rows, channels = out_ref.shape
+    x_copies = [
+        token_copies(x_hbm[i * each : (i + 1) * each], x_buf.at[i], x_sem.at[i]) for i in range(count)
+    ]
+    pair_copies = weight_copies(order_ref, pair_hbm, pair_buf, pair_sem)
+    for copy in pair_copies + sum(x_copies[:2], []):
+        copy.start()
+    for copy in pair_copies:
+        copy.wait()
+    for i in range(count):
+        for copy in x_copies[i]:
+            copy.wait()
+        for copy in x_copies[i + 2] if i + 2 < count else ():
+            copy.start()
+        out_ref[i] = product_rows(x_buf.at[i], pair_buf, channels)
+
+
+def early_products(order, xs, pair):
+    quarters, share, width = pair[0].shape
+    rows, depth = xs[0][0].shape[1:]
+    anywhere = pl.BlockSpec(memory_space=pl.ANY)
+    arrays = [*pair, *sum(xs, [])]
+    return pl.pallas_call(
+        functools.partial(product_kernel, len(pair), len(xs[0])),
+        out_shape=jax.ShapeDtypeStruct((len(xs), rows, width), jnp.bfloat16),
+        in_specs=[pl.BlockSpec(memory_space=pltpu.SMEM)] + [anywhere] * len(arrays),
+        out_specs=pl.BlockSpec(memory_space=pltpu.VMEM),
+        scratch_shapes=[
+            pltpu.VMEM((len(xs), rows, quarters * depth), jnp.bfloat16),
+            pltpu.VMEM((quarters * depth, 2 * width), jnp.bfloat16),
+            pltpu.SemaphoreType.DMA((len(xs), quarters)),
+            pltpu.SemaphoreType.DMA((len(pair) + 2 >> 1, quarters)),
+        ],
+        compiler_params=pltpu.CompilerParams(vmem_limit_bytes=KERNEL_BYTES),
+        cost_estimate=pl.CostEstimate(
+            flops=len(xs) * rows * quarters * depth * width // 4,
+            bytes_accessed=depth * rows,
+            transcendentals=0,
+        ),
+        name="early_products",
+    )(order, *arrays)
+
+
 def modes_over_time(modes_ref, prod, out, ends, conv_ref, state_ref):
     groups, length, lane_width = prod.shape
     modes = modes_ref.shape[1]
@@ -275,6 +326,7 @@
         del refs[:count]
         return taken
 
+    (early_ref,) = take(1)
     pair_hbm, query_hbm = take(2 * n_weights), take(n_weights)
     x_hbm = [take(count) for count in counts]
     outs, (state_ref,) = take(seq), take(1)
@@ -283,26 +335,27 @@
     channels = conv_buf.shape[1]
     groups = prod.shape[0]
     first = 2 * pair_sem.shape[1] + (n_weights + 1) // 2
+    last = seq - 1
     x_copies = [token_copies(x_hbm[i], x_buf.at[i], x_sem.at[i]) for i in range(seq)]
     pair_copies = weight_copies(order_ref, pair_hbm, pair_buf, pair_sem)
     query_copies = weight_copies(order_ref, query_hbm, query_buf, query_sem)
-    for copy in pair_copies + x_copies[0] + x_copies[1]:
+    for copy in pair_copies + x_copies[last]:
         copy.start()
-    for copy in pair_copies:
-        copy.wait()
-    for i in range(seq):
-        for copy in x_copies[i]:
-            copy.wait()
-        for copy in x_copies[i + 2] if i + 2 < seq else query_copies if i + 2 == seq else ():
-            copy.start()
-        acc = jnp.dot(x_buf[i], pair_buf[...], preferred_element_type=jnp.float32)
-        rounded = acc.astype(jnp.bfloat16).astype(jnp.float32)
-        product = (rounded[:, :channels] * rounded[:, channels:]).astype(jnp.bfloat16)
+
+    def put(i, product):
         to = pl.ds(pl.multiple_of(order_ref[first + i] * rows, rows), rows)
         for g in range(groups):
             prod[g, to, :] = product[:, g * LANES : (g + 1) * LANES].astype(jnp.float32)
+
+    for i in range(last):
+        put(i, early_ref[i])
+    for copy in pair_copies + x_copies[last]:
+        copy.wait()
+    for copy in query_copies + sum(x_copies[:last], []):
+        copy.start()
+    put(last, product_rows(x_buf.at[last], pair_buf, channels))
     modes_over_time(modes_ref, prod, out, ends, conv_buf, state_ref)
-    for copy in query_copies:
+    for copy in query_copies + sum(x_copies[:last], []):
         copy.wait()
     for i in range(seq):
         shard = order_ref[first + i]
@@ -317,7 +370,7 @@
                 outs[step][...] = gated
 
 
-def finish(order, xs, pair, query, decay_rate, residue, carried):
+def finish(order, early, xs, pair, query, decay_rate, residue, carried):
     quarters, share, width = query[0].shape
     seq = len(xs)
     rows, depth = xs[0][0].shape[1:]
@@ -338,7 +391,7 @@
         functools.partial(finish_kernel, len(query), [len(x) for x in xs]),
         out_shape=tuple(jax.ShapeDtypeStruct((rows, width), jnp.bfloat16) for _ in range(seq))
         + (jax.ShapeDtypeStruct((modes, width), jnp.float32),),
-        in_specs=[pl.BlockSpec(memory_space=pltpu.SMEM), vmem]
+        in_specs=[pl.BlockSpec(memory_space=pltpu.SMEM), vmem, vmem]
         + [anywhere] * len(arrays),
         out_specs=(vmem,) * (seq + 1),
         scratch_shapes=[
@@ -360,7 +413,7 @@
             transcendentals=0,
         ),
         name="finish",
-    )(order, table, *arrays)
+    )(order, table, early, *arrays)
     return gated, state.T
 
 
@@ -409,7 +462,8 @@
             last = lax.ppermute(arrival, "chan", ring(chan, turn))
             group.append(last)
         if phase == seq:
-            group[-1] = after(group[-1], w_queries[-1])
+            early = early_products(by_feature, xs, w_keys + w_values)
+            group[-1] = after(group[-1], early, w_queries[-1])
             group = [x[None] for x in group]
         else:
             group = [jnp.stack(group)]
@@ -435,7 +489,7 @@
     steps = [place ^ origin for origin in origins]
     order = jnp.concatenate([by_feature, jnp.stack([jnp.int32(i) for i in origins + steps])])
 
-    gated, new_state = finish(order, xs, w_keys + w_values, w_queries, decay_rate, residue, carried)
+    gated, new_state = finish(order, early, xs, w_keys + w_values, w_queries, decay_rate, residue, carried)
     pieces = [
         lax.ppermute(gated[step], "seq", mirror(seq, step)) if step else gated[0] for step in range(seq)
     ]

time: 233 us -> 228 us (0.979)
  waiting for transfers between devices: 108 us -> 99.2 us
  Pallas kernels: 45.7 us -> 51.2 us
    all_to_all x3, waiting for transfers between devices: 15.3 us -> 32.2 us  [exchange_weights(): mine = lax.all_to_all(mine, 'seq', split_axis=0, concat_axis=0, tiled=True)]
    ppermute x3, waiting for transfers between devices: 17.9 us -> 1.72 us  [exchange_weights(): shares += [own, lax.ppermute(fetched, 'parts', ring(parts, turn))]]
    pallas_call x0 -> x1, Pallas kernels: none -> 12.8 us  [early_products(): pl.pallas_call(functools.partial(product_kernel, len(pair), len(xs[0])),...]
    ppermute x3, waiting for transfers between devices: 54.5 us -> 45.3 us  [by_channels(): ways[1][phase] = lax.ppermute(ways[1][phase - 1], 'seq', downs)]
    pallas_call x1, Pallas kernels: 34.4 us -> 27.1 us  [finish(): pl.pallas_call(functools.partial(finish_kernel, len(query), [len(x) for x...]
  transfers between devices with their start and end apart: 24 -> 24, of which waited for: 9 -> 9; matrix products, arithmetic and copies ran while one was open for 7% -> 8% of each run, Pallas kernels for 4% -> 8%
where the time goes in v5:
time: 228 us; the launch traced here: 225 us
  waiting for transfers between devices  99.2 us (44%)
  Pallas kernels  51.2 us (22%)
  starting transfers between devices  48.9 us (21%)
  other arithmetic  12.7 us (6%)
  local copies, waits for them, and re-layouts  11.9 us (5%)
    ppermute x3, waiting for transfers between devices, by_channels(): ways[1][phase] = lax.ppermute(ways[1][phase - 1], 'seq', downs)  45.3 us
    all_to_all x3, waiting for transfers between devices, exchange_weights(): mine = lax.all_to_all(mine, 'seq', split_axis=0, concat_axis=0, tiled=True)  32.2 us
    pallas_call x1, Pallas kernels, finish(): pl.pallas_call(functools.partial(finish_kernel, len(query), [len(x) for x...  27.1 us
    all_to_all x3, starting transfers between devices, exchange_weights(): mine = lax.all_to_all(mine, 'seq', split_axis=0, concat_axis=0, tiled=True)  21.6 us
    ppermute x3, waiting for transfers between devices, by_channels(): lax.ppermute(gated[step], 'seq', mirror(seq, step))  17.2 us
    pallas_call x1, Pallas kernels, early_products(): pl.pallas_call(functools.partial(product_kernel, len(pair), len(xs[0])),...  12.8 us
    pallas_call x3, Pallas kernels, choose(): pl.pallas_call(kernel, out_shape=jax.ShapeDtypeStruct(shape.shape, shape....  8.99 us
    ppermute x3, starting transfers between devices, by_channels(): ways[0][phase] = lax.ppermute(ways[0][phase - 1], 'seq', ups)  8.88 us
  transfers between devices with their start and end apart: 24, of which 9 were waited for; matrix products, arithmetic and copies ran while one was open for 8% of the time, Pallas kernels for 8%

profile of v5, /device:TPU:0, one launch (start us, length us, event | category | flops | bytes accessed | tf_op | source)
XLA Modules:
  0.0 224.8 jit_solution(16430238288466168469)
XLA Ops:
  0.7 2.1 fusion.2
  3.8 6.3 %all-to-all-start = ((bf16[4,512,256]{2,1,0:T(8,128)(2,1)}), bf16[4,512,256]{2,1,0:T(8,128)(2,1)S(1)}, u32[]{:S(2)}, u32[]{:S(2)}) async-start(bf16[4,512,256]{2,1,0:T(8,128)(2,1)} %pad_maximum_fusion.3), calls=%async_computation | async-start | bytes 2097152 | tf_op jit(solution)/shard_map/all_to_all | solution.py:181
  11.4 5.5 %collective-permute-start.4 = (bf16[512,1024]{1,0:T(8,128)(2,1)}, bf16[512,1024]{1,0:T(8,128)(2,1)}, u32[]{:S(2)}, u32[]{:S(2)}) collective-permute-start(bf16[512,1024]{1,0:T(8,128)(2,1)} %param.7), channel_id=1, source_target_pairs={{0,4},{4,8},{8,12},{1,5},{5,9},{9,13},{2,6},{6,10},{10,14},{3,7},{... | collective-permute-start | bytes 3145736 | tf_op jit(solution)/shard_map/ppermute | solution.py:476
  18.5 2.1 fusion.1
  21.7 15.3 %all-to-all-done.refs_3_.refs_0_.refs_1_ = bf16[4,512,256]{2,1,0:T(8,128)(2,1)S(1)} async-done(((bf16[4,512,256]{2,1,0:T(8,128)(2,1)}), bf16[4,512,256]{2,1,0:T(8,128)(2,1)S(1)}, u32[]{:S(2)}, u32[]{:S(2)}) %all-to-all-start) | async-done | bytes 1048608 | tf_op jit(solution)/shard_map/all_to_all | solution.py:181
  37.0 3.5 %all-to-all-start.1 = ((bf16[4,512,256]{2,1,0:T(8,128)(2,1)}), bf16[4,512,256]{2,1,0:T(8,128)(2,1)S(1)}, u32[]{:S(2)}, u32[]{:S(2)}) async-start(bf16[4,512,256]{2,1,0:T(8,128)(2,1)} %pad_maximum_fusion.4), calls=%async_computation.1 | async-start | bytes 2097152 | tf_op jit(solution)/shard_map/all_to_all | solution.py:181
  40.5 13.8 %collective-permute-done.5.refs_1_ = bf16[512,1024]{1,0:T(8,128)(2,1)S(1)} collective-permute-done((bf16[512,1024]{1,0:T(8,128)(2,1)}, bf16[512,1024]{1,0:T(8,128)(2,1)S(1)}, u32[]{:S(2)}, u32[]{:S(2)}) %collective-permute-start.5) | collective-permute-done | bytes 1048608 | tf_op jit(solution)/shard_map/ppermute | solution.py:477
  55.6 1.7 collective-permute-start.8
  57.3 2.6 %choose.3 = bf16[512,1024]{1,0:T(8,128)(2,1)} custom-call(s32[1]{0:T(128)} %bitcast.33.index_ref, bf16[512,1024]{1,0:T(8,128)(2,1)} %collective-permute-done.4.refs_0_, bf16[512,1024]{1,0:T(8,128)(2,1)} %copy-done.3, bf16[512,1024]{1,0:T(8,128)(2,1)} %collective-permute-done.2.refs_2_, bf16[4,512,256]{2,1,0:T(8,128)(2,1)} %copy-done.1), custom_call_target="tpu_custom_call" | custom-call | bytes 1048576 | tf_op jit(solution)/shard_map/choose/pallas_call | solution.py:133
  63.6 1.5 collective-permute-start
  65.1 16.9 %all-to-all-done.1.refs_5_.refs_3_.refs_4_ = bf16[4,512,256]{2,1,0:T(8,128)(2,1)S(1)} async-done(((bf16[4,512,256]{2,1,0:T(8,128)(2,1)}), bf16[4,512,256]{2,1,0:T(8,128)(2,1)S(1)}, u32[]{:S(2)}, u32[]{:S(2)}) %all-to-all-start.1) | async-done | bytes 1048608 | tf_op jit(solution)/shard_map/all_to_all | solution.py:181
  82.0 12.6 %collective-permute-done.9.refs_2_ = bf16[512,1024]{1,0:T(8,128)(2,1)} collective-permute-done((bf16[512,1024]{1,0:T(8,128)(2,1)S(1)}, bf16[512,1024]{1,0:T(8,128)(2,1)}, u32[]{:S(2)}, u32[]{:S(2)}) %collective-permute-start.9) | collective-permute-done | bytes 1048608 | tf_op jit(solution)/shard_map/ppermute | solution.py:477
  95.6 2.9 %choose.4 = bf16[512,1024]{1,0:T(8,128)(2,1)} custom-call(s32[1]{0:T(128)} %bitcast.36.index_ref, bf16[512,1024]{1,0:T(8,128)(2,1)} %collective-permute-done.8.refs_0_, bf16[512,1024]{1,0:T(8,128)(2,1)} %copy-done.3, bf16[512,1024]{1,0:T(8,128)(2,1)} %collective-permute-done.9.refs_2_, bf16[512,1024]{1,0:T(8,128)(2,1)} %copy-done.4, ...), custom_call_target="tpu_custom_call" | custom-call | bytes 1048576 | tf_op jit(solution)/shard_map/choose/pallas_call | solution.py:133
  98.5 1.5 collective-permute-start.10
  101.3 1.6 collective-permute-start.13
  105.1 1.5 collective-permute-start.1
  108.5 11.7 %all-to-all-start.2 = ((bf16[4,512,256]{2,1,0:T(8,128)(2,1)}), bf16[4,512,256]{2,1,0:T(8,128)(2,1)S(1)}, u32[]{:S(2)}, u32[]{:S(2)}) async-start(bf16[4,512,256]{2,1,0:T(8,128)(2,1)} %pad_maximum_fusion.5), calls=%async_computation.2 | async-start | bytes 2097152 | tf_op jit(solution)/shard_map/all_to_all | solution.py:181
  120.3 1.9 pad_maximum_fusion.refs_6_.refs_10_
  122.4 1.5 pad_maximum_fusion.1.refs_8_.refs_12_
  124.4 2.8 %pad_maximum_fusion.2.refs_10_.refs_14_ = bf16[2,512,1024]{2,1,0:T(8,128)(2,1)} fusion(bf16[1,512,1024]{2,1,0:T(8,128)(2,1)} %bitcast.38, bf16[1,512,1024]{2,1,0:T(8,128)(2,1)S(1)} %bitcast.65), kind=kLoop, calls=%fused_computation.2 | loop fusion | flops 1048576 | bytes 4194304 | tf_op jit(solution)/shard_map/stack | solution.py:469
  127.4 18.9 %collective-permute-done.14.refs_3_ = bf16[512,1024]{1,0:T(8,128)(2,1)} collective-permute-done((bf16[512,1024]{1,0:T(8,128)(2,1)}, bf16[512,1024]{1,0:T(8,128)(2,1)}, u32[]{:S(2)}, u32[]{:S(2)}) %collective-permute-start.14) | collective-permute-done | bytes 1048608 | tf_op jit(solution)/shard_map/ppermute | solution.py:477
  146.4 3.4 %choose.5 = bf16[512,1024]{1,0:T(8,128)(2,1)} custom-call(s32[1]{0:T(128)} %bitcast.43.index_ref, bf16[512,1024]{1,0:T(8,128)(2,1)} %collective-permute-done.8.refs_0_, bf16[512,1024]{1,0:T(8,128)(2,1)} %collective-permute-done.13.refs_1_, bf16[512,1024]{1,0:T(8,128)(2,1)} %collective-permute-done.9.refs_2_, ...), custom_call_target="tpu_custom_call" | custom-call | flops 23000000512 | bytes 1048576 | tf_op jit(solution)/shard_map/choose/pallas_call | solution.py:133
  151.6 1.5 collective-permute-start.12
  154.4 12.8 %early_products.1.refs_1_.refs_0_ = bf16[3,512,256]{2,1,0:T(8,128)(2,1)} custom-call(s32[10]{0:T(128)} %stack.164.order_ref, bf16[4,512,256]{2,1,0:T(8,128)(2,1)} %copy-done.1, bf16[512,256]{1,0:T(8,128)(2,1)} %get-tuple-element.22.refs_1_.refs_2_, bf16[3,512,256]{2,1,0:T(8,128)(2,1)} %collective-permute-done.refs_4_.refs_2_.refs_3_, ...), custom_call_target="tpu_custom_call" | custom-call | flops 402653184 | bytes 524288 | tf_op jit(solution)/shard_map/early_products/pallas_call | solution.py:257
  167.3 1.7 collective-permute-done.12.refs_2_.refs_9_
  169.2 2.7 %collective-permute-done.17.refs_19_ = bf16[1,512,1024]{2,1,0:T(8,128)(2,1)S(1)} collective-permute-done((bf16[1,512,1024]{2,1,0:T(8,128)(2,1)}, bf16[1,512,1024]{2,1,0:T(8,128)(2,1)S(1)}, u32[]{:S(2)}, u32[]{:S(2)}) %collective-permute-start.17) | collective-permute-done | bytes 1048608 | tf_op jit(solution)/shard_map/ppermute | solution.py:470
  172.8 27.1 %finish.1 = (bf16[512,256]{1,0:T(8,128)(2,1)}, bf16[512,256]{1,0:T(8,128)(2,1)}, bf16[512,256]{1,0:T(8,128)(2,1)}, bf16[512,256]{1,0:T(8,128)(2,1)}, f32[16,256]{1,0:T(8,128)}) custom-call(s32[18]{0:T(128)} %concatenate.13.order_ref, f32[5,16,256]{2,1,0:T(8,128)} %bitcast.67, bf16[3,512,256]{2,1,0:T(8,128)(2,1)} %early_products.1.refs_1_.refs_0_, ...), custom_call_target="tpu_custom_call" | custom-call | flops 8589934592 | bytes 23068672 | tf_op jit(solution)/shard_map/finish/pallas_call | solution.py:390
  200.1 2.8 %collective-permute-start.19 = (bf16[512,256]{1,0:T(8,128)(2,1)}, bf16[512,256]{1,0:T(8,128)(2,1)S(1)}, u32[]{:S(2)}, u32[]{:S(2)}) collective-permute-start(bf16[512,256]{1,0:T(8,128)(2,1)} %get-tuple-element.9), channel_id=1, source_target_pairs={{0,8},{4,12},{8,0},{12,4},{1,9},{5,13},{9,1},{13,5},{2,10},{6,14},... | collective-permute-start | bytes 786440 | tf_op jit(solution)/shard_map/ppermute | solution.py:494
  202.9 1.5 collective-permute-start.20
  204.4 9.2 %collective-permute-done.18.refs_1_ = bf16[512,256]{1,0:T(8,128)(2,1)S(1)} collective-permute-done((bf16[512,256]{1,0:T(8,128)(2,1)}, bf16[512,256]{1,0:T(8,128)(2,1)S(1)}, u32[]{:S(2)}, u32[]{:S(2)}) %collective-permute-start.18) | collective-permute-done | bytes 262176 | tf_op jit(solution)/shard_map/ppermute | solution.py:494
  213.6 8.0 %collective-permute-done.19.refs_2_ = bf16[512,256]{1,0:T(8,128)(2,1)S(1)} collective-permute-done((bf16[512,256]{1,0:T(8,128)(2,1)}, bf16[512,256]{1,0:T(8,128)(2,1)S(1)}, u32[]{:S(2)}, u32[]{:S(2)}) %collective-permute-start.19) | collective-permute-done | bytes 262176 | tf_op jit(solution)/shard_map/ppermute | solution.py:494
  222.5 2.3 %place_columns.1 = bf16[512,1024]{1,0:T(8,128)(2,1)} custom-call(s32[1]{0:T(128)} %bitcast.place_ref, bf16[512,256]{1,0:T(8,128)(2,1)} %get-tuple-element.7.refs_0_, bf16[512,256]{1,0:T(8,128)(2,1)} %copy-done.11, bf16[512,256]{1,0:T(8,128)(2,1)} %copy-done.12, bf16[512,256]{1,0:T(8,128)(2,1)} %copy-done.13), custom_call_target="tpu_custom_call" | custom-call | tf_op jit(solution)/shard_map/place_columns/pallas_call | solution.py:430
  (83 shorter events, 22.2 us)
Async XLA Ops:
  3.8 33.1 %all-to-all-start = ((bf16[4,512,256]{2,1,0:T(8,128)(2,1)}), bf16[4,512,256]{2,1,0:T(8,128)(2,1)S(1)}, u32[]{:S(2)}, u32[]{:S(2)}) async-start(bf16[4,512,256]{2,1,0:T(8,128)(2,1)} %pad_maximum_fusion.3), calls=%async_computation | async-start | bytes 2097152 | tf_op jit(solution)/shard_map/all_to_all | solution.py:181
  10.2 44.1 %collective-permute-start.5 = (bf16[512,1024]{1,0:T(8,128)(2,1)}, bf16[512,1024]{1,0:T(8,128)(2,1)S(1)}, u32[]{:S(2)}, u32[]{:S(2)}) collective-permute-start(bf16[512,1024]{1,0:T(8,128)(2,1)} %param.7), channel_id=1, source_target_pairs={{4,0},{8,4},{12,8},{5,1},{9,5},{13,9},{6,2},{10,6},{14,10},{7,3},{... | collective-permute-start | bytes 3145736 | tf_op jit(solution)/shard_map/ppermute | solution.py:477
  11.4 44.1 %collective-permute-start.4 = (bf16[512,1024]{1,0:T(8,128)(2,1)}, bf16[512,1024]{1,0:T(8,128)(2,1)}, u32[]{:S(2)}, u32[]{:S(2)}) collective-permute-start(bf16[512,1024]{1,0:T(8,128)(2,1)} %param.7), channel_id=1, source_target_pairs={{0,4},{4,8},{8,12},{1,5},{5,9},{9,13},{2,6},{6,10},{10,14},{3,7},{... | collective-permute-start | bytes 3145736 | tf_op jit(solution)/shard_map/ppermute | solution.py:476
  17.0 40.3 %collective-permute-start.2 = (bf16[512,1024]{1,0:T(8,128)(2,1)}, bf16[512,1024]{1,0:T(8,128)(2,1)}, u32[]{:S(2)}, u32[]{:S(2)}) collective-permute-start(bf16[512,1024]{1,0:T(8,128)(2,1)} %param.7), channel_id=1, source_target_pairs={{0,2},{2,0},{1,3},{3,1},{4,6},{6,4},{5,7},{7,5},{8,10},{10,8},{9,1... | collective-permute-start | bytes 3145736 | tf_op jit(solution)/shard_map/ppermute | solution.py:462
  37.0 20.3 %copy-start.1 = (bf16[4,512,256]{2,1,0:T(8,128)(2,1)}, bf16[4,512,256]{2,1,0:T(8,128)(2,1)S(1)}, u32[]{:S(2)}) copy-start(bf16[4,512,256]{2,1,0:T(8,128)(2,1)S(1)} %all-to-all-done.refs_3_.refs_0_.refs_1_) | copy-start | bytes 3145732
  37.0 45.0 %all-to-all-start.1 = ((bf16[4,512,256]{2,1,0:T(8,128)(2,1)}), bf16[4,512,256]{2,1,0:T(8,128)(2,1)S(1)}, u32[]{:S(2)}, u32[]{:S(2)}) async-start(bf16[4,512,256]{2,1,0:T(8,128)(2,1)} %pad_maximum_fusion.4), calls=%async_computation.1 | async-start | bytes 2097152 | tf_op jit(solution)/shard_map/all_to_all | solution.py:181
  54.3 3.0 %copy-start.3 = (bf16[512,1024]{1,0:T(8,128)(2,1)}, bf16[512,1024]{1,0:T(8,128)(2,1)S(1)}, u32[]{:S(2)}) copy-start(bf16[512,1024]{1,0:T(8,128)(2,1)S(1)} %collective-permute-done.5.refs_1_) | copy-start | bytes 3145732
  54.3 40.3 %collective-permute-start.9 = (bf16[512,1024]{1,0:T(8,128)(2,1)S(1)}, bf16[512,1024]{1,0:T(8,128)(2,1)}, u32[]{:S(2)}, u32[]{:S(2)}) collective-permute-start(bf16[512,1024]{1,0:T(8,128)(2,1)S(1)} %collective-permute-done.5.refs_1_), channel_id=1, source_target_pairs={{4,0},{8,4},{5,1},{9,5},{6,2},{10,6},{7,3},{11,7},{20,16},{24,20},... | collective-permute-start | bytes 3145736 | tf_op jit(solution)/shard_map/ppermute | solution.py:477
  55.6 39.0 %collective-permute-start.8 = (bf16[512,1024]{1,0:T(8,128)(2,1)}, bf16[512,1024]{1,0:T(8,128)(2,1)}, u32[]{:S(2)}, u32[]{:S(2)}) collective-permute-start(bf16[512,1024]{1,0:T(8,128)(2,1)} %collective-permute-done.4.refs_0_), channel_id=1, source_target_pairs={{4,8},{8,12},{5,9},{9,13},{6,10},{10,14},{7,11},{11,15},{20,24},{2... | collective-permute-start | bytes 3145736 | tf_op jit(solution)/shard_map/ppermute | solution.py:476
  60.0 34.6 %collective-permute-start.6 = (bf16[512,1024]{1,0:T(8,128)(2,1)}, bf16[512,1024]{1,0:T(8,128)(2,1)S(1)}, u32[]{:S(2)}, u32[]{:S(2)}) collective-permute-start(bf16[512,1024]{1,0:T(8,128)(2,1)} %choose.3), channel_id=1, source_target_pairs={{0,2},{2,0},{1,3},{3,1},{4,6},{6,4},{5,7},{7,5},{8,10},{10,8},{9,1... | collective-permute-start | bytes 3145736 | tf_op jit(solution)/shard_map/ppermute | solution.py:462
  63.6 31.0 %collective-permute-start = (bf16[3,512,256]{2,1,0:T(8,128)(2,1)}, bf16[3,512,256]{2,1,0:T(8,128)(2,1)}, u32[]{:S(2)}, u32[]{:S(2)}) collective-permute-start(bf16[3,512,256]{2,1,0:T(8,128)(2,1)} %pad_maximum_fusion.6), channel_id=1, source_target_pairs={{0,16},{16,0},{1,17},{17,1},{2,18},{18,2},{3,19},{19,3},{4,20},{20... | collective-permute-start | bytes 2359304 | tf_op jit(solution)/shard_map/ppermute | solution.py:189
  82.0 12.6 %copy-start = (bf16[4,512,256]{2,1,0:T(8,128)(2,1)}, bf16[4,512,256]{2,1,0:T(8,128)(2,1)S(1)}, u32[]{:S(2)}) copy-start(bf16[4,512,256]{2,1,0:T(8,128)(2,1)S(1)} %all-to-all-done.1.refs_5_.refs_3_.refs_4_) | copy-start | bytes 3145732
  98.5 8.1 %copy-start.9 = (bf16[1024,1024]{1,0:T(8,128)(2,1)S(1)}, bf16[1024,1024]{1,0:T(8,128)(2,1)}, u32[]{:S(2)}) copy-start(bf16[1024,1024]{1,0:T(8,128)(2,1)} %param.8) | copy-start | bytes 6291460
  98.5 25.6 %collective-permute-start.10 = (bf16[512,1024]{1,0:T(8,128)(2,1)}, bf16[512,1024]{1,0:T(8,128)(2,1)}, u32[]{:S(2)}, u32[]{:S(2)}) collective-permute-start(bf16[512,1024]{1,0:T(8,128)(2,1)} %choose.4), channel_id=1, source_target_pairs={{0,2},{2,0},{1,3},{3,1},{4,6},{6,4},{5,7},{7,5},{8,10},{10,8},{9,1... | collective-permute-start | bytes 3145736 | tf_op jit(solution)/shard_map/ppermute | solution.py:462
  100.0 46.4 %collective-permute-start.14 = (bf16[512,1024]{1,0:T(8,128)(2,1)}, bf16[512,1024]{1,0:T(8,128)(2,1)}, u32[]{:S(2)}, u32[]{:S(2)}) collective-permute-start(bf16[512,1024]{1,0:T(8,128)(2,1)} %collective-permute-done.9.refs_2_), channel_id=1, source_target_pairs={{4,0},{5,1},{6,2},{7,3},{20,16},{21,17},{22,18},{23,19}} | collective-permute-start | bytes 3145736 | tf_op jit(solution)/shard_map/ppermute | solution.py:477
  101.3 45.1 %collective-permute-start.13 = (bf16[512,1024]{1,0:T(8,128)(2,1)}, bf16[512,1024]{1,0:T(8,128)(2,1)}, u32[]{:S(2)}, u32[]{:S(2)}) collective-permute-start(bf16[512,1024]{1,0:T(8,128)(2,1)} %collective-permute-done.8.refs_0_), channel_id=1, source_target_pairs={{8,12},{9,13},{10,14},{11,15},{24,28},{25,29},{26,30},{27,31}} | collective-permute-start | bytes 3145736 | tf_op jit(solution)/shard_map/ppermute | solution.py:476
  105.1 22.1 %collective-permute-start.1 = (bf16[3,512,256]{2,1,0:T(8,128)(2,1)}, bf16[3,512,256]{2,1,0:T(8,128)(2,1)}, u32[]{:S(2)}, u32[]{:S(2)}) collective-permute-start(bf16[3,512,256]{2,1,0:T(8,128)(2,1)} %pad_maximum_fusion.7), channel_id=1, source_target_pairs={{0,16},{16,0},{1,17},{17,1},{2,18},{18,2},{3,19},{19,3},{4,20},{20... | collective-permute-start | bytes 2359304 | tf_op jit(solution)/shard_map/ppermute | solution.py:189
  108.5 41.9 %all-to-all-start.2 = ((bf16[4,512,256]{2,1,0:T(8,128)(2,1)}), bf16[4,512,256]{2,1,0:T(8,128)(2,1)S(1)}, u32[]{:S(2)}, u32[]{:S(2)}) async-start(bf16[4,512,256]{2,1,0:T(8,128)(2,1)} %pad_maximum_fusion.5), calls=%async_computation.2 | async-start | bytes 2097152 | tf_op jit(solution)/shard_map/all_to_all | solution.py:181
  122.1 32.3 %collective-permute-start.3 = (bf16[2,512,1024]{2,1,0:T(8,128)(2,1)S(1)}, bf16[2,512,1024]{2,1,0:T(8,128)(2,1)}, u32[]{:S(2)}, u32[]{:S(2)}) collective-permute-start(bf16[2,512,1024]{2,1,0:T(8,128)(2,1)S(1)} %pad_maximum_fusion.refs_6_.refs_10_), channel_id=1, source_target_pairs={{0,1},{1,0},{2,3},{3,2},{4,5},{5,4},{6,7},{7,6},{8,9},{9,8},{10,11... | collective-permute-start | bytes 6291464 | tf_op jit(solution)/shard_map/ppermute | solution.py:470
  124.2 30.3 %collective-permute-start.7 = (bf16[2,512,1024]{2,1,0:T(8,128)(2,1)}, bf16[2,512,1024]{2,1,0:T(8,128)(2,1)}, u32[]{:S(2)}, u32[]{:S(2)}) collective-permute-start(bf16[2,512,1024]{2,1,0:T(8,128)(2,1)} %pad_maximum_fusion.1.refs_8_.refs_12_), channel_id=1, source_target_pairs={{0,1},{1,0},{2,3},{3,2},{4,5},{5,4},{6,7},{7,6},{8,9},{9,8},{10,11... | collective-permute-start | bytes 6291464 | tf_op jit(solution)/shard_map/ppermute | solution.py:470
  127.2 27.2 %collective-permute-start.11 = (bf16[2,512,1024]{2,1,0:T(8,128)(2,1)}, bf16[2,512,1024]{2,1,0:T(8,128)(2,1)}, u32[]{:S(2)}, u32[]{:S(2)}) collective-permute-start(bf16[2,512,1024]{2,1,0:T(8,128)(2,1)} %pad_maximum_fusion.2.refs_10_.refs_14_), channel_id=1, source_target_pairs={{0,1},{1,0},{2,3},{3,2},{4,5},{5,4},{6,7},{7,6},{8,9},{9,8},{10,11... | collective-permute-start | bytes 6291464 | tf_op jit(solution)/shard_map/ppermute | solution.py:470
  149.8 19.2 %collective-permute-start.15 = (bf16[512,1024]{1,0:T(8,128)(2,1)}, bf16[512,1024]{1,0:T(8,128)(2,1)}, u32[]{:S(2)}, u32[]{:S(2)}) collective-permute-start(bf16[512,1024]{1,0:T(8,128)(2,1)} %choose.5), channel_id=1, source_target_pairs={{0,2},{2,0},{1,3},{3,1},{4,6},{6,4},{5,7},{7,5},{8,10},{10,8},{9,1... | collective-permute-start | bytes 3145736 | tf_op jit(solution)/shard_map/ppermute | solution.py:462
  150.4 16.8 %copy-start.8 = (bf16[4,512,256]{2,1,0:T(8,128)(2,1)}, bf16[4,512,256]{2,1,0:T(8,128)(2,1)S(1)}, u32[]{:S(2)}) copy-start(bf16[4,512,256]{2,1,0:T(8,128)(2,1)S(1)} %all-to-all-done.2.refs_7_) | copy-start | bytes 3145732
  151.6 17.4 %collective-permute-start.12 = (bf16[3,512,256]{2,1,0:T(8,128)(2,1)}, bf16[3,512,256]{2,1,0:T(8,128)(2,1)}, u32[]{:S(2)}, u32[]{:S(2)}) collective-permute-start(bf16[3,512,256]{2,1,0:T(8,128)(2,1)} %pad_maximum_fusion.8), channel_id=1, source_target_pairs={{0,16},{16,0},{1,17},{17,1},{2,18},{18,2},{3,19},{19,3},{4,20},{20... | collective-permute-start | bytes 2359304 | tf_op jit(solution)/shard_map/ppermute | solution.py:189
  154.4 14.7 %collective-permute-start.16 = (bf16[1,512,1024]{2,1,0:T(8,128)(2,1)}, bf16[1,512,1024]{2,1,0:T(8,128)(2,1)S(1)}, u32[]{:S(2)}, u32[]{:S(2)}) collective-permute-start(bf16[1,512,1024]{2,1,0:T(8,128)(2,1)} %bitcast.68), channel_id=1, source_target_pairs={{0,1},{1,0},{2,3},{3,2},{4,5},{5,4},{6,7},{7,6},{8,9},{9,8},{10,11... | collective-permute-start | bytes 3145736 | tf_op jit(solution)/shard_map/ppermute | solution.py:470
  169.0 2.9 %collective-permute-start.17 = (bf16[1,512,1024]{2,1,0:T(8,128)(2,1)}, bf16[1,512,1024]{2,1,0:T(8,128)(2,1)S(1)}, u32[]{:S(2)}, u32[]{:S(2)}) collective-permute-start(bf16[1,512,1024]{2,1,0:T(8,128)(2,1)} %bitcast.45.refs_17_), channel_id=1, source_target_pairs={{0,1},{1,0},{2,3},{3,2},{4,5},{5,4},{6,7},{7,6},{8,9},{9,8},{10,11... | collective-permute-start | bytes 3145736 | tf_op jit(solution)/shard_map/ppermute | solution.py:470
  169.2 2.7 %copy-start.16 = (f32[5,256,16]{1,2,0:T(8,128)}, f32[5,256,16]{1,2,0:T(8,128)S(1)}, u32[]{:S(2)}) copy-start(f32[5,256,16]{1,2,0:T(8,128)S(1)} %bitcast_dynamic-update-slice_fusion) | copy-start | bytes 245764
  169.2 2.7 %copy-start.17 = (bf16[1,512,1024]{2,1,0:T(8,128)(2,1)}, bf16[1,512,1024]{2,1,0:T(8,128)(2,1)S(1)}, u32[]{:S(2)}) copy-start(bf16[1,512,1024]{2,1,0:T(8,128)(2,1)S(1)} %collective-permute-done.16.refs_18_) | copy-start | bytes 3145732
  200.0 13.6 %collective-permute-start.18 = (bf16[512,256]{1,0:T(8,128)(2,1)}, bf16[512,256]{1,0:T(8,128)(2,1)S(1)}, u32[]{:S(2)}, u32[]{:S(2)}) collective-permute-start(bf16[512,256]{1,0:T(8,128)(2,1)} %get-tuple-element.8), channel_id=1, source_target_pairs={{0,4},{4,0},{8,12},{12,8},{1,5},{5,1},{9,13},{13,9},{2,6},{6,2},{1... | collective-permute-start | bytes 786440 | tf_op jit(solution)/shard_map/ppermute | solution.py:494
  200.1 21.6 %collective-permute-start.19 = (bf16[512,256]{1,0:T(8,128)(2,1)}, bf16[512,256]{1,0:T(8,128)(2,1)S(1)}, u32[]{:S(2)}, u32[]{:S(2)}) collective-permute-start(bf16[512,256]{1,0:T(8,128)(2,1)} %get-tuple-element.9), channel_id=1, source_target_pairs={{0,8},{4,12},{8,0},{12,4},{1,9},{5,13},{9,1},{13,5},{2,10},{6,14},... | collective-permute-start | bytes 786440 | tf_op jit(solution)/shard_map/ppermute | solution.py:494
  202.9 18.8 %collective-permute-start.20 = (bf16[512,256]{1,0:T(8,128)(2,1)}, bf16[512,256]{1,0:T(8,128)(2,1)S(1)}, u32[]{:S(2)}, u32[]{:S(2)}) collective-permute-start(bf16[512,256]{1,0:T(8,128)(2,1)} %get-tuple-element.10), channel_id=1, source_target_pairs={{0,12},{4,8},{8,4},{12,0},{1,13},{5,9},{9,5},{13,1},{2,14},{6,10},... | collective-permute-start | bytes 786440 | tf_op jit(solution)/shard_map/ppermute | solution.py:494
  213.6 8.1 %copy-start.11 = (bf16[512,256]{1,0:T(8,128)(2,1)}, bf16[512,256]{1,0:T(8,128)(2,1)S(1)}, u32[]{:S(2)}) copy-start(bf16[512,256]{1,0:T(8,128)(2,1)S(1)} %collective-permute-done.18.refs_1_) | copy-start | bytes 786436
  (11 other events, 17.0 us)

commit v6 on v5

--- a/solution.py
+++ b/solution.py
@@ -14,6 +14,7 @@
 GATHER_BYTES = 24 << 20
 KERNEL_BYTES = 56 << 20
 FINISH_COST = 4
+AHEAD = 2 * 10**9
 WEIGHT = 23 * 10**9
 
 
@@ -142,7 +143,7 @@
     )(index.reshape(1).astype(jnp.int32), *candidates, *waits)
 
 
-def after(x, *waits):
+def after(x, *waits, weight=0):
     def nothing(*refs):
         del refs
 
@@ -153,6 +154,7 @@
         in_specs=[anywhere] * (1 + len(waits)),
         out_specs=anywhere,
         input_output_aliases={0: 0},
+        cost_estimate=pl.CostEstimate(flops=weight, bytes_accessed=weight // 300, transcendentals=0),
         name="after",
     )(x, *waits)
 
@@ -329,17 +331,17 @@
     (early_ref,) = take(1)
     pair_hbm, query_hbm = take(2 * n_weights), take(n_weights)
     x_hbm = [take(count) for count in counts]
-    outs, (state_ref,) = take(seq), take(1)
-    x_buf, pair_buf, query_buf, prod, out, ends, conv_buf, x_sem, pair_sem, query_sem = take(10)
+    outs, (conv_buf, state_ref) = take(seq - seq // 2), take(2)
+    x_buf, pair_buf, query_buf, prod, out, ends, x_sem, pair_sem, query_sem = take(9)
     rows = x_buf.shape[1]
     channels = conv_buf.shape[1]
     groups = prod.shape[0]
     first = 2 * pair_sem.shape[1] + (n_weights + 1) // 2
-    last = seq - 1
+    late = early_ref.shape[0]
     x_copies = [token_copies(x_hbm[i], x_buf.at[i], x_sem.at[i]) for i in range(seq)]
     pair_copies = weight_copies(order_ref, pair_hbm, pair_buf, pair_sem)
     query_copies = weight_copies(order_ref, query_hbm, query_buf, query_sem)
-    for copy in pair_copies + x_copies[last]:
+    for copy in pair_copies + sum(x_copies[late:], []):
         copy.start()
 
     def put(i, product):
@@ -347,27 +349,97 @@
         for g in range(groups):
             prod[g, to, :] = product[:, g * LANES : (g + 1) * LANES].astype(jnp.float32)
 
-    for i in range(last):
+    for i in range(late):
         put(i, early_ref[i])
-    for copy in pair_copies + x_copies[last]:
+    for copy in pair_copies:
         copy.wait()
-    for copy in query_copies + sum(x_copies[:last], []):
+    for i in range(late, seq):
+        for copy in x_copies[i]:
+            copy.wait()
+        if i == late:
+            for copy in query_copies + sum(x_copies[:late], []):
+                copy.start()
+        put(i, product_rows(x_buf.at[i], pair_buf, channels))
+    modes_over_time(modes_ref, prod, out, ends, conv_buf, state_ref)
+    for copy in query_copies + sum(x_copies[:late], []):
+        copy.wait()
+    for step in range(seq // 2, seq):
+        i = order_ref[first + 2 * seq + step]
+        shard = order_ref[first + i]
+        outs[step - seq // 2][...] = gated_rows(x_buf[i], query_buf, conv_buf, shard, rows)
+
+
+def gated_rows(x, query_buf, conv_buf, shard, rows):
+    acc = jnp.dot(x, query_buf[...], preferred_element_type=jnp.float32)
+    query = acc.astype(jnp.bfloat16).astype(jnp.float32)
+    conv = conv_buf[pl.ds(pl.multiple_of(shard * rows, rows), rows), :].astype(jnp.float32)
+    return (query * conv).astype(jnp.bfloat16)
+
+
+def near_kernel(n_weights, counts, order_ref, conv_ref, *refs):
+    refs, seq = list(refs), len(counts)
+
+    def take(count):
+        taken = refs[:count]
+        del refs[:count]
+        return taken
+
+    query_hbm = take(n_weights)
+    x_hbm = [take(count) for count in counts]
+    outs = take(seq // 2)
+    x_buf, query_buf, x_sem, query_sem = take(4)
+    rows = x_buf.shape[1]
+    first = 2 * query_sem.shape[1] + (n_weights + 1) // 2
+    query_copies = weight_copies(order_ref, query_hbm, query_buf, query_sem)
+    x_copies = [token_copies(x_hbm[i], x_buf.at[i], x_sem.at[i]) for i in range(seq)]
+    for copy in query_copies:
         copy.start()
-    put(last, product_rows(x_buf.at[last], pair_buf, channels))
-    modes_over_time(modes_ref, prod, out, ends, conv_buf, state_ref)
-    for copy in query_copies + sum(x_copies[:last], []):
+    for i in range(seq):
+
+        @pl.when(order_ref[first + seq + i] < seq // 2)
+        def _():
+            for copy in x_copies[i]:
+                copy.start()
+
+    for copy in query_copies:
         copy.wait()
     for i in range(seq):
-        shard = order_ref[first + i]
-        acc = jnp.dot(x_buf[i], query_buf[...], preferred_element_type=jnp.float32)
-        query = acc.astype(jnp.bfloat16).astype(jnp.float32)
-        conv = conv_buf[pl.ds(pl.multiple_of(shard * rows, rows), rows), :].astype(jnp.float32)
-        gated = (query * conv).astype(jnp.bfloat16)
-        for step in range(seq):
-
-            @pl.when(order_ref[first + seq + i] == step)
-            def _():
-                outs[step][...] = gated
+
+        @pl.when(order_ref[first + seq + i] < seq // 2)
+        def _():
+            for copy in x_copies[i]:
+                copy.wait()
+
+    for step in range(seq // 2):
+        i = order_ref[first + 2 * seq + step]
+        outs[step][...] = gated_rows(x_buf[i], query_buf, conv_ref, order_ref[first + i], rows)
+
+
+def gate_near(order, xs, query, conv):
+    quarters, share, width = query[0].shape
+    seq = len(xs)
+    rows, depth = xs[0][0].shape[1:]
+    vmem, anywhere = pl.BlockSpec(memory_space=pltpu.VMEM), pl.BlockSpec(memory_space=pl.ANY)
+    arrays = [*query, *sum(xs, [])]
+    return pl.pallas_call(
+        functools.partial(near_kernel, len(query), [len(x) for x in xs]),
+        out_shape=tuple(jax.ShapeDtypeStruct((rows, width), jnp.bfloat16) for _ in range(seq // 2)),
+        in_specs=[pl.BlockSpec(memory_space=pltpu.SMEM), vmem] + [anywhere] * len(arrays),
+        out_specs=(vmem,) * (seq // 2),
+        scratch_shapes=[
+            pltpu.VMEM((seq, rows, quarters * depth), jnp.bfloat16),
+            pltpu.VMEM((quarters * depth, width), jnp.bfloat16),
+            pltpu.SemaphoreType.DMA((seq, quarters)),
+            pltpu.SemaphoreType.DMA((len(query) + 1 >> 1, quarters)),
+        ],
+        compiler_params=pltpu.CompilerParams(vmem_limit_bytes=KERNEL_BYTES),
+        cost_estimate=pl.CostEstimate(
+            flops=seq * rows * depth * quarters * width,
+            bytes_accessed=quarters * depth * (seq * rows + 2 * width),
+            transcendentals=0,
+        ),
+        name="gate_near",
+    )(order, conv, *arrays)
 
 
 def finish(order, early, xs, pair, query, decay_rate, residue, carried):
@@ -387,13 +459,16 @@
     ).transpose(0, 2, 1)
     vmem, anywhere = pl.BlockSpec(memory_space=pltpu.VMEM), pl.BlockSpec(memory_space=pl.ANY)
     arrays = [*pair, *query, *sum(xs, [])]
-    *gated, state = pl.pallas_call(
+    *gated, conv, state = pl.pallas_call(
         functools.partial(finish_kernel, len(query), [len(x) for x in xs]),
-        out_shape=tuple(jax.ShapeDtypeStruct((rows, width), jnp.bfloat16) for _ in range(seq))
-        + (jax.ShapeDtypeStruct((modes, width), jnp.float32),),
+        out_shape=tuple(jax.ShapeDtypeStruct((rows, width), jnp.bfloat16) for _ in range(seq - seq // 2))
+        + (
+            jax.ShapeDtypeStruct((length, width), jnp.bfloat16),
+            jax.ShapeDtypeStruct((modes, width), jnp.float32),
+        ),
         in_specs=[pl.BlockSpec(memory_space=pltpu.SMEM), vmem, vmem]
         + [anywhere] * len(arrays),
-        out_specs=(vmem,) * (seq + 1),
+        out_specs=(vmem,) * (seq - seq // 2 + 2),
         scratch_shapes=[
             pltpu.VMEM((seq, rows, quarters * depth), jnp.bfloat16),
             pltpu.VMEM((quarters * depth, 2 * width), jnp.bfloat16),
@@ -401,7 +476,6 @@
             pltpu.VMEM((width // LANES, length, LANES), jnp.float32),
             pltpu.VMEM((width // LANES, length, LANES), jnp.float32),
             pltpu.VMEM((modes, SUBLANES, LANES), jnp.float32),
-            pltpu.VMEM((length, width), jnp.bfloat16),
             pltpu.SemaphoreType.DMA((seq, quarters)),
             pltpu.SemaphoreType.DMA((len(pair) + 2 >> 1, quarters)),
             pltpu.SemaphoreType.DMA((len(query) + 1 >> 1, quarters)),
@@ -414,7 +488,7 @@
         ),
         name="finish",
     )(order, table, early, *arrays)
-    return gated, state.T
+    return gated, conv, state.T
 
 
 def place_columns(pieces, place):
@@ -462,7 +536,7 @@
             last = lax.ppermute(arrival, "chan", ring(chan, turn))
             group.append(last)
         if phase == seq:
-            early = early_products(by_feature, xs, w_keys + w_values)
+            early = early_products(by_feature, xs[:-1], w_keys + w_values)
             group[-1] = after(group[-1], early, w_queries[-1])
             group = [x[None] for x in group]
         else:
@@ -487,12 +561,18 @@
         origins.append(at_place([jnp.int32(origin) for way, step, origin in chosen]))
 
     steps = [place ^ origin for origin in origins]
-    order = jnp.concatenate([by_feature, jnp.stack([jnp.int32(i) for i in origins + steps])])
-
-    gated, new_state = finish(order, early, xs, w_keys + w_values, w_queries, decay_rate, residue, carried)
-    pieces = [
-        lax.ppermute(gated[step], "seq", mirror(seq, step)) if step else gated[0] for step in range(seq)
-    ]
+    by_step = [sum(jnp.where(near == step, i, 0) for i, near in enumerate(steps)) for step in range(seq)]
+    order = jnp.concatenate([by_feature, jnp.stack([jnp.int32(i) for i in origins + steps + by_step])])
+
+    far, conv, new_state = finish(order, early, xs, w_keys + w_values, w_queries, decay_rate, residue, carried)
+    half = seq // 2
+    pieces = {
+        step: after(lax.ppermute(far[step - half], "seq", mirror(seq, step)), weight=AHEAD)
+        for step in range(half, seq)
+    }
+    for step, piece in enumerate(gate_near(order, xs, w_queries, conv)):
+        pieces[step] = lax.ppermute(piece, "seq", mirror(seq, step)) if step else piece
+    pieces = [pieces[step] for step in range(seq)]
     return place_columns(pieces, place), new_state
 
 

time: 228 us -> 222 us (0.974); the launches traced: 225 us -> 222 us
  waiting for transfers between devices: 99.2 us -> 92.7 us
    all_to_all x3, waiting for transfers between devices: 32.2 us -> 16.1 us  [exchange_weights(): mine = lax.all_to_all(mine, 'seq', split_axis=0, concat_axis=0, tiled=True)]
    ppermute x3, waiting for transfers between devices: 45.3 us -> 54.7 us  [by_channels(): ways[1][phase] = lax.ppermute(ways[1][phase - 1], 'seq', downs)]
    pallas_call x0 -> x1, Pallas kernels: none -> 8.55 us  [gate_near(): pl.pallas_call(functools.partial(near_kernel, len(query), [len(x) for x i...]
    ppermute x3, waiting for transfers between devices: 1.72 us -> 6.49 us  [exchange_weights(): shares += [own, lax.ppermute(fetched, 'parts', ring(parts, turn))]]
    ppermute x3, waiting for transfers between devices: 17.2 us -> 12.7 us  [the longest x2 8.63 us: by_channels(): lax.ppermute(far[step - half], 'seq', mirror(seq, step))]
    pallas_call x1, Pallas kernels: 27.1 us -> 23 us  [finish(): pl.pallas_call(functools.partial(finish_kernel, len(query), [len(x) for x...]
    pallas_call x1, Pallas kernels: 12.8 us -> 10.3 us  [early_products(): pl.pallas_call(functools.partial(product_kernel, len(pair), len(xs[0])),...]
    unnamed x38 -> x36, local copies, waits for them, and re-layouts: 3.29 us -> 4.64 us
  transfers between devices with their start and end apart: 24 -> 24, of which waited for: 9 -> 9; matrix products, arithmetic and copies ran while one was open for 8% -> 8% of each run, Pallas kernels for 8% -> 13%
where the time goes in v6:
time: 222 us
  waiting for transfers between devices  92.7 us (42%)
  Pallas kernels  53.1 us (24%)
  starting transfers between devices  48.7 us (22%)
  local copies, waits for them, and re-layouts  13.2 us (6%)
  other arithmetic  13.1 us (6%)
    ppermute x3, waiting for transfers between devices, by_channels(): ways[1][phase] = lax.ppermute(ways[1][phase - 1], 'seq', downs)  54.7 us
    pallas_call x1, Pallas kernels, finish(): pl.pallas_call(functools.partial(finish_kernel, len(query), [len(x) for x...  23 us
    all_to_all x3, starting transfers between devices, exchange_weights(): mine = lax.all_to_all(mine, 'seq', split_axis=0, concat_axis=0, tiled=True)  21.5 us
    all_to_all x3, waiting for transfers between devices, exchange_weights(): mine = lax.all_to_all(mine, 'seq', split_axis=0, concat_axis=0, tiled=True)  16.1 us
    pallas_call x1, Pallas kernels, early_products(): pl.pallas_call(functools.partial(product_kernel, len(pair), len(xs[0])),...  10.3 us
    ppermute x3, starting transfers between devices, by_channels(): ways[0][phase] = lax.ppermute(ways[0][phase - 1], 'seq', ups)  8.92 us
    pallas_call x3, Pallas kernels, choose(): pl.pallas_call(kernel, out_shape=jax.ShapeDtypeStruct(shape.shape, shape....  8.9 us
    ppermute x2, waiting for transfers between devices, by_channels(): lax.ppermute(far[step - half], 'seq', mirror(seq, step))  8.63 us
  transfers between devices with their start and end apart: 24, of which 9 were waited for; matrix products, arithmetic and copies ran while one was open for 8% of the time, Pallas kernels for 13%

profile of v6, /device:TPU:0, one launch (start us, length us, event | category | flops | bytes accessed | tf_op | source)
XLA Modules:
  0.0 221.8 jit_solution(6042998852968732576)
XLA Ops:
  0.7 2.1 fusion.2
  3.8 6.3 %all-to-all-start = ((bf16[4,512,256]{2,1,0:T(8,128)(2,1)}), bf16[4,512,256]{2,1,0:T(8,128)(2,1)S(1)}, u32[]{:S(2)}, u32[]{:S(2)}) async-start(bf16[4,512,256]{2,1,0:T(8,128)(2,1)} %pad_maximum_fusion.3), calls=%async_computation | async-start | bytes 2097152 | tf_op jit(solution)/shard_map/all_to_all | solution.py:183
  11.4 5.6 %collective-permute-start.4 = (bf16[512,1024]{1,0:T(8,128)(2,1)}, bf16[512,1024]{1,0:T(8,128)(2,1)}, u32[]{:S(2)}, u32[]{:S(2)}) collective-permute-start(bf16[512,1024]{1,0:T(8,128)(2,1)} %param.7), channel_id=1, source_target_pairs={{0,4},{4,8},{8,12},{1,5},{5,9},{9,13},{2,6},{6,10},{10,14},{3,7},{... | collective-permute-start | bytes 3145736 | tf_op jit(solution)/shard_map/ppermute | solution.py:550
  17.0 1.5 collective-permute-start.2
  18.5 2.1 fusion.1
  21.7 15.3 %all-to-all-done.refs_3_.refs_0_.refs_1_ = bf16[4,512,256]{2,1,0:T(8,128)(2,1)S(1)} async-done(((bf16[4,512,256]{2,1,0:T(8,128)(2,1)}), bf16[4,512,256]{2,1,0:T(8,128)(2,1)S(1)}, u32[]{:S(2)}, u32[]{:S(2)}) %all-to-all-start) | async-done | bytes 1048608 | tf_op jit(solution)/shard_map/all_to_all | solution.py:183
  37.0 3.5 %all-to-all-start.1 = ((bf16[4,512,256]{2,1,0:T(8,128)(2,1)}), bf16[4,512,256]{2,1,0:T(8,128)(2,1)S(1)}, u32[]{:S(2)}, u32[]{:S(2)}) async-start(bf16[4,512,256]{2,1,0:T(8,128)(2,1)} %pad_maximum_fusion.4), calls=%async_computation.1 | async-start | bytes 2097152 | tf_op jit(solution)/shard_map/all_to_all | solution.py:183
  40.5 13.8 %collective-permute-done.5.refs_1_ = bf16[512,1024]{1,0:T(8,128)(2,1)S(1)} collective-permute-done((bf16[512,1024]{1,0:T(8,128)(2,1)}, bf16[512,1024]{1,0:T(8,128)(2,1)S(1)}, u32[]{:S(2)}, u32[]{:S(2)}) %collective-permute-start.5) | collective-permute-done | bytes 1048608 | tf_op jit(solution)/shard_map/ppermute | solution.py:551
  55.6 1.6 collective-permute-start.9
  57.2 2.6 %choose.3 = bf16[512,1024]{1,0:T(8,128)(2,1)} custom-call(s32[1]{0:T(128)} %bitcast.37.index_ref, bf16[512,1024]{1,0:T(8,128)(2,1)} %collective-permute-done.4.refs_0_, bf16[512,1024]{1,0:T(8,128)(2,1)} %copy-done.4, bf16[512,1024]{1,0:T(8,128)(2,1)} %collective-permute-done.2.refs_2_, bf16[4,512,256]{2,1,0:T(8,128)(2,1)} %copy-done.2), custom_call_target="tpu_custom_call" | custom-call | bytes 1048576 | tf_op jit(solution)/shard_map/choose/pallas_call | solution.py:134
  59.8 1.5 collective-permute-start.6
  63.5 1.5 collective-permute-start
  65.0 29.6 %collective-permute-done.10.refs_2_ = bf16[512,1024]{1,0:T(8,128)(2,1)} collective-permute-done((bf16[512,1024]{1,0:T(8,128)(2,1)S(1)}, bf16[512,1024]{1,0:T(8,128)(2,1)}, u32[]{:S(2)}, u32[]{:S(2)}) %collective-permute-start.10) | collective-permute-done | bytes 1048608 | tf_op jit(solution)/shard_map/ppermute | solution.py:551
  95.9 1.7 collective-permute-start.13
  98.9 2.9 %choose.4 = bf16[512,1024]{1,0:T(8,128)(2,1)} custom-call(s32[1]{0:T(128)} %bitcast.44.index_ref, bf16[512,1024]{1,0:T(8,128)(2,1)} %collective-permute-done.9.refs_0_, bf16[512,1024]{1,0:T(8,128)(2,1)} %copy-done.4, bf16[512,1024]{1,0:T(8,128)(2,1)} %collective-permute-done.10.refs_2_, bf16[512,1024]{1,0:T(8,128)(2,1)} %copy-done.5, ...), custom_call_target="tpu_custom_call" | custom-call | bytes 1048576 | tf_op jit(solution)/shard_map/choose/pallas_call | solution.py:134
  105.5 1.5 collective-permute-start.1
  108.9 11.7 %all-to-all-start.2 = ((bf16[4,512,256]{2,1,0:T(8,128)(2,1)}), bf16[4,512,256]{2,1,0:T(8,128)(2,1)S(1)}, u32[]{:S(2)}, u32[]{:S(2)}) async-start(bf16[4,512,256]{2,1,0:T(8,128)(2,1)} %pad_maximum_fusion.5), calls=%async_computation.2 | async-start | bytes 2097152 | tf_op jit(solution)/shard_map/all_to_all | solution.py:183
  120.6 1.9 pad_maximum_fusion.refs_6_.refs_10_.refs_3_
  122.8 1.7 pad_maximum_fusion.1.refs_8_.refs_12_.refs_5_
  124.6 11.3 %collective-permute-done.14.refs_3_ = bf16[512,1024]{1,0:T(8,128)(2,1)} collective-permute-done((bf16[512,1024]{1,0:T(8,128)(2,1)}, bf16[512,1024]{1,0:T(8,128)(2,1)}, u32[]{:S(2)}, u32[]{:S(2)}) %collective-permute-start.14) | collective-permute-done | bytes 1048608 | tf_op jit(solution)/shard_map/ppermute | solution.py:551
  135.9 3.4 %choose.5 = bf16[512,1024]{1,0:T(8,128)(2,1)} custom-call(s32[1]{0:T(128)} %bitcast.47.index_ref, bf16[512,1024]{1,0:T(8,128)(2,1)} %collective-permute-done.9.refs_0_, bf16[512,1024]{1,0:T(8,128)(2,1)} %collective-permute-done.13.refs_1_, bf16[512,1024]{1,0:T(8,128)(2,1)} %collective-permute-done.10.refs_2_, ...), custom_call_target="tpu_custom_call" | custom-call | flops 23000000512 | bytes 1048576 | tf_op jit(solution)/shard_map/choose/pallas_call | solution.py:134
  139.3 1.8 collective-permute-start.15
  141.1 3.0 %pad_maximum_fusion.2.refs_14_.refs_7_ = bf16[2,512,1024]{2,1,0:T(8,128)(2,1)} fusion(bf16[1,512,1024]{2,1,0:T(8,128)(2,1)} %bitcast.46, bf16[1,512,1024]{2,1,0:T(8,128)(2,1)} %bitcast.69), kind=kLoop, calls=%fused_computation.2 | loop fusion | flops 1048576 | bytes 4194304 | tf_op jit(solution)/shard_map/stack | solution.py:543
  148.7 10.3 %early_products.1.refs_1_.refs_0_ = bf16[2,512,256]{2,1,0:T(8,128)(2,1)} custom-call(s32[10]{0:T(128)} %stack.180.order_ref, bf16[4,512,256]{2,1,0:T(8,128)(2,1)} %copy-done.2, bf16[512,256]{1,0:T(8,128)(2,1)} %get-tuple-element.24.refs_1_.refs_2_, bf16[3,512,256]{2,1,0:T(8,128)(2,1)} %collective-permute-done.refs_2_.refs_4_.refs_3_, ...), custom_call_target="tpu_custom_call" | custom-call | flops 268435456 | bytes 524288 | tf_op jit(solution)/shard_map/early_products/pallas_call | solution.py:259
  159.1 6.5 %collective-permute-done.8.refs_2_.refs_9_ = bf16[3,512,256]{2,1,0:T(8,128)(2,1)} collective-permute-done((bf16[3,512,256]{2,1,0:T(8,128)(2,1)}, bf16[3,512,256]{2,1,0:T(8,128)(2,1)}, u32[]{:S(2)}, u32[]{:S(2)}) %collective-permute-start.8) | collective-permute-done | bytes 786464 | tf_op jit(solution)/shard_map/ppermute | solution.py:191
  165.8 2.7 %collective-permute-done.17.refs_19_.refs_12_ = bf16[1,512,1024]{2,1,0:T(8,128)(2,1)S(1)} collective-permute-done((bf16[1,512,1024]{2,1,0:T(8,128)(2,1)}, bf16[1,512,1024]{2,1,0:T(8,128)(2,1)S(1)}, u32[]{:S(2)}, u32[]{:S(2)}) %collective-permute-start.17) | collective-permute-done | bytes 1048608 | tf_op jit(solution)/shard_map/ppermute | solution.py:544
  169.4 23.0 %finish.1 = (bf16[512,256]{1,0:T(8,128)(2,1)}, bf16[512,256]{1,0:T(8,128)(2,1)}, bf16[2048,256]{1,0:T(8,128)(2,1)}, f32[16,256]{1,0:T(8,128)}) custom-call(s32[22]{0:T(128)} %concatenate.13.order_ref, f32[5,16,256]{2,1,0:T(8,128)} %bitcast.74, bf16[2,512,256]{2,1,0:T(8,128)(2,1)} %early_products.1.refs_1_.refs_0_, bf16[4,512,256]{2,1,0:T(8,128)(2,1)} %copy-done.2, ...), custom_call_target="tpu_custom_call" | custom-call | flops 8589934592 | bytes 23068672 | tf_op jit(solution)/shard_map/finish/pallas_call | solution.py:462
  192.6 2.8 %collective-permute-start.20 = (bf16[512,256]{1,0:T(8,128)(2,1)}, bf16[512,256]{1,0:T(8,128)(2,1)S(1)}, u32[]{:S(2)}, u32[]{:S(2)}) collective-permute-start(bf16[512,256]{1,0:T(8,128)(2,1)} %get-tuple-element.12), channel_id=1, source_target_pairs={{0,12},{4,8},{8,4},{12,0},{1,13},{5,9},{9,5},{13,1},{2,14},{6,10},... | collective-permute-start | bytes 786440 | tf_op jit(solution)/shard_map/ppermute | solution.py:570
  195.4 8.6 %gate_near.1 = (bf16[512,256]{1,0:T(8,128)(2,1)}, bf16[512,256]{1,0:T(8,128)(2,1)}) custom-call(s32[22]{0:T(128)} %concatenate.13.order_ref, bf16[2048,256]{1,0:T(8,128)(2,1)} %get-tuple-element.8.conv_ref, bf16[4,512,256]{2,1,0:T(8,128)(2,1)} %copy-done.3, bf16[512,256]{1,0:T(8,128)(2,1)} %get-tuple-element.14.refs_8_.refs_1_, ...), custom_call_target="tpu_custom_call" | custom-call | flops 2147483648 | bytes 10485760 | tf_op jit(solution)/shard_map/gate_near/pallas_call | solution.py:424
  204.7 8.6 %collective-permute-done.19.refs_0_ = bf16[512,256]{1,0:T(8,128)(2,1)S(1)} collective-permute-done((bf16[512,256]{1,0:T(8,128)(2,1)}, bf16[512,256]{1,0:T(8,128)(2,1)S(1)}, u32[]{:S(2)}, u32[]{:S(2)}) %collective-permute-start.19) | collective-permute-done | bytes 262176 | tf_op jit(solution)/shard_map/ppermute | solution.py:570
  214.7 4.1 %collective-permute-done.18.refs_1_ = bf16[512,256]{1,0:T(8,128)(2,1)S(1)} collective-permute-done((bf16[512,256]{1,0:T(8,128)(2,1)}, bf16[512,256]{1,0:T(8,128)(2,1)S(1)}, u32[]{:S(2)}, u32[]{:S(2)}) %collective-permute-start.18) | collective-permute-done | bytes 262176 | tf_op jit(solution)/shard_map/ppermute | solution.py:574
  219.5 2.3 %place_columns.1 = bf16[512,1024]{1,0:T(8,128)(2,1)} custom-call(s32[1]{0:T(128)} %bitcast.place_ref, bf16[512,256]{1,0:T(8,128)(2,1)} %get-tuple-element.9.refs_0_, bf16[512,256]{1,0:T(8,128)(2,1)} %copy-done.14, bf16[512,256]{1,0:T(8,128)(2,1)} %after.4.refs_2_, bf16[512,256]{1,0:T(8,128)(2,1)} %after.5.refs_3_), custom_call_target="tpu_custom_call" | custom-call | tf_op jit(solution)/shard_map/place_columns/pallas_call | solution.py:504
  (84 shorter events, 24.0 us)
Async XLA Ops:
  3.8 33.1 %all-to-all-start = ((bf16[4,512,256]{2,1,0:T(8,128)(2,1)}), bf16[4,512,256]{2,1,0:T(8,128)(2,1)S(1)}, u32[]{:S(2)}, u32[]{:S(2)}) async-start(bf16[4,512,256]{2,1,0:T(8,128)(2,1)} %pad_maximum_fusion.3), calls=%async_computation | async-start | bytes 2097152 | tf_op jit(solution)/shard_map/all_to_all | solution.py:183
  10.2 44.1 %collective-permute-start.5 = (bf16[512,1024]{1,0:T(8,128)(2,1)}, bf16[512,1024]{1,0:T(8,128)(2,1)S(1)}, u32[]{:S(2)}, u32[]{:S(2)}) collective-permute-start(bf16[512,1024]{1,0:T(8,128)(2,1)} %param.7), channel_id=1, source_target_pairs={{4,0},{8,4},{12,8},{5,1},{9,5},{13,9},{6,2},{10,6},{14,10},{7,3},{... | collective-permute-start | bytes 3145736 | tf_op jit(solution)/shard_map/ppermute | solution.py:551
  11.4 44.1 %collective-permute-start.4 = (bf16[512,1024]{1,0:T(8,128)(2,1)}, bf16[512,1024]{1,0:T(8,128)(2,1)}, u32[]{:S(2)}, u32[]{:S(2)}) collective-permute-start(bf16[512,1024]{1,0:T(8,128)(2,1)} %param.7), channel_id=1, source_target_pairs={{0,4},{4,8},{8,12},{1,5},{5,9},{9,13},{2,6},{6,10},{10,14},{3,7},{... | collective-permute-start | bytes 3145736 | tf_op jit(solution)/shard_map/ppermute | solution.py:550
  17.0 40.2 %collective-permute-start.2 = (bf16[512,1024]{1,0:T(8,128)(2,1)}, bf16[512,1024]{1,0:T(8,128)(2,1)}, u32[]{:S(2)}, u32[]{:S(2)}) collective-permute-start(bf16[512,1024]{1,0:T(8,128)(2,1)} %param.7), channel_id=1, source_target_pairs={{0,2},{2,0},{1,3},{3,1},{4,6},{6,4},{5,7},{7,5},{8,10},{10,8},{9,1... | collective-permute-start | bytes 3145736 | tf_op jit(solution)/shard_map/ppermute | solution.py:536
  37.0 20.3 %copy-start.2 = (bf16[4,512,256]{2,1,0:T(8,128)(2,1)}, bf16[4,512,256]{2,1,0:T(8,128)(2,1)S(1)}, u32[]{:S(2)}) copy-start(bf16[4,512,256]{2,1,0:T(8,128)(2,1)S(1)} %all-to-all-done.refs_3_.refs_0_.refs_1_) | copy-start | bytes 3145732
  37.0 60.6 %all-to-all-start.1 = ((bf16[4,512,256]{2,1,0:T(8,128)(2,1)}), bf16[4,512,256]{2,1,0:T(8,128)(2,1)S(1)}, u32[]{:S(2)}, u32[]{:S(2)}) async-start(bf16[4,512,256]{2,1,0:T(8,128)(2,1)} %pad_maximum_fusion.4), calls=%async_computation.1 | async-start | bytes 2097152 | tf_op jit(solution)/shard_map/all_to_all | solution.py:183
  54.3 2.9 %copy-start.4 = (bf16[512,1024]{1,0:T(8,128)(2,1)}, bf16[512,1024]{1,0:T(8,128)(2,1)S(1)}, u32[]{:S(2)}) copy-start(bf16[512,1024]{1,0:T(8,128)(2,1)S(1)} %collective-permute-done.5.refs_1_) | copy-start | bytes 3145732
  54.3 40.3 %collective-permute-start.10 = (bf16[512,1024]{1,0:T(8,128)(2,1)S(1)}, bf16[512,1024]{1,0:T(8,128)(2,1)}, u32[]{:S(2)}, u32[]{:S(2)}) collective-permute-start(bf16[512,1024]{1,0:T(8,128)(2,1)S(1)} %collective-permute-done.5.refs_1_), channel_id=1, source_target_pairs={{4,0},{8,4},{5,1},{9,5},{6,2},{10,6},{7,3},{11,7},{20,16},{24,20},... | collective-permute-start | bytes 3145736 | tf_op jit(solution)/shard_map/ppermute | solution.py:551
  55.6 40.3 %collective-permute-start.9 = (bf16[512,1024]{1,0:T(8,128)(2,1)}, bf16[512,1024]{1,0:T(8,128)(2,1)}, u32[]{:S(2)}, u32[]{:S(2)}) collective-permute-start(bf16[512,1024]{1,0:T(8,128)(2,1)} %collective-permute-done.4.refs_0_), channel_id=1, source_target_pairs={{4,8},{8,12},{5,9},{9,13},{6,10},{10,14},{7,11},{11,15},{20,24},{2... | collective-permute-start | bytes 3145736 | tf_op jit(solution)/shard_map/ppermute | solution.py:550
  59.8 37.8 %collective-permute-start.6 = (bf16[512,1024]{1,0:T(8,128)(2,1)}, bf16[512,1024]{1,0:T(8,128)(2,1)S(1)}, u32[]{:S(2)}, u32[]{:S(2)}) collective-permute-start(bf16[512,1024]{1,0:T(8,128)(2,1)} %choose.3), channel_id=1, source_target_pairs={{0,2},{2,0},{1,3},{3,1},{4,6},{6,4},{5,7},{7,5},{8,10},{10,8},{9,1... | collective-permute-start | bytes 3145736 | tf_op jit(solution)/shard_map/ppermute | solution.py:536
  63.5 34.1 %collective-permute-start = (bf16[3,512,256]{2,1,0:T(8,128)(2,1)}, bf16[3,512,256]{2,1,0:T(8,128)(2,1)}, u32[]{:S(2)}, u32[]{:S(2)}) collective-permute-start(bf16[3,512,256]{2,1,0:T(8,128)(2,1)} %pad_maximum_fusion.6), channel_id=1, source_target_pairs={{0,16},{16,0},{1,17},{17,1},{2,18},{18,2},{3,19},{19,3},{4,20},{20... | collective-permute-start | bytes 2359304 | tf_op jit(solution)/shard_map/ppermute | solution.py:191
  94.6 41.3 %collective-permute-start.14 = (bf16[512,1024]{1,0:T(8,128)(2,1)}, bf16[512,1024]{1,0:T(8,128)(2,1)}, u32[]{:S(2)}, u32[]{:S(2)}) collective-permute-start(bf16[512,1024]{1,0:T(8,128)(2,1)} %collective-permute-done.10.refs_2_), channel_id=1, source_target_pairs={{4,0},{5,1},{6,2},{7,3},{20,16},{21,17},{22,18},{23,19}} | collective-permute-start | bytes 3145736 | tf_op jit(solution)/shard_map/ppermute | solution.py:551
  95.9 40.0 %collective-permute-start.13 = (bf16[512,1024]{1,0:T(8,128)(2,1)}, bf16[512,1024]{1,0:T(8,128)(2,1)}, u32[]{:S(2)}, u32[]{:S(2)}) collective-permute-start(bf16[512,1024]{1,0:T(8,128)(2,1)} %collective-permute-done.9.refs_0_), channel_id=1, source_target_pairs={{8,12},{9,13},{10,14},{11,15},{24,28},{25,29},{26,30},{27,31}} | collective-permute-start | bytes 3145736 | tf_op jit(solution)/shard_map/ppermute | solution.py:550
  101.8 5.1 %copy-start.10 = (bf16[1024,1024]{1,0:T(8,128)(2,1)S(1)}, bf16[1024,1024]{1,0:T(8,128)(2,1)}, u32[]{:S(2)}) copy-start(bf16[1024,1024]{1,0:T(8,128)(2,1)} %param.8) | copy-start | bytes 6291460
  101.8 34.1 %collective-permute-start.11 = (bf16[512,1024]{1,0:T(8,128)(2,1)}, bf16[512,1024]{1,0:T(8,128)(2,1)}, u32[]{:S(2)}, u32[]{:S(2)}) collective-permute-start(bf16[512,1024]{1,0:T(8,128)(2,1)} %choose.4), channel_id=1, source_target_pairs={{0,2},{2,0},{1,3},{3,1},{4,6},{6,4},{5,7},{7,5},{8,10},{10,8},{9,1... | collective-permute-start | bytes 3145736 | tf_op jit(solution)/shard_map/ppermute | solution.py:536
  105.5 19.0 %collective-permute-start.1 = (bf16[3,512,256]{2,1,0:T(8,128)(2,1)}, bf16[3,512,256]{2,1,0:T(8,128)(2,1)}, u32[]{:S(2)}, u32[]{:S(2)}) collective-permute-start(bf16[3,512,256]{2,1,0:T(8,128)(2,1)} %pad_maximum_fusion.7), channel_id=1, source_target_pairs={{0,16},{16,0},{1,17},{17,1},{2,18},{18,2},{3,19},{19,3},{4,20},{20... | collective-permute-start | bytes 2359304 | tf_op jit(solution)/shard_map/ppermute | solution.py:191
  108.9 36.1 %all-to-all-start.2 = ((bf16[4,512,256]{2,1,0:T(8,128)(2,1)}), bf16[4,512,256]{2,1,0:T(8,128)(2,1)S(1)}, u32[]{:S(2)}, u32[]{:S(2)}) async-start(bf16[4,512,256]{2,1,0:T(8,128)(2,1)} %pad_maximum_fusion.5), calls=%async_computation.2 | async-start | bytes 2097152 | tf_op jit(solution)/shard_map/all_to_all | solution.py:183
  122.5 26.2 %collective-permute-start.3 = (bf16[2,512,1024]{2,1,0:T(8,128)(2,1)S(1)}, bf16[2,512,1024]{2,1,0:T(8,128)(2,1)}, u32[]{:S(2)}, u32[]{:S(2)}) collective-permute-start(bf16[2,512,1024]{2,1,0:T(8,128)(2,1)S(1)} %pad_maximum_fusion.refs_6_.refs_10_.refs_3_), channel_id=1, source_target_pairs={{0,1},{1,0},{2,3},{3,2},{4,5},{5,4},{6,7},{7,6},{8,9},{9,8},{10,11... | collective-permute-start | bytes 6291464 | tf_op jit(solution)/shard_map/ppermute | solution.py:544
  124.5 24.3 %collective-permute-start.7 = (bf16[2,512,1024]{2,1,0:T(8,128)(2,1)}, bf16[2,512,1024]{2,1,0:T(8,128)(2,1)}, u32[]{:S(2)}, u32[]{:S(2)}) collective-permute-start(bf16[2,512,1024]{2,1,0:T(8,128)(2,1)} %pad_maximum_fusion.1.refs_8_.refs_12_.refs_5_), channel_id=1, source_target_pairs={{0,1},{1,0},{2,3},{3,2},{4,5},{5,4},{6,7},{7,6},{8,9},{9,8},{10,11... | collective-permute-start | bytes 6291464 | tf_op jit(solution)/shard_map/ppermute | solution.py:544
  139.3 26.3 %collective-permute-start.15 = (bf16[512,1024]{1,0:T(8,128)(2,1)}, bf16[512,1024]{1,0:T(8,128)(2,1)}, u32[]{:S(2)}, u32[]{:S(2)}) collective-permute-start(bf16[512,1024]{1,0:T(8,128)(2,1)} %choose.5), channel_id=1, source_target_pairs={{0,2},{2,0},{1,3},{3,1},{4,6},{6,4},{5,7},{7,5},{8,10},{10,8},{9,1... | collective-permute-start | bytes 3145736 | tf_op jit(solution)/shard_map/ppermute | solution.py:536
  144.1 21.6 %collective-permute-start.12 = (bf16[2,512,1024]{2,1,0:T(8,128)(2,1)}, bf16[2,512,1024]{2,1,0:T(8,128)(2,1)}, u32[]{:S(2)}, u32[]{:S(2)}) collective-permute-start(bf16[2,512,1024]{2,1,0:T(8,128)(2,1)} %pad_maximum_fusion.2.refs_14_.refs_7_), channel_id=1, source_target_pairs={{0,1},{1,0},{2,3},{3,2},{4,5},{5,4},{6,7},{7,6},{8,9},{9,8},{10,11... | collective-permute-start | bytes 6291464 | tf_op jit(solution)/shard_map/ppermute | solution.py:544
  145.0 14.1 %copy-start.3 = (bf16[4,512,256]{2,1,0:T(8,128)(2,1)}, bf16[4,512,256]{2,1,0:T(8,128)(2,1)S(1)}, u32[]{:S(2)}) copy-start(bf16[4,512,256]{2,1,0:T(8,128)(2,1)S(1)} %all-to-all-done.2.refs_7_.refs_0_) | copy-start | bytes 3145732
  146.1 19.4 %collective-permute-start.8 = (bf16[3,512,256]{2,1,0:T(8,128)(2,1)}, bf16[3,512,256]{2,1,0:T(8,128)(2,1)}, u32[]{:S(2)}, u32[]{:S(2)}) collective-permute-start(bf16[3,512,256]{2,1,0:T(8,128)(2,1)} %pad_maximum_fusion.8), channel_id=1, source_target_pairs={{0,16},{16,0},{1,17},{17,1},{2,18},{18,2},{3,19},{19,3},{4,20},{20... | collective-permute-start | bytes 2359304 | tf_op jit(solution)/shard_map/ppermute | solution.py:191
  148.7 17.0 %collective-permute-start.16 = (bf16[1,512,1024]{2,1,0:T(8,128)(2,1)}, bf16[1,512,1024]{2,1,0:T(8,128)(2,1)S(1)}, u32[]{:S(2)}, u32[]{:S(2)}) collective-permute-start(bf16[1,512,1024]{2,1,0:T(8,128)(2,1)} %bitcast.71), channel_id=1, source_target_pairs={{0,1},{1,0},{2,3},{3,2},{4,5},{5,4},{6,7},{7,6},{8,9},{9,8},{10,11... | collective-permute-start | bytes 3145736 | tf_op jit(solution)/shard_map/ppermute | solution.py:544
  159.1 6.5 %copy-start.11 = (f32[256,16]{0,1:T(8,128)S(1)}, f32[256,16]{0,1:T(8,128)}, u32[]{:S(2)}) copy-start(f32[256,16]{0,1:T(8,128)} %param.11) | copy-start | bytes 49156
  159.1 6.6 %copy-start.15 = (f32[256,16]{0,1:T(8,128)S(1)}, f32[256,16]{0,1:T(8,128)}, u32[]{:S(2)}) copy-start(f32[256,16]{0,1:T(8,128)} %param.12) | copy-start | bytes 49156
  159.1 6.6 %copy-start.16 = (f32[256,16]{0,1:T(8,128)S(1)}, f32[256,16]{0,1:T(8,128)}, u32[]{:S(2)}) copy-start(f32[256,16]{0,1:T(8,128)} %param.13) | copy-start | bytes 49156
  165.6 2.9 %collective-permute-start.17 = (bf16[1,512,1024]{2,1,0:T(8,128)(2,1)}, bf16[1,512,1024]{2,1,0:T(8,128)(2,1)S(1)}, u32[]{:S(2)}, u32[]{:S(2)}) collective-permute-start(bf16[1,512,1024]{2,1,0:T(8,128)(2,1)} %bitcast.49.refs_17_.refs_10_), channel_id=1, source_target_pairs={{0,1},{1,0},{2,3},{3,2},{4,5},{5,4},{6,7},{7,6},{8,9},{9,8},{10,11... | collective-permute-start | bytes 3145736 | tf_op jit(solution)/shard_map/ppermute | solution.py:544
  165.7 2.7 %copy-start.17 = (f32[5,256,16]{1,2,0:T(8,128)}, f32[5,256,16]{1,2,0:T(8,128)S(1)}, u32[]{:S(2)}) copy-start(f32[5,256,16]{1,2,0:T(8,128)S(1)} %bitcast_dynamic-update-slice_fusion) | copy-start | bytes 245764
  192.5 20.8 %collective-permute-start.19 = (bf16[512,256]{1,0:T(8,128)(2,1)}, bf16[512,256]{1,0:T(8,128)(2,1)S(1)}, u32[]{:S(2)}, u32[]{:S(2)}) collective-permute-start(bf16[512,256]{1,0:T(8,128)(2,1)} %get-tuple-element.11), channel_id=1, source_target_pairs={{0,8},{4,12},{8,0},{12,4},{1,9},{5,13},{9,1},{13,5},{2,10},{6,14},... | collective-permute-start | bytes 786440 | tf_op jit(solution)/shard_map/ppermute | solution.py:570
  192.6 21.4 %collective-permute-start.20 = (bf16[512,256]{1,0:T(8,128)(2,1)}, bf16[512,256]{1,0:T(8,128)(2,1)S(1)}, u32[]{:S(2)}, u32[]{:S(2)}) collective-permute-start(bf16[512,256]{1,0:T(8,128)(2,1)} %get-tuple-element.12), channel_id=1, source_target_pairs={{0,12},{4,8},{8,4},{12,0},{1,13},{5,9},{9,5},{13,1},{2,14},{6,10},... | collective-permute-start | bytes 786440 | tf_op jit(solution)/shard_map/ppermute | solution.py:570
  204.0 14.8 %collective-permute-start.18 = (bf16[512,256]{1,0:T(8,128)(2,1)}, bf16[512,256]{1,0:T(8,128)(2,1)S(1)}, u32[]{:S(2)}, u32[]{:S(2)}) collective-permute-start(bf16[512,256]{1,0:T(8,128)(2,1)} %get-tuple-element.10), channel_id=1, source_target_pairs={{0,4},{4,0},{8,12},{12,8},{1,5},{5,1},{9,13},{13,9},{2,6},{6,2},{1... | collective-permute-start | bytes 786440 | tf_op jit(solution)/shard_map/ppermute | solution.py:574
  (10 other events, 14.2 us)

commit v7 on v6

--- a/solution.py
+++ b/solution.py
@@ -538,6 +538,7 @@
         if phase == seq:
             early = early_products(by_feature, xs[:-1], w_keys + w_values)
             group[-1] = after(group[-1], early, w_queries[-1])
+        if phase >= seq - 1:
             group = [x[None] for x in group]
         else:
             group = [jnp.stack(group)]

time: 222 us -> 221 us (level)
  other arithmetic: 13.1 us -> 10.1 us
    another operation x3 -> x2, other arithmetic: 6.63 us -> 3.58 us  [by_channels(): group = [jnp.stack(group)]]
    all_to_all x3, waiting for transfers between devices: 16.1 us -> 19 us  [exchange_weights(): mine = lax.all_to_all(mine, 'seq', split_axis=0, concat_axis=0, tiled=True)]
    unnamed x36 -> x38, local copies, waits for them, and re-layouts: 4.64 us -> 4.63 us
  transfers between devices with their start and end apart: 24 -> 25, of which waited for: 9 -> 9; matrix products, arithmetic and copies ran while one was open for 8% -> 7% of each run, Pallas kernels for 13% -> 13%
where the time goes in v7:
time: 221 us; the launch traced here: 220 us
  waiting for transfers between devices  93 us (42%)
  Pallas kernels  53.4 us (24%)
  starting transfers between devices  49.3 us (22%)
  local copies, waits for them, and re-layouts  13.1 us (6%)
  other arithmetic  10.1 us (5%)
    ppermute x3, waiting for transfers between devices, by_channels(): ways[1][phase] = lax.ppermute(ways[1][phase - 1], 'seq', downs)  54.7 us
    pallas_call x1, Pallas kernels, finish(): pl.pallas_call(functools.partial(finish_kernel, len(query), [len(x) for x...  23.3 us
    all_to_all x3, starting transfers between devices, exchange_weights(): mine = lax.all_to_all(mine, 'seq', split_axis=0, concat_axis=0, tiled=True)  21.5 us
    all_to_all x3, waiting for transfers between devices, exchange_weights(): mine = lax.all_to_all(mine, 'seq', split_axis=0, concat_axis=0, tiled=True)  19 us
    pallas_call x1, Pallas kernels, early_products(): pl.pallas_call(functools.partial(product_kernel, len(pair), len(xs[0])),...  10.3 us
    pallas_call x3, Pallas kernels, choose(): pl.pallas_call(kernel, out_shape=jax.ShapeDtypeStruct(shape.shape, shape....  8.96 us
    ppermute x3, starting transfers between devices, by_channels(): ways[0][phase] = lax.ppermute(ways[0][phase - 1], 'seq', ups)  8.82 us
    pallas_call x1, Pallas kernels, gate_near(): pl.pallas_call(functools.partial(near_kernel, len(query), [len(x) for x i...  8.52 us
  transfers between devices with their start and end apart: 25, of which 9 were waited for; matrix products, arithmetic and copies ran while one was open for 7% of the time, Pallas kernels for 13%

profile of v7, /device:TPU:0, one launch (start us, length us, event | category | flops | bytes accessed | tf_op | source)
XLA Modules:
  0.0 219.9 jit_solution(3162884439737111730)
XLA Ops:
  0.7 2.1 fusion.2
  3.8 6.3 %all-to-all-start = ((bf16[4,512,256]{2,1,0:T(8,128)(2,1)}), bf16[4,512,256]{2,1,0:T(8,128)(2,1)S(1)}, u32[]{:S(2)}, u32[]{:S(2)}) async-start(bf16[4,512,256]{2,1,0:T(8,128)(2,1)} %pad_maximum_fusion.2), calls=%async_computation | async-start | bytes 2097152 | tf_op jit(solution)/shard_map/all_to_all | solution.py:183
  11.4 5.5 %collective-permute-start.4 = (bf16[512,1024]{1,0:T(8,128)(2,1)}, bf16[512,1024]{1,0:T(8,128)(2,1)}, u32[]{:S(2)}, u32[]{:S(2)}) collective-permute-start(bf16[512,1024]{1,0:T(8,128)(2,1)} %param.7), channel_id=1, source_target_pairs={{0,4},{4,8},{8,12},{1,5},{5,9},{9,13},{2,6},{6,10},{10,14},{3,7},{... | collective-permute-start | bytes 3145736 | tf_op jit(solution)/shard_map/ppermute | solution.py:551
  17.0 1.5 collective-permute-start.2
  18.5 2.1 fusion.1
  21.7 15.3 %all-to-all-done.refs_3_.refs_0_.refs_1_ = bf16[4,512,256]{2,1,0:T(8,128)(2,1)S(1)} async-done(((bf16[4,512,256]{2,1,0:T(8,128)(2,1)}), bf16[4,512,256]{2,1,0:T(8,128)(2,1)S(1)}, u32[]{:S(2)}, u32[]{:S(2)}) %all-to-all-start) | async-done | bytes 1048608 | tf_op jit(solution)/shard_map/all_to_all | solution.py:183
  37.0 3.5 %all-to-all-start.1 = ((bf16[4,512,256]{2,1,0:T(8,128)(2,1)}), bf16[4,512,256]{2,1,0:T(8,128)(2,1)S(1)}, u32[]{:S(2)}, u32[]{:S(2)}) async-start(bf16[4,512,256]{2,1,0:T(8,128)(2,1)} %pad_maximum_fusion.3), calls=%async_computation.1 | async-start | bytes 2097152 | tf_op jit(solution)/shard_map/all_to_all | solution.py:183
  40.5 13.8 %collective-permute-done.5.refs_1_ = bf16[512,1024]{1,0:T(8,128)(2,1)S(1)} collective-permute-done((bf16[512,1024]{1,0:T(8,128)(2,1)}, bf16[512,1024]{1,0:T(8,128)(2,1)S(1)}, u32[]{:S(2)}, u32[]{:S(2)}) %collective-permute-start.5) | collective-permute-done | bytes 1048608 | tf_op jit(solution)/shard_map/ppermute | solution.py:552
  55.6 1.6 collective-permute-start.9
  57.2 2.6 %choose.3 = bf16[512,1024]{1,0:T(8,128)(2,1)} custom-call(s32[1]{0:T(128)} %bitcast.37.index_ref, bf16[512,1024]{1,0:T(8,128)(2,1)} %collective-permute-done.4.refs_0_, bf16[512,1024]{1,0:T(8,128)(2,1)} %copy-done.4, bf16[512,1024]{1,0:T(8,128)(2,1)} %collective-permute-done.2.refs_2_, bf16[4,512,256]{2,1,0:T(8,128)(2,1)} %copy-done.2), custom_call_target="tpu_custom_call" | custom-call | bytes 1048576 | tf_op jit(solution)/shard_map/choose/pallas_call | solution.py:134
  59.8 1.5 collective-permute-start.6
  63.5 1.5 collective-permute-start
  65.0 29.6 %collective-permute-done.10.refs_2_ = bf16[512,1024]{1,0:T(8,128)(2,1)} collective-permute-done((bf16[512,1024]{1,0:T(8,128)(2,1)S(1)}, bf16[512,1024]{1,0:T(8,128)(2,1)}, u32[]{:S(2)}, u32[]{:S(2)}) %collective-permute-start.10) | collective-permute-done | bytes 1048608 | tf_op jit(solution)/shard_map/ppermute | solution.py:552
  95.9 1.7 collective-permute-start.14
  98.9 2.9 %choose.4 = bf16[512,1024]{1,0:T(8,128)(2,1)} custom-call(s32[1]{0:T(128)} %bitcast.44.index_ref, bf16[512,1024]{1,0:T(8,128)(2,1)} %collective-permute-done.9.refs_0_, bf16[512,1024]{1,0:T(8,128)(2,1)} %copy-done.4, bf16[512,1024]{1,0:T(8,128)(2,1)} %collective-permute-done.10.refs_2_, bf16[512,1024]{1,0:T(8,128)(2,1)} %copy-done.5, ...), custom_call_target="tpu_custom_call" | custom-call | bytes 1048576 | tf_op jit(solution)/shard_map/choose/pallas_call | solution.py:134
  105.4 1.5 collective-permute-start.1
  108.8 11.7 %all-to-all-start.2 = ((bf16[4,512,256]{2,1,0:T(8,128)(2,1)}), bf16[4,512,256]{2,1,0:T(8,128)(2,1)S(1)}, u32[]{:S(2)}, u32[]{:S(2)}) async-start(bf16[4,512,256]{2,1,0:T(8,128)(2,1)} %pad_maximum_fusion.4), calls=%async_computation.2 | async-start | bytes 2097152 | tf_op jit(solution)/shard_map/all_to_all | solution.py:183
  120.5 1.9 pad_maximum_fusion.refs_6_.refs_10_.refs_3_
  122.7 1.7 pad_maximum_fusion.1.refs_8_.refs_12_.refs_5_
  124.6 11.4 %collective-permute-done.15.refs_3_ = bf16[512,1024]{1,0:T(8,128)(2,1)} collective-permute-done((bf16[512,1024]{1,0:T(8,128)(2,1)}, bf16[512,1024]{1,0:T(8,128)(2,1)}, u32[]{:S(2)}, u32[]{:S(2)}) %collective-permute-start.15) | collective-permute-done | bytes 1048608 | tf_op jit(solution)/shard_map/ppermute | solution.py:552
  135.9 3.5 %choose.5 = bf16[512,1024]{1,0:T(8,128)(2,1)} custom-call(s32[1]{0:T(128)} %bitcast.47.index_ref, bf16[512,1024]{1,0:T(8,128)(2,1)} %collective-permute-done.9.refs_0_, bf16[512,1024]{1,0:T(8,128)(2,1)} %collective-permute-done.14.refs_1_, bf16[512,1024]{1,0:T(8,128)(2,1)} %collective-permute-done.10.refs_2_, ...), custom_call_target="tpu_custom_call" | custom-call | flops 23000000512 | bytes 1048576 | tf_op jit(solution)/shard_map/choose/pallas_call | solution.py:134
  139.4 1.8 collective-permute-start.16
  141.2 3.7 %all-to-all-done.2.refs_7_.refs_0_ = bf16[4,512,256]{2,1,0:T(8,128)(2,1)S(1)} async-done(((bf16[4,512,256]{2,1,0:T(8,128)(2,1)}), bf16[4,512,256]{2,1,0:T(8,128)(2,1)S(1)}, u32[]{:S(2)}, u32[]{:S(2)}) %all-to-all-start.2) | async-done | bytes 1048608 | tf_op jit(solution)/shard_map/all_to_all | solution.py:183
  149.2 10.3 %early_products.1.refs_1_.refs_0_ = bf16[2,512,256]{2,1,0:T(8,128)(2,1)} custom-call(s32[10]{0:T(128)} %stack.171.order_ref, bf16[4,512,256]{2,1,0:T(8,128)(2,1)} %copy-done.2, bf16[512,256]{1,0:T(8,128)(2,1)} %get-tuple-element.24.refs_1_.refs_2_, bf16[3,512,256]{2,1,0:T(8,128)(2,1)} %collective-permute-done.refs_2_.refs_4_.refs_3_, ...), custom_call_target="tpu_custom_call" | custom-call | flops 268435456 | bytes 524288 | tf_op jit(solution)/shard_map/early_products/pallas_call | solution.py:259
  159.6 5.3 %collective-permute-done.8.refs_2_.refs_9_ = bf16[3,512,256]{2,1,0:T(8,128)(2,1)} collective-permute-done((bf16[3,512,256]{2,1,0:T(8,128)(2,1)}, bf16[3,512,256]{2,1,0:T(8,128)(2,1)}, u32[]{:S(2)}, u32[]{:S(2)}) %collective-permute-start.8) | collective-permute-done | bytes 786464 | tf_op jit(solution)/shard_map/ppermute | solution.py:191
  165.1 2.6 %collective-permute-done.18.refs_21_.refs_14_ = bf16[1,512,1024]{2,1,0:T(8,128)(2,1)S(1)} collective-permute-done((bf16[1,512,1024]{2,1,0:T(8,128)(2,1)}, bf16[1,512,1024]{2,1,0:T(8,128)(2,1)S(1)}, u32[]{:S(2)}, u32[]{:S(2)}) %collective-permute-start.18) | collective-permute-done | bytes 1048608 | tf_op jit(solution)/shard_map/ppermute | solution.py:545
  168.7 23.3 %finish.1 = (bf16[512,256]{1,0:T(8,128)(2,1)}, bf16[512,256]{1,0:T(8,128)(2,1)}, bf16[2048,256]{1,0:T(8,128)(2,1)}, f32[16,256]{1,0:T(8,128)}) custom-call(s32[22]{0:T(128)} %concatenate.13.order_ref, f32[5,16,256]{2,1,0:T(8,128)} %bitcast.76, bf16[2,512,256]{2,1,0:T(8,128)(2,1)} %early_products.1.refs_1_.refs_0_, bf16[4,512,256]{2,1,0:T(8,128)(2,1)} %copy-done.2, ...), custom_call_target="tpu_custom_call" | custom-call | flops 8589934592 | bytes 23068672 | tf_op jit(solution)/shard_map/finish/pallas_call | solution.py:462
  193.4 8.5 %gate_near.1 = (bf16[512,256]{1,0:T(8,128)(2,1)}, bf16[512,256]{1,0:T(8,128)(2,1)}) custom-call(s32[22]{0:T(128)} %concatenate.13.order_ref, bf16[2048,256]{1,0:T(8,128)(2,1)} %get-tuple-element.8.conv_ref, bf16[4,512,256]{2,1,0:T(8,128)(2,1)} %copy-done.3, bf16[512,256]{1,0:T(8,128)(2,1)} %get-tuple-element.14.refs_8_.refs_1_, ...), custom_call_target="tpu_custom_call" | custom-call | flops 2147483648 | bytes 10485760 | tf_op jit(solution)/shard_map/gate_near/pallas_call | solution.py:424
  201.9 2.3 %collective-permute-start.19 = (bf16[512,256]{1,0:T(8,128)(2,1)}, bf16[512,256]{1,0:T(8,128)(2,1)S(1)}, u32[]{:S(2)}, u32[]{:S(2)}) collective-permute-start(bf16[512,256]{1,0:T(8,128)(2,1)} %get-tuple-element.10), channel_id=1, source_target_pairs={{0,4},{4,0},{8,12},{12,8},{1,5},{5,1},{9,13},{13,9},{2,6},{6,2},{1... | collective-permute-start | bytes 786440 | tf_op jit(solution)/shard_map/ppermute | solution.py:575
  204.2 7.2 %collective-permute-done.20.refs_0_ = bf16[512,256]{1,0:T(8,128)(2,1)S(1)} collective-permute-done((bf16[512,256]{1,0:T(8,128)(2,1)}, bf16[512,256]{1,0:T(8,128)(2,1)S(1)}, u32[]{:S(2)}, u32[]{:S(2)}) %collective-permute-start.20) | collective-permute-done | bytes 262176 | tf_op jit(solution)/shard_map/ppermute | solution.py:571
  212.8 4.1 %collective-permute-done.19.refs_1_ = bf16[512,256]{1,0:T(8,128)(2,1)S(1)} collective-permute-done((bf16[512,256]{1,0:T(8,128)(2,1)}, bf16[512,256]{1,0:T(8,128)(2,1)S(1)}, u32[]{:S(2)}, u32[]{:S(2)}) %collective-permute-start.19) | collective-permute-done | bytes 262176 | tf_op jit(solution)/shard_map/ppermute | solution.py:575
  217.6 2.3 %place_columns.1 = bf16[512,1024]{1,0:T(8,128)(2,1)} custom-call(s32[1]{0:T(128)} %bitcast.place_ref, bf16[512,256]{1,0:T(8,128)(2,1)} %get-tuple-element.9.refs_0_, bf16[512,256]{1,0:T(8,128)(2,1)} %copy-done.15, bf16[512,256]{1,0:T(8,128)(2,1)} %after.4.refs_2_, bf16[512,256]{1,0:T(8,128)(2,1)} %after.5.refs_3_), custom_call_target="tpu_custom_call" | custom-call | tf_op jit(solution)/shard_map/place_columns/pallas_call | solution.py:504
  (87 shorter events, 24.3 us)
Async XLA Ops:
  3.8 33.1 %all-to-all-start = ((bf16[4,512,256]{2,1,0:T(8,128)(2,1)}), bf16[4,512,256]{2,1,0:T(8,128)(2,1)S(1)}, u32[]{:S(2)}, u32[]{:S(2)}) async-start(bf16[4,512,256]{2,1,0:T(8,128)(2,1)} %pad_maximum_fusion.2), calls=%async_computation | async-start | bytes 2097152 | tf_op jit(solution)/shard_map/all_to_all | solution.py:183
  10.2 44.1 %collective-permute-start.5 = (bf16[512,1024]{1,0:T(8,128)(2,1)}, bf16[512,1024]{1,0:T(8,128)(2,1)S(1)}, u32[]{:S(2)}, u32[]{:S(2)}) collective-permute-start(bf16[512,1024]{1,0:T(8,128)(2,1)} %param.7), channel_id=1, source_target_pairs={{4,0},{8,4},{12,8},{5,1},{9,5},{13,9},{6,2},{10,6},{14,10},{7,3},{... | collective-permute-start | bytes 3145736 | tf_op jit(solution)/shard_map/ppermute | solution.py:552
  11.4 44.1 %collective-permute-start.4 = (bf16[512,1024]{1,0:T(8,128)(2,1)}, bf16[512,1024]{1,0:T(8,128)(2,1)}, u32[]{:S(2)}, u32[]{:S(2)}) collective-permute-start(bf16[512,1024]{1,0:T(8,128)(2,1)} %param.7), channel_id=1, source_target_pairs={{0,4},{4,8},{8,12},{1,5},{5,9},{9,13},{2,6},{6,10},{10,14},{3,7},{... | collective-permute-start | bytes 3145736 | tf_op jit(solution)/shard_map/ppermute | solution.py:551
  17.0 40.3 %collective-permute-start.2 = (bf16[512,1024]{1,0:T(8,128)(2,1)}, bf16[512,1024]{1,0:T(8,128)(2,1)}, u32[]{:S(2)}, u32[]{:S(2)}) collective-permute-start(bf16[512,1024]{1,0:T(8,128)(2,1)} %param.7), channel_id=1, source_target_pairs={{0,2},{2,0},{1,3},{3,1},{4,6},{6,4},{5,7},{7,5},{8,10},{10,8},{9,1... | collective-permute-start | bytes 3145736 | tf_op jit(solution)/shard_map/ppermute | solution.py:536
  37.0 20.3 %copy-start.2 = (bf16[4,512,256]{2,1,0:T(8,128)(2,1)}, bf16[4,512,256]{2,1,0:T(8,128)(2,1)S(1)}, u32[]{:S(2)}) copy-start(bf16[4,512,256]{2,1,0:T(8,128)(2,1)S(1)} %all-to-all-done.refs_3_.refs_0_.refs_1_) | copy-start | bytes 3145732
  37.0 60.6 %all-to-all-start.1 = ((bf16[4,512,256]{2,1,0:T(8,128)(2,1)}), bf16[4,512,256]{2,1,0:T(8,128)(2,1)S(1)}, u32[]{:S(2)}, u32[]{:S(2)}) async-start(bf16[4,512,256]{2,1,0:T(8,128)(2,1)} %pad_maximum_fusion.3), calls=%async_computation.1 | async-start | bytes 2097152 | tf_op jit(solution)/shard_map/all_to_all | solution.py:183
  54.3 3.0 %copy-start.4 = (bf16[512,1024]{1,0:T(8,128)(2,1)}, bf16[512,1024]{1,0:T(8,128)(2,1)S(1)}, u32[]{:S(2)}) copy-start(bf16[512,1024]{1,0:T(8,128)(2,1)S(1)} %collective-permute-done.5.refs_1_) | copy-start | bytes 3145732
  54.3 40.3 %collective-permute-start.10 = (bf16[512,1024]{1,0:T(8,128)(2,1)S(1)}, bf16[512,1024]{1,0:T(8,128)(2,1)}, u32[]{:S(2)}, u32[]{:S(2)}) collective-permute-start(bf16[512,1024]{1,0:T(8,128)(2,1)S(1)} %collective-permute-done.5.refs_1_), channel_id=1, source_target_pairs={{4,0},{8,4},{5,1},{9,5},{6,2},{10,6},{7,3},{11,7},{20,16},{24,20},... | collective-permute-start | bytes 3145736 | tf_op jit(solution)/shard_map/ppermute | solution.py:552
  55.6 40.3 %collective-permute-start.9 = (bf16[512,1024]{1,0:T(8,128)(2,1)}, bf16[512,1024]{1,0:T(8,128)(2,1)}, u32[]{:S(2)}, u32[]{:S(2)}) collective-permute-start(bf16[512,1024]{1,0:T(8,128)(2,1)} %collective-permute-done.4.refs_0_), channel_id=1, source_target_pairs={{4,8},{8,12},{5,9},{9,13},{6,10},{10,14},{7,11},{11,15},{20,24},{2... | collective-permute-start | bytes 3145736 | tf_op jit(solution)/shard_map/ppermute | solution.py:551
  59.8 37.7 %collective-permute-start.6 = (bf16[512,1024]{1,0:T(8,128)(2,1)}, bf16[512,1024]{1,0:T(8,128)(2,1)S(1)}, u32[]{:S(2)}, u32[]{:S(2)}) collective-permute-start(bf16[512,1024]{1,0:T(8,128)(2,1)} %choose.3), channel_id=1, source_target_pairs={{0,2},{2,0},{1,3},{3,1},{4,6},{6,4},{5,7},{7,5},{8,10},{10,8},{9,1... | collective-permute-start | bytes 3145736 | tf_op jit(solution)/shard_map/ppermute | solution.py:536
  63.5 34.1 %collective-permute-start = (bf16[3,512,256]{2,1,0:T(8,128)(2,1)}, bf16[3,512,256]{2,1,0:T(8,128)(2,1)}, u32[]{:S(2)}, u32[]{:S(2)}) collective-permute-start(bf16[3,512,256]{2,1,0:T(8,128)(2,1)} %pad_maximum_fusion.5), channel_id=1, source_target_pairs={{0,16},{16,0},{1,17},{17,1},{2,18},{18,2},{3,19},{19,3},{4,20},{20... | collective-permute-start | bytes 2359304 | tf_op jit(solution)/shard_map/ppermute | solution.py:191
  94.6 41.4 %collective-permute-start.15 = (bf16[512,1024]{1,0:T(8,128)(2,1)}, bf16[512,1024]{1,0:T(8,128)(2,1)}, u32[]{:S(2)}, u32[]{:S(2)}) collective-permute-start(bf16[512,1024]{1,0:T(8,128)(2,1)} %collective-permute-done.10.refs_2_), channel_id=1, source_target_pairs={{4,0},{5,1},{6,2},{7,3},{20,16},{21,17},{22,18},{23,19}} | collective-permute-start | bytes 3145736 | tf_op jit(solution)/shard_map/ppermute | solution.py:552
  95.9 40.1 %collective-permute-start.14 = (bf16[512,1024]{1,0:T(8,128)(2,1)}, bf16[512,1024]{1,0:T(8,128)(2,1)}, u32[]{:S(2)}, u32[]{:S(2)}) collective-permute-start(bf16[512,1024]{1,0:T(8,128)(2,1)} %collective-permute-done.9.refs_0_), channel_id=1, source_target_pairs={{8,12},{9,13},{10,14},{11,15},{24,28},{25,29},{26,30},{27,31}} | collective-permute-start | bytes 3145736 | tf_op jit(solution)/shard_map/ppermute | solution.py:551
  101.8 5.1 %copy-start.11 = (bf16[1024,1024]{1,0:T(8,128)(2,1)S(1)}, bf16[1024,1024]{1,0:T(8,128)(2,1)}, u32[]{:S(2)}) copy-start(bf16[1024,1024]{1,0:T(8,128)(2,1)} %param.8) | copy-start | bytes 6291460
  101.8 34.2 %collective-permute-start.11 = (bf16[512,1024]{1,0:T(8,128)(2,1)}, bf16[512,1024]{1,0:T(8,128)(2,1)}, u32[]{:S(2)}, u32[]{:S(2)}) collective-permute-start(bf16[512,1024]{1,0:T(8,128)(2,1)} %choose.4), channel_id=1, source_target_pairs={{0,2},{2,0},{1,3},{3,1},{4,6},{6,4},{5,7},{7,5},{8,10},{10,8},{9,1... | collective-permute-start | bytes 3145736 | tf_op jit(solution)/shard_map/ppermute | solution.py:536
  105.4 19.0 %collective-permute-start.1 = (bf16[3,512,256]{2,1,0:T(8,128)(2,1)}, bf16[3,512,256]{2,1,0:T(8,128)(2,1)}, u32[]{:S(2)}, u32[]{:S(2)}) collective-permute-start(bf16[3,512,256]{2,1,0:T(8,128)(2,1)} %pad_maximum_fusion.6), channel_id=1, source_target_pairs={{0,16},{16,0},{1,17},{17,1},{2,18},{18,2},{3,19},{19,3},{4,20},{20... | collective-permute-start | bytes 2359304 | tf_op jit(solution)/shard_map/ppermute | solution.py:191
  108.8 36.1 %all-to-all-start.2 = ((bf16[4,512,256]{2,1,0:T(8,128)(2,1)}), bf16[4,512,256]{2,1,0:T(8,128)(2,1)S(1)}, u32[]{:S(2)}, u32[]{:S(2)}) async-start(bf16[4,512,256]{2,1,0:T(8,128)(2,1)} %pad_maximum_fusion.4), calls=%async_computation.2 | async-start | bytes 2097152 | tf_op jit(solution)/shard_map/all_to_all | solution.py:183
  122.4 26.2 %collective-permute-start.3 = (bf16[2,512,1024]{2,1,0:T(8,128)(2,1)S(1)}, bf16[2,512,1024]{2,1,0:T(8,128)(2,1)}, u32[]{:S(2)}, u32[]{:S(2)}) collective-permute-start(bf16[2,512,1024]{2,1,0:T(8,128)(2,1)S(1)} %pad_maximum_fusion.refs_6_.refs_10_.refs_3_), channel_id=1, source_target_pairs={{0,1},{1,0},{2,3},{3,2},{4,5},{5,4},{6,7},{7,6},{8,9},{9,8},{10,11... | collective-permute-start | bytes 6291464 | tf_op jit(solution)/shard_map/ppermute | solution.py:545
  124.4 24.8 %collective-permute-start.7 = (bf16[2,512,1024]{2,1,0:T(8,128)(2,1)}, bf16[2,512,1024]{2,1,0:T(8,128)(2,1)}, u32[]{:S(2)}, u32[]{:S(2)}) collective-permute-start(bf16[2,512,1024]{2,1,0:T(8,128)(2,1)} %pad_maximum_fusion.1.refs_8_.refs_12_.refs_5_), channel_id=1, source_target_pairs={{0,1},{1,0},{2,3},{3,2},{4,5},{5,4},{6,7},{7,6},{8,9},{9,8},{10,11... | collective-permute-start | bytes 6291464 | tf_op jit(solution)/shard_map/ppermute | solution.py:545
  139.4 25.5 %collective-permute-start.16 = (bf16[512,1024]{1,0:T(8,128)(2,1)}, bf16[512,1024]{1,0:T(8,128)(2,1)}, u32[]{:S(2)}, u32[]{:S(2)}) collective-permute-start(bf16[512,1024]{1,0:T(8,128)(2,1)} %choose.5), channel_id=1, source_target_pairs={{0,2},{2,0},{1,3},{3,1},{4,6},{6,4},{5,7},{7,5},{8,10},{10,8},{9,1... | collective-permute-start | bytes 3145736 | tf_op jit(solution)/shard_map/ppermute | solution.py:536
  144.9 14.6 %copy-start.3 = (bf16[4,512,256]{2,1,0:T(8,128)(2,1)}, bf16[4,512,256]{2,1,0:T(8,128)(2,1)S(1)}, u32[]{:S(2)}) copy-start(bf16[4,512,256]{2,1,0:T(8,128)(2,1)S(1)} %all-to-all-done.2.refs_7_.refs_0_) | copy-start | bytes 3145732
  146.1 18.8 %collective-permute-start.8 = (bf16[3,512,256]{2,1,0:T(8,128)(2,1)}, bf16[3,512,256]{2,1,0:T(8,128)(2,1)}, u32[]{:S(2)}, u32[]{:S(2)}) collective-permute-start(bf16[3,512,256]{2,1,0:T(8,128)(2,1)} %pad_maximum_fusion.7), channel_id=1, source_target_pairs={{0,16},{16,0},{1,17},{17,1},{2,18},{18,2},{3,19},{19,3},{4,20},{20... | collective-permute-start | bytes 2359304 | tf_op jit(solution)/shard_map/ppermute | solution.py:191
  148.6 16.4 %collective-permute-start.12 = (bf16[1,512,1024]{2,1,0:T(8,128)(2,1)}, bf16[1,512,1024]{2,1,0:T(8,128)(2,1)}, u32[]{:S(2)}, u32[]{:S(2)}) collective-permute-start(bf16[1,512,1024]{2,1,0:T(8,128)(2,1)} %bitcast.68), channel_id=1, source_target_pairs={{0,1},{1,0},{2,3},{3,2},{4,5},{5,4},{6,7},{7,6},{8,9},{9,8},{10,11... | collective-permute-start | bytes 3145736 | tf_op jit(solution)/shard_map/ppermute | solution.py:545
  148.6 16.4 %collective-permute-start.13 = (bf16[1,512,1024]{2,1,0:T(8,128)(2,1)}, bf16[1,512,1024]{2,1,0:T(8,128)(2,1)S(1)}, u32[]{:S(2)}, u32[]{:S(2)}) collective-permute-start(bf16[1,512,1024]{2,1,0:T(8,128)(2,1)} %bitcast.46.refs_15_.refs_8_), channel_id=1, source_target_pairs={{0,1},{1,0},{2,3},{3,2},{4,5},{5,4},{6,7},{7,6},{8,9},{9,8},{10,11... | collective-permute-start | bytes 3145736 | tf_op jit(solution)/shard_map/ppermute | solution.py:545
  149.2 15.9 %collective-permute-start.17 = (bf16[1,512,1024]{2,1,0:T(8,128)(2,1)}, bf16[1,512,1024]{2,1,0:T(8,128)(2,1)S(1)}, u32[]{:S(2)}, u32[]{:S(2)}) collective-permute-start(bf16[1,512,1024]{2,1,0:T(8,128)(2,1)} %bitcast.73), channel_id=1, source_target_pairs={{0,1},{1,0},{2,3},{3,2},{4,5},{5,4},{6,7},{7,6},{8,9},{9,8},{10,11... | collective-permute-start | bytes 3145736 | tf_op jit(solution)/shard_map/ppermute | solution.py:545
  159.6 5.3 %copy-start.12 = (f32[256,16]{0,1:T(8,128)S(1)}, f32[256,16]{0,1:T(8,128)}, u32[]{:S(2)}) copy-start(f32[256,16]{0,1:T(8,128)} %param.11) | copy-start | bytes 49156
  159.6 5.4 %copy-start.16 = (f32[256,16]{0,1:T(8,128)S(1)}, f32[256,16]{0,1:T(8,128)}, u32[]{:S(2)}) copy-start(f32[256,16]{0,1:T(8,128)} %param.12) | copy-start | bytes 49156
  159.6 5.4 %copy-start.17 = (f32[256,16]{0,1:T(8,128)S(1)}, f32[256,16]{0,1:T(8,128)}, u32[]{:S(2)}) copy-start(f32[256,16]{0,1:T(8,128)} %param.13) | copy-start | bytes 49156
  164.9 2.9 %collective-permute-start.18 = (bf16[1,512,1024]{2,1,0:T(8,128)(2,1)}, bf16[1,512,1024]{2,1,0:T(8,128)(2,1)S(1)}, u32[]{:S(2)}, u32[]{:S(2)}) collective-permute-start(bf16[1,512,1024]{2,1,0:T(8,128)(2,1)} %bitcast.49.refs_19_.refs_12_), channel_id=1, source_target_pairs={{0,1},{1,0},{2,3},{3,2},{4,5},{5,4},{6,7},{7,6},{8,9},{9,8},{10,11... | collective-permute-start | bytes 3145736 | tf_op jit(solution)/shard_map/ppermute | solution.py:545
  192.1 19.3 %collective-permute-start.20 = (bf16[512,256]{1,0:T(8,128)(2,1)}, bf16[512,256]{1,0:T(8,128)(2,1)S(1)}, u32[]{:S(2)}, u32[]{:S(2)}) collective-permute-start(bf16[512,256]{1,0:T(8,128)(2,1)} %get-tuple-element.11), channel_id=1, source_target_pairs={{0,8},{4,12},{8,0},{12,4},{1,9},{5,13},{9,1},{13,5},{2,10},{6,14},... | collective-permute-start | bytes 786440 | tf_op jit(solution)/shard_map/ppermute | solution.py:571
  192.1 20.0 %collective-permute-start.21 = (bf16[512,256]{1,0:T(8,128)(2,1)}, bf16[512,256]{1,0:T(8,128)(2,1)S(1)}, u32[]{:S(2)}, u32[]{:S(2)}) collective-permute-start(bf16[512,256]{1,0:T(8,128)(2,1)} %get-tuple-element.12), channel_id=1, source_target_pairs={{0,12},{4,8},{8,4},{12,0},{1,13},{5,9},{9,5},{13,1},{2,14},{6,10},... | collective-permute-start | bytes 786440 | tf_op jit(solution)/shard_map/ppermute | solution.py:571
  201.9 15.0 %collective-permute-start.19 = (bf16[512,256]{1,0:T(8,128)(2,1)}, bf16[512,256]{1,0:T(8,128)(2,1)S(1)}, u32[]{:S(2)}, u32[]{:S(2)}) collective-permute-start(bf16[512,256]{1,0:T(8,128)(2,1)} %get-tuple-element.10), channel_id=1, source_target_pairs={{0,4},{4,0},{8,12},{12,8},{1,5},{5,1},{9,13},{13,9},{2,6},{6,2},{1... | collective-permute-start | bytes 786440 | tf_op jit(solution)/shard_map/ppermute | solution.py:575
  (12 other events, 19.6 us)
